TPU v7x, 256 devices: a whole 4x4x8 slice. The times are simulated.
256 devices in a mesh: rep: 32 (over z_hi, y, core), fsdp: 8 (over x, z_lo).
Axes of the slice: x: 4, y: 4, z: 8 (z_hi: 4, z_lo: 2; z = z_hi * 2 + z_lo), core: 2. Of those that a mesh axis runs over, the one named last changes fastest.
Arguments:
- local_fragment: bfloat16 [32, 2, 8192, 1024], P('rep', None, 'fsdp'), may hold values from -6 to 6
- anchor: float32 [2, 8192, 1024], P(None, ('fsdp', 'rep')), may hold values from -6 to 6
- momentum: float32 [2, 8192, 1024], P(None, ('fsdp', 'rep')), may hold values from -4 to 4
- next_weights: bfloat16 [32, 8192, 1024], P('rep', 'fsdp'), may hold values from -0.0625 to 0.0625
- activations: bfloat16 [65536, 8192], P(('rep', 'fsdp')), may hold values from -6 to 6
- norm_gain: float32 [8192], replicated, may hold values from 0.25 to 1.75
Outputs:
- new_anchor: float32 [2, 8192, 1024], P(None, ('fsdp', 'rep'))
- new_momentum: float32 [2, 8192, 1024], P(None, ('fsdp', 'rep'))
- keys_values: bfloat16 [65536, 1024], P(('rep', 'fsdp'))
All inputs are finite; a program needn't handle non-finite values.
Results may differ from a plain program's by a relative error of at most 0.011.
Values may be sent and summed in bfloat16 or wider, within the bound.
No kernel may reach another device: no remote copies, remote signals or barrier semaphores. Data moves between devices by JAX's collectives and lax.ppermute only.
A program may use at most 128 MiB of HBM per device.

v0:
```python
import jax
import jax.numpy as jnp
from jax import lax
from jax.sharding import PartitionSpec as P


def shards(local_fragment, anchor, momentum, next_weights, activations, norm_gain):
    replicas = lax.axis_size("rep")
    term = local_fragment[0].astype(jnp.float32)
    total = lax.psum_scatter(
        term.astype(jnp.bfloat16), "rep", scatter_dimension=1, tiled=True
    ).astype(jnp.float32)
    pseudo = anchor - total / replicas
    new_momentum = 0.9 * momentum + pseudo
    new_anchor = anchor - 0.7 * (pseudo + 0.9 * new_momentum)
    wide = activations.astype(jnp.float32)
    square_mean = jnp.mean(wide * wide, axis=-1, keepdims=True)
    normed = (wide * lax.rsqrt(square_mean + 1e-05) * norm_gain).astype(jnp.bfloat16)
    layer_shard = next_weights[0]
    projected = jnp.dot(
        normed,
        lax.all_gather(layer_shard, "fsdp", axis=0, tiled=True),
        preferred_element_type=jnp.float32,
    )
    return (new_anchor, new_momentum, projected.astype(jnp.bfloat16))


def solution(mesh):
    placed = (
        P("rep", None, "fsdp", None),
        P(None, ("fsdp", "rep"), None),
        P(None, ("fsdp", "rep"), None),
        P("rep", "fsdp", None),
        P(("rep", "fsdp"), None),
        P(),
    )
    return jax.shard_map(
        shards,
        mesh=mesh,
        in_specs=placed,
        out_specs=(
            P(None, ("fsdp", "rep"), None),
            P(None, ("fsdp", "rep"), None),
            P(("rep", "fsdp"), None),
        ),
        check_vma=False,
    )
```

profile of v0, /device:TPU:8, one launch (start us, length us, event | category | flops | bytes accessed | tf_op | source)
XLA Modules:
  0.0 388.4 jit_solution(14028977883587527610)
XLA Ops:
  8.0 0.0 copy-start.1
  8.0 0.0 copy-start
  8.0 0.0 copy-start.2
  8.0 0.0 reduce-scatter.2.cloned.1.call-start
  8.1 0.7 reduce-scatter.2.cloned.1.call-update
  8.8 0.0 all-gather.3.cloned.1.call-start
  8.8 0.5 all-gather.3.cloned.1.call-update
  9.3 3.1 fusion.2
  12.5 354.3 %reduce-scatter.2.cloned.1.call-done = bf16[2,32,1024]{2,1,0:T(8,128)(2,1)} async-done(((bf16[2,1024,1024]{2,1,0:T(8,128)(2,1)}), bf16[2,32,1024]{2,1,0:T(8,128)(2,1)}) %reduce-scatter.2.cloned.1.call-update) | async-done | bytes 131088 | tf_op jit(solution)/shard_map/reduce_scatter | solution.py:10
  366.8 0.0 copy-done.1
  366.8 0.0 copy-done
  366.8 1.8 multiply_subtract_fusion
  368.6 0.0 all-gather.3.cloned.1.call-done
  368.6 0.0 copy-done.2
  368.6 12.4 %fusion.8 = bf16[256,1024]{1,0:T(8,128)(2,1)} fusion(bf16[1,8192,1024]{2,1,0:T(8,128)(2,1)} %all-gather.3.cloned.1.call-done, bf16[256,8192]{1,0:T(8,128)(2,1)} %param.10, f32[8192]{0:T(1024)S(1)} %copy-done.2, f32[256]{0:T(256)S(1)} %add_rsqrt_fusion), kind=kOutput, calls=%fused_computation.9 | convolution fusion | flops 4303618048 | bytes 21529600 | tf_op jit(solution)/shard_map/dot_general | solution.py:20
  (1 shorter events, 0.0 us)
Async XLA Ops:
  8.0 358.8 %copy-start.1 = (f32[2,32,1024]{2,1,0:T(8,128)S(1)}, f32[2,32,1024]{2,1,0:T(8,128)}, u32[]{:S(2)}) copy-start(f32[2,32,1024]{2,1,0:T(8,128)} %param.8) | copy-start | bytes 786436
  8.0 358.8 %copy-start = (f32[2,32,1024]{2,1,0:T(8,128)S(1)}, f32[2,32,1024]{2,1,0:T(8,128)}, u32[]{:S(2)}) copy-start(f32[2,32,1024]{2,1,0:T(8,128)} %param.7) | copy-start | bytes 786436
  8.0 360.6 %copy-start.2 = (f32[8192]{0:T(1024)S(1)}, f32[8192]{0:T(1024)}, u32[]{:S(2)}) copy-start(f32[8192]{0:T(1024)} %param.11) | copy-start | bytes 98308
  8.0 358.8 %reduce-scatter.2.cloned.1.call-start = ((), (), s32[]{:S(2)}) async-start(), calls=%async_computation.1 | async-start | bytes 4325376 | tf_op jit(solution)/shard_map/reduce_scatter | solution.py:10
  8.8 359.8 %all-gather.3.cloned.1.call-start = ((), (), s32[]{:S(2)}) async-start(), calls=%async_computation.2 | async-start | bytes 18874368 | tf_op jit(solution)/shard_map/all_gather | solution.py:22
Sparse Core Ops, SparseCore 0:
  12.8 353.9 reduce-scatter.1
Sparse Core Ops, SparseCore 1:
  11.2 351.7 all-gather.2
where the time goes:
time: 389 us; the launch traced here: 388 us
  waiting for transfers between devices  356 us (92%)
  between operations  15.5 us (4%)
  matrix products  12.4 us (3%)
  other arithmetic  4.89 us (1%)
    reduce_scatter x1, waiting for transfers between devices, shards(): lax.psum_scatter(term.astype(jnp.bfloat16), 'rep', scatter_dimension=1, t...  354 us
    dot_general x1, matrix products, shards(): jnp.dot(normed, lax.all_gather(layer_shard, 'fsdp', axis=0, tiled=True),...  12.4 us
  transfers between devices with their start and end apart: 2, of which 1 were waited for; matrix products, arithmetic and copies ran while one was open for 1% of the time, Pallas kernels for 0%

commit v1 on v0

v1 whole, which is shorter than its diff:
```python
import jax
import jax.numpy as jnp
from jax import lax
from jax.sharding import PartitionSpec as P

F32, BF16 = jnp.float32, jnp.bfloat16
EPS = 1e-05


def along(sizes, axis, shift):
    pairs = []
    total = 1
    for size in sizes:
        total *= size
    stride = 1
    for size in sizes[axis + 1 :]:
        stride *= size
    for index in range(total):
        at = index // stride % sizes[axis]
        pairs.append((index, index + ((at + shift) % sizes[axis] - at) * stride))
    return pairs


REP = (4, 4, 2)
FSDP = (4, 2)


def move(value, mesh_axis, sizes, axis, shift):
    return lax.ppermute(value, mesh_axis, along(sizes, axis, shift))


def shards(local_fragment, anchor, momentum, next_weights, activations, norm_gain):
    replicas = lax.axis_size("rep")
    rep, fsdp = lax.axis_index("rep"), lax.axis_index("fsdp")
    z_hi, y, core = rep // 8, rep // 2 % 4, rep % 2
    x, z_lo = fsdp // 2, fsdp % 2

    mine = next_weights[0]
    rows = mine.shape[0]
    other = move(mine, "fsdp", FSDP, 1, 1)

    def block(shift):
        owner = (x + shift) % 4
        parts = []
        for which in (z_lo, 1 - z_lo):
            at = (owner * 2 + which) * rows
            a = lax.dynamic_slice_in_dim(activations, at, rows, 1).astype(F32)
            g = lax.dynamic_slice_in_dim(norm_gain, at, rows, 0)
            parts.append((a * g).astype(BF16))
        return jnp.concatenate(parts, 1)

    sent2 = move(block(2), "fsdp", FSDP, 0, 2)
    sent_p = move(block(1), "fsdp", FSDP, 0, 1)
    sent_m = move(block(3), "fsdp", FSDP, 0, 3)
    own = block(0)

    frag = local_fragment[0].reshape(2, 4, 4, 2, 32, 1024)
    pick = lambda a, i, d: lax.dynamic_index_in_dim(a, i, d, keepdims=False)
    got = move(pick(frag, 1 - core, 3), "rep", REP, 2, 1)
    pair = (pick(frag, core, 3).astype(F32) + got.astype(F32)).astype(BF16)
    ys = [move(pick(pair, (y + s) % 4, 2), "rep", REP, 1, s) for s in (1, 2, 3)]
    line = pick(pair, y, 2).astype(F32)
    for part in ys:
        line = line + part.astype(F32)
    line = line.astype(BF16)
    zs = [move(pick(line, (z_hi + s) % 4, 1), "rep", REP, 0, s) for s in (1, 2, 3)]
    total = pick(line, z_hi, 1).astype(F32)
    for part in zs:
        total = total + part.astype(F32)
    pseudo = anchor - total / replicas
    new_momentum = 0.9 * momentum + pseudo
    new_anchor = anchor - 0.7 * (pseudo + 0.9 * new_momentum)

    wide = activations.astype(F32)
    scale = lax.rsqrt(jnp.mean(wide * wide, axis=-1, keepdims=True) + EPS)

    def partial(a):
        return jnp.dot(a[:, :rows], mine, preferred_element_type=F32) + jnp.dot(
            a[:, rows:], other, preferred_element_type=F32
        )

    half = 512
    p2 = partial(sent2).astype(BF16)
    via_p = move(p2[:, :half], "fsdp", FSDP, 0, 1)
    via_m = move(p2[:, half:], "fsdp", FSDP, 0, 3)
    back_m, back_p = partial(sent_p), partial(sent_m)
    to_p = jnp.concatenate([back_p[:, :half] + via_p.astype(F32), back_p[:, half:]], 1).astype(BF16)
    to_m = jnp.concatenate([back_m[:, :half], back_m[:, half:] + via_m.astype(F32)], 1).astype(BF16)
    got_p = move(to_p, "fsdp", FSDP, 0, 1)
    got_m = move(to_m, "fsdp", FSDP, 0, 3)
    projected = partial(own) + got_p.astype(F32) + got_m.astype(F32)
    return (new_anchor, new_momentum, (projected * scale).astype(BF16))


def solution(mesh):
    placed = (
        P("rep", None, "fsdp", None),
        P(None, ("fsdp", "rep"), None),
        P(None, ("fsdp", "rep"), None),
        P("rep", "fsdp", None),
        P(("rep", "fsdp"), None),
        P(),
    )
    return jax.shard_map(
        shards,
        mesh=mesh,
        in_specs=placed,
        out_specs=(
            P(None, ("fsdp", "rep"), None),
            P(None, ("fsdp", "rep"), None),
            P(("rep", "fsdp"), None),
        ),
        check_vma=False,
    )
```

time: 389 us -> 120 us (0.31)
  waiting for transfers between devices: 356 us -> 52.1 us
  starting transfers between devices: 0.08 us -> 34.7 us
  between operations: 15.5 us -> 0.83 us
  other arithmetic: 4.89 us -> 13.4 us
  local copies, waits for them, and re-layouts: 0.01 us -> 4.77 us
    reduce_scatter x1 -> x0, waiting for transfers between devices: 354 us -> none  [shards(): lax.psum_scatter(term.astype(jnp.bfloat16), 'rep', scatter_dimension=1, t...]
    ppermute x0 -> x15, waiting for transfers between devices: none -> 52.1 us  [move(): return lax.ppermute(value, mesh_axis, along(sizes, axis, shift))]
    ppermute x0 -> x15, starting transfers between devices: none -> 34.7 us  [move(): return lax.ppermute(value, mesh_axis, along(sizes, axis, shift))]
    convert_element_type x0 -> x3, other arithmetic: none -> 5.65 us  [the longest x1 2.74 us: block(): parts.append((a * g).astype(BF16))]
    dot_general x1 -> x8, matrix products: 12.4 us -> 13 us  [the longest x4 6.88 us: partial(): jnp.dot(a[:, rows:], other, preferred_element_type=F32)]
  transfers between devices with their start and end apart: 2 -> 15, of which waited for: 1 -> 7; matrix products, arithmetic and copies ran while one was open for 1% -> 24% of each run, Pallas kernels for 0% -> 0%
where the time goes in v1:
time: 120 us; the launch traced here: 119 us
  waiting for transfers between devices  52.1 us (43%)
  starting transfers between devices  34.7 us (29%)
  other arithmetic  13.4 us (11%)
  matrix products  13 us (11%)
  local copies, waits for them, and re-layouts  4.77 us (4%)
    ppermute x15, waiting for transfers between devices, move(): return lax.ppermute(value, mesh_axis, along(sizes, axis, shift))  52.1 us
    ppermute x15, starting transfers between devices, move(): return lax.ppermute(value, mesh_axis, along(sizes, axis, shift))  34.7 us
    dot_general x4, matrix products, partial(): jnp.dot(a[:, rows:], other, preferred_element_type=F32)  6.88 us
    dot_general x4, matrix products, partial(): jnp.dot(a[:, :rows], mine, preferred_element_type=F32)  6.11 us
    squeeze x3, local copies, waits for them, and re-layouts, shards(): pick = lambda a, i, d: lax.dynamic_index_in_dim(a, i, d, keepdims=False)  3.43 us
    concatenate x3, other arithmetic, block(): return jnp.concatenate(parts, 1)  3.3 us
    reduce_sum x1, other arithmetic, shards(): scale = lax.rsqrt(jnp.mean(wide * wide, axis=-1, keepdims=True) + EPS)  3.25 us
    convert_element_type x1, other arithmetic, block(): parts.append((a * g).astype(BF16))  2.74 us
  transfers between devices with their start and end apart: 15, of which 7 were waited for; matrix products, arithmetic and copies ran while one was open for 24% of the time, Pallas kernels for 0%

profile of v1, /device:TPU:8, one launch (start us, length us, event | category | flops | bytes accessed | tf_op | source)
XLA Modules:
  0.0 118.8 jit_solution(8398853543134395225)
XLA Ops:
  0.6 2.0 %collective-permute-start.7 = (bf16[1024,1024]{1,0:T(8,128)(2,1)}, bf16[1024,1024]{1,0:T(8,128)(2,1)S(1)}, u32[]{:S(2)}, u32[]{:S(2)}) collective-permute-start(bf16[1024,1024]{1,0:T(8,128)(2,1)} %bitcast.42), channel_id=1, source_target_pairs={{0,1},{1,0},{2,3},{3,2},{4,5},{5,4},{6,7},{7,6},{8,9},{9,8},{10,11... | collective-permute-start | bytes 6291464 | tf_op jit(solution)/shard_map/ppermute | solution.py:29
  3.4 2.7 %multiply_convert_fusion.5 = (bf16[256,1024]{1,0:T(8,128)(2,1)S(1)}, bf16[256,1024]{1,0:T(8,128)(2,1)S(1)}, bf16[256,1024]{1,0:T(8,128)(2,1)S(1)}, bf16[256,1024...) fusion(f32[1024]{0:T(1024)S(1)} %get-tuple-element.23, ...), kind=kLoop, calls=%fused_computation.25 | loop fusion | flops 4718592 | bytes 6316056 | tf_op jit(solution)/shard_map/convert_element_type | solution.py:49
  6.2 1.1 pad_maximum_fusion
  7.3 2.8 %collective-permute-start.8 = (bf16[256,2048]{1,0:T(8,128)(2,1)}, bf16[256,2048]{1,0:T(8,128)(2,1)S(1)}, u32[]{:S(2)}, u32[]{:S(2)}) collective-permute-start(bf16[256,2048]{1,0:T(8,128)(2,1)} %pad_maximum_fusion), channel_id=1, source_target_pairs={{0,6},{1,7},{2,0},{3,1},{4,2},{5,3},{6,4},{7,5},{8,14},{9,15},{10,... | collective-permute-start | bytes 3145736 | tf_op jit(solution)/shard_map/ppermute | solution.py:29
  10.0 1.1 pad_maximum_fusion.1
  12.0 1.1 pad_maximum_fusion.2
  13.9 3.2 %dynamic-slice_bitcast_fusion = bf16[2,4,4,32,1024]{4,3,2,1,0:T(8,128)(2,1)} fusion(bf16[2,4,4,2,32,1024]{5,4,3,2,1,0:T(8,128)(2,1)} %bitcast.43, s32[]{:T(128)S(6)} %select_n.132), kind=kLoop, calls=%fused_computation.3 | loop fusion | bytes 4194308 | tf_op jit(solution)/shard_map/jit(dynamic_index_in_dim)/squeeze | solution.py:58
  17.1 3.3 %multiply_reduce_fusion = f32[256]{0:T(256)S(1)} fusion(bf16[256,8192]{1,0:T(8,128)(2,1)} %param.10), kind=kLoop, calls=%fused_computation | loop fusion | flops 6291200 | bytes 4195328 | tf_op jit(solution)/shard_map/reduce_sum | solution.py:75
  20.4 1.8 %fusion.9 = f32[256,1024]{1,0:T(8,128)S(1)} fusion(f32[1024]{0:T(1024)S(1)} %get-tuple-element.24, bf16[256,8192]{1,0:T(8,128)(2,1)} %param.10, s32[]{:T(128)S(6)} %select_n.153, bf16[1,1024,1024]{2,1,0:T(8,128)(2,1)S(1)} %copy-done), kind=kOutput, calls=%fused_computation.28 | convolution fusion | flops 537657344 | bytes 3674116 | tf_op jit(solution)/shard_map/dot_general | solution.py:78
  22.2 17.0 %collective-permute-done.9 = bf16[256,2048]{1,0:T(8,128)(2,1)} collective-permute-done((bf16[256,2048]{1,0:T(8,128)(2,1)}, bf16[256,2048]{1,0:T(8,128)(2,1)}, u32[]{:S(2)}, u32[]{:S(2)}) %collective-permute-start.9) | collective-permute-done | bytes 1048608 | tf_op jit(solution)/shard_map/ppermute | solution.py:29
  39.1 9.4 %collective-permute-done.7 = bf16[1024,1024]{1,0:T(8,128)(2,1)S(1)} collective-permute-done((bf16[1024,1024]{1,0:T(8,128)(2,1)}, bf16[1024,1024]{1,0:T(8,128)(2,1)S(1)}, u32[]{:S(2)}, u32[]{:S(2)}) %collective-permute-start.7) | collective-permute-done | bytes 2097184 | tf_op jit(solution)/shard_map/ppermute | solution.py:29
  48.5 1.7 %fusion.14 = f32[256,1024]{1,0:T(8,128)S(1)} fusion(bf16[1024,1024]{1,0:T(8,128)(2,1)S(1)} %collective-permute-done.7, bf16[256,2048]{1,0:T(8,128)(2,1)} %collective-permute-done.9), kind=kOutput, calls=%fused_computation.36 | convolution fusion | flops 536870912 | bytes 3670016 | tf_op jit(solution)/shard_map/dot_general | solution.py:78
  50.2 1.8 %fusion.5 = bf16[256,1024]{1,0:T(8,128)(2,1)S(1)} fusion(f32[256,1024]{1,0:T(8,128)S(1)} %fusion.14, bf16[256,2048]{1,0:T(8,128)(2,1)} %collective-permute-done.9, bf16[1,1024,1024]{2,1,0:T(8,128)(2,1)S(1)} %copy-done), kind=kOutput, calls=%fused_computation.12 | convolution fusion | flops 537395200 | bytes 4194304 | tf_op jit(solution)/shard_map/dot_general | solution.py:78
  52.0 8.7 %collective-permute-start.10 = (bf16[256,512]{1,0:T(8,128)(2,1)S(1)}, bf16[256,512]{1,0:T(8,128)(2,1)S(1)}, u32[]{:S(2)}, u32[]{:S(2)}) collective-permute-start(bf16[256,512]{1,0:T(8,128)(2,1)S(1)} %get-tuple-element.14), channel_id=1, source_target_pairs={{0,2},{1,3},{2,4},{3,5},{4,6},{5,7},{6,0},{7,1},{8,10},{9,11},{10,... | collective-permute-start | bytes 786440 | tf_op jit(solution)/shard_map/ppermute | solution.py:29
  62.1 1.7 %fusion.11 = f32[256,1024]{1,0:T(8,128)S(1)} fusion(bf16[1024,1024]{1,0:T(8,128)(2,1)S(1)} %collective-permute-done.7, bf16[256,2048]{1,0:T(8,128)(2,1)} %collective-permute-done.12), kind=kOutput, calls=%fused_computation.32 | convolution fusion | flops 536870912 | bytes 3670016 | tf_op jit(solution)/shard_map/dot_general | solution.py:78
  64.6 1.9 %convolution_add_fusion = f32[256,1024]{1,0:T(8,128)S(1)} fusion(f32[256,1024]{1,0:T(8,128)S(1)} %fusion.11, bf16[256,2048]{1,0:T(8,128)(2,1)} %collective-permute-done.12, bf16[1,1024,1024]{2,1,0:T(8,128)(2,1)S(1)} %copy-done), kind=kOutput, calls=%fused_computation.4 | convolution fusion | flops 537133056 | bytes 4718592 | tf_op jit(solution)/shard_map/dot_general | solution.py:78
  66.9 2.5 %fusion = bf16[2,4,4,32,1024]{4,3,2,1,0:T(8,128)(2,1)S(1)} fusion(bf16[2,4,4,32,1024]{4,3,2,1,0:T(8,128)(2,1)} %collective-permute-done, bf16[2,4,4,2,32,1024]{5,4,3,2,1,0:T(8,128)(2,1)S(1)} %bitcast.44, s32[]{:T(128)S(6)} %select_n.131), kind=kLoop, calls=%fused_computation.2 | loop fusion | flops 4194304 | bytes 6291460 | tf_op jit(solution)/shard_map/convert_element_type | solution.py:60
  69.7 1.7 %collective-permute-start.1 = (bf16[2,4,32,1024]{3,2,1,0:T(8,128)(2,1)S(1)}, bf16[2,4,32,1024]{3,2,1,0:T(8,128)(2,1)S(1)}, u32[]{:S(2)}, u32[]{:S(2)}) collective-permute-start(bf16[2,4,32,1024]{3,2,1,0:T(8,128)(2,1)S(1)} %get-tuple-element.11), channel_id=1, source_target_pairs={{0,16},{8,24},{16,32},{24,40},{32,48},{40,56},{48,0},{56,8},{64,80... | collective-permute-start | bytes 1572872 | tf_op jit(solution)/shard_map/ppermute | solution.py:29
  71.4 0.9 collective-permute-start.2
  72.3 2.4 %collective-permute-start.3 = (bf16[2,4,32,1024]{3,2,1,0:T(8,128)(2,1)S(1)}, bf16[2,4,32,1024]{3,2,1,0:T(8,128)(2,1)S(1)}, u32[]{:S(2)}, u32[]{:S(2)}) collective-permute-start(bf16[2,4,32,1024]{3,2,1,0:T(8,128)(2,1)S(1)} %get-tuple-element.12), channel_id=1, source_target_pairs={{0,48},{8,56},{16,0},{24,8},{32,16},{40,24},{48,32},{56,40},{64,11... | collective-permute-start | bytes 1572872 | tf_op jit(solution)/shard_map/ppermute | solution.py:29
  74.9 1.5 %collective-permute-start.11 = (bf16[256,1024]{1,0:T(8,128)(2,1)S(1)}, bf16[256,1024]{1,0:T(8,128)(2,1)S(1)}, u32[]{:S(2)}, u32[]{:S(2)}) collective-permute-start(bf16[256,1024]{1,0:T(8,128)(2,1)S(1)} %pad_maximum_fusion.3), channel_id=1, source_target_pairs={{0,2},{1,3},{2,4},{3,5},{4,6},{5,7},{6,0},{7,1},{8,10},{9,11},{10,... | collective-permute-start | bytes 1572872 | tf_op jit(solution)/shard_map/ppermute | solution.py:29
  76.5 1.9 %collective-permute-start.14 = (bf16[256,1024]{1,0:T(8,128)(2,1)S(1)}, bf16[256,1024]{1,0:T(8,128)(2,1)S(1)}, u32[]{:S(2)}, u32[]{:S(2)}) collective-permute-start(bf16[256,1024]{1,0:T(8,128)(2,1)S(1)} %pad_maximum_fusion.4), channel_id=1, source_target_pairs={{0,6},{1,7},{2,0},{3,1},{4,2},{5,3},{6,4},{7,5},{8,14},{9,15},{10,... | collective-permute-start | bytes 1572872 | tf_op jit(solution)/shard_map/ppermute | solution.py:29
  78.4 6.2 %collective-permute-done.1 = bf16[2,4,32,1024]{3,2,1,0:T(8,128)(2,1)S(1)} collective-permute-done((bf16[2,4,32,1024]{3,2,1,0:T(8,128)(2,1)S(1)}, bf16[2,4,32,1024]{3,2,1,0:T(8,128)(2,1)S(1)}, u32[]{:S(2)}, u32[]{:S(2)}) %collective-permute-start.1) | collective-permute-done | bytes 524320 | tf_op jit(solution)/shard_map/ppermute | solution.py:29
  84.7 3.1 %collective-permute-done.2 = bf16[2,4,32,1024]{3,2,1,0:T(8,128)(2,1)S(1)} collective-permute-done((bf16[2,4,32,1024]{3,2,1,0:T(8,128)(2,1)S(1)}, bf16[2,4,32,1024]{3,2,1,0:T(8,128)(2,1)S(1)}, u32[]{:S(2)}, u32[]{:S(2)}) %collective-permute-start.2) | collective-permute-done | bytes 524320 | tf_op jit(solution)/shard_map/ppermute | solution.py:29
  87.8 7.5 %collective-permute-done.3 = bf16[2,4,32,1024]{3,2,1,0:T(8,128)(2,1)S(1)} collective-permute-done((bf16[2,4,32,1024]{3,2,1,0:T(8,128)(2,1)S(1)}, bf16[2,4,32,1024]{3,2,1,0:T(8,128)(2,1)S(1)}, u32[]{:S(2)}, u32[]{:S(2)}) %collective-permute-start.3) | collective-permute-done | bytes 524320 | tf_op jit(solution)/shard_map/ppermute | solution.py:29
  95.7 3.3 %collective-permute-start.4 = (bf16[2,32,1024]{2,1,0:T(8,128)(2,1)S(1)}, bf16[2,32,1024]{2,1,0:T(8,128)(2,1)S(1)}, u32[]{:S(2)}, u32[]{:S(2)}) collective-permute-start(bf16[2,32,1024]{2,1,0:T(8,128)(2,1)S(1)} %get-tuple-element.16), channel_id=1, source_target_pairs={{0,64},{8,72},{16,80},{24,88},{32,96},{40,104},{48,112},{56,120},{... | collective-permute-start | bytes 393224 | tf_op jit(solution)/shard_map/ppermute | solution.py:29
  99.1 4.5 %collective-permute-start.5 = (bf16[2,32,1024]{2,1,0:T(8,128)(2,1)S(1)}, bf16[2,32,1024]{2,1,0:T(8,128)(2,1)S(1)}, u32[]{:S(2)}, u32[]{:S(2)}) collective-permute-start(bf16[2,32,1024]{2,1,0:T(8,128)(2,1)S(1)} %get-tuple-element.18), channel_id=1, source_target_pairs={{0,128},{8,136},{16,144},{24,152},{32,160},{40,168},{48,176},{56,1... | collective-permute-start | bytes 393224 | tf_op jit(solution)/shard_map/ppermute | solution.py:29
  103.6 2.7 %collective-permute-start.6 = (bf16[2,32,1024]{2,1,0:T(8,128)(2,1)S(1)}, bf16[2,32,1024]{2,1,0:T(8,128)(2,1)S(1)}, u32[]{:S(2)}, u32[]{:S(2)}) collective-permute-start(bf16[2,32,1024]{2,1,0:T(8,128)(2,1)S(1)} %get-tuple-element.17), channel_id=1, source_target_pairs={{0,192},{8,200},{16,208},{24,216},{32,224},{40,232},{48,240},{56,2... | collective-permute-start | bytes 393224 | tf_op jit(solution)/shard_map/ppermute | solution.py:29
  106.2 5.9 %collective-permute-done.5 = bf16[2,32,1024]{2,1,0:T(8,128)(2,1)S(1)} collective-permute-done((bf16[2,32,1024]{2,1,0:T(8,128)(2,1)S(1)}, bf16[2,32,1024]{2,1,0:T(8,128)(2,1)S(1)}, u32[]{:S(2)}, u32[]{:S(2)}) %collective-permute-start.5) | collective-permute-done | bytes 131104 | tf_op jit(solution)/shard_map/ppermute | solution.py:29
  112.2 3.0 %collective-permute-done.6 = bf16[2,32,1024]{2,1,0:T(8,128)(2,1)S(1)} collective-permute-done((bf16[2,32,1024]{2,1,0:T(8,128)(2,1)S(1)}, bf16[2,32,1024]{2,1,0:T(8,128)(2,1)S(1)}, u32[]{:S(2)}, u32[]{:S(2)}) %collective-permute-start.6) | collective-permute-done | bytes 131104 | tf_op jit(solution)/shard_map/ppermute | solution.py:29
  115.2 0.9 multiply_subtract_fusion
  116.1 2.7 %fusion.4 = bf16[256,1024]{1,0:T(8,128)(2,1)} fusion(f32[256,1024]{1,0:T(8,128)S(1)} %fusion.9, bf16[1024,1024]{1,0:T(8,128)(2,1)S(1)} %collective-permute-done.7, bf16[256,1024]{1,0:T(8,128)(2,1)S(1)} %collective-permute-done.14, bf16[256,1024]{1,0:T(8,128)(2,1)S(1)} %collective-permute-done.11, f32[256]{0:T(256)S(1)} %add_rsqrt_fusion, ...), kind=kOutput, calls=%fused_computation.11 | convolution fusion | flops 539492352 | bytes 5248004 | tf_op jit(solution)/shard_map/dot_general | solution.py:78
  (34 shorter events, 6.0 us)
Async XLA Ops:
  0.6 47.8 %collective-permute-start.7 = (bf16[1024,1024]{1,0:T(8,128)(2,1)}, bf16[1024,1024]{1,0:T(8,128)(2,1)S(1)}, u32[]{:S(2)}, u32[]{:S(2)}) collective-permute-start(bf16[1024,1024]{1,0:T(8,128)(2,1)} %bitcast.42), channel_id=1, source_target_pairs={{0,1},{1,0},{2,3},{3,2},{4,5},{5,4},{6,7},{7,6},{8,9},{9,8},{10,11... | collective-permute-start | bytes 6291464 | tf_op jit(solution)/shard_map/ppermute | solution.py:29
  7.3 54.1 %collective-permute-start.8 = (bf16[256,2048]{1,0:T(8,128)(2,1)}, bf16[256,2048]{1,0:T(8,128)(2,1)S(1)}, u32[]{:S(2)}, u32[]{:S(2)}) collective-permute-start(bf16[256,2048]{1,0:T(8,128)(2,1)} %pad_maximum_fusion), channel_id=1, source_target_pairs={{0,6},{1,7},{2,0},{3,1},{4,2},{5,3},{6,4},{7,5},{8,14},{9,15},{10,... | collective-permute-start | bytes 3145736 | tf_op jit(solution)/shard_map/ppermute | solution.py:29
  11.2 28.0 %collective-permute-start.9 = (bf16[256,2048]{1,0:T(8,128)(2,1)}, bf16[256,2048]{1,0:T(8,128)(2,1)}, u32[]{:S(2)}, u32[]{:S(2)}) collective-permute-start(bf16[256,2048]{1,0:T(8,128)(2,1)} %pad_maximum_fusion.1), channel_id=1, source_target_pairs={{0,4},{1,5},{2,6},{3,7},{4,0},{5,1},{6,2},{7,3},{8,12},{9,13},{10,... | collective-permute-start | bytes 3145736 | tf_op jit(solution)/shard_map/ppermute | solution.py:29
  13.0 49.0 %collective-permute-start.12 = (bf16[256,2048]{1,0:T(8,128)(2,1)}, bf16[256,2048]{1,0:T(8,128)(2,1)}, u32[]{:S(2)}, u32[]{:S(2)}) collective-permute-start(bf16[256,2048]{1,0:T(8,128)(2,1)} %pad_maximum_fusion.2), channel_id=1, source_target_pairs={{0,2},{1,3},{2,4},{3,5},{4,6},{5,7},{6,0},{7,1},{8,10},{9,11},{10,... | collective-permute-start | bytes 3145736 | tf_op jit(solution)/shard_map/ppermute | solution.py:29
  17.1 49.3 %collective-permute-start = (bf16[2,4,4,32,1024]{4,3,2,1,0:T(8,128)(2,1)}, bf16[2,4,4,32,1024]{4,3,2,1,0:T(8,128)(2,1)}, u32[]{:S(2)}, u32[]{:S(2)}) collective-permute-start(bf16[2,4,4,32,1024]{4,3,2,1,0:T(8,128)(2,1)} %dynamic-slice_bitcast_fusion), channel_id=1, source_target_pairs={{0,8},{8,0},{16,24},{24,16},{32,40},{40,32},{48,56},{56,48},{64,72... | collective-permute-start | bytes 6291464 | tf_op jit(solution)/shard_map/ppermute | solution.py:29
  17.1 3.3 %copy-start = (bf16[1,1024,1024]{2,1,0:T(8,128)(2,1)S(1)}, bf16[1,1024,1024]{2,1,0:T(8,128)(2,1)}, u32[]{:S(2)}) copy-start(bf16[1,1024,1024]{2,1,0:T(8,128)(2,1)} %param.9) | copy-start | bytes 6291460
  52.0 22.7 %collective-permute-start.10 = (bf16[256,512]{1,0:T(8,128)(2,1)S(1)}, bf16[256,512]{1,0:T(8,128)(2,1)S(1)}, u32[]{:S(2)}, u32[]{:S(2)}) collective-permute-start(bf16[256,512]{1,0:T(8,128)(2,1)S(1)} %get-tuple-element.14), channel_id=1, source_target_pairs={{0,2},{1,3},{2,4},{3,5},{4,6},{5,7},{6,0},{7,1},{8,10},{9,11},{10,... | collective-permute-start | bytes 786440 | tf_op jit(solution)/shard_map/ppermute | solution.py:29
  60.7 15.6 %collective-permute-start.13 = (bf16[256,512]{1,0:T(8,128)(2,1)S(1)}, bf16[256,512]{1,0:T(8,128)(2,1)S(1)}, u32[]{:S(2)}, u32[]{:S(2)}) collective-permute-start(bf16[256,512]{1,0:T(8,128)(2,1)S(1)} %get-tuple-element.15), channel_id=1, source_target_pairs={{0,6},{1,7},{2,0},{3,1},{4,2},{5,3},{6,4},{7,5},{8,14},{9,15},{10,... | collective-permute-start | bytes 786440 | tf_op jit(solution)/shard_map/ppermute | solution.py:29
  64.5 2.3 %copy-start.1 = (bf16[1,2,1024,1024]{3,2,1,0:T(8,128)(2,1)S(1)}, bf16[1,2,1024,1024]{3,2,1,0:T(8,128)(2,1)}, u32[]{:S(2)}) copy-start(bf16[1,2,1024,1024]{3,2,1,0:T(8,128)(2,1)} %param.6) | copy-start | bytes 12582916
  69.7 14.9 %collective-permute-start.1 = (bf16[2,4,32,1024]{3,2,1,0:T(8,128)(2,1)S(1)}, bf16[2,4,32,1024]{3,2,1,0:T(8,128)(2,1)S(1)}, u32[]{:S(2)}, u32[]{:S(2)}) collective-permute-start(bf16[2,4,32,1024]{3,2,1,0:T(8,128)(2,1)S(1)} %get-tuple-element.11), channel_id=1, source_target_pairs={{0,16},{8,24},{16,32},{24,40},{32,48},{40,56},{48,0},{56,8},{64,80... | collective-permute-start | bytes 1572872 | tf_op jit(solution)/shard_map/ppermute | solution.py:29
  71.4 16.4 %collective-permute-start.2 = (bf16[2,4,32,1024]{3,2,1,0:T(8,128)(2,1)S(1)}, bf16[2,4,32,1024]{3,2,1,0:T(8,128)(2,1)S(1)}, u32[]{:S(2)}, u32[]{:S(2)}) collective-permute-start(bf16[2,4,32,1024]{3,2,1,0:T(8,128)(2,1)S(1)} %get-tuple-element.13), channel_id=1, source_target_pairs={{0,32},{8,40},{16,48},{24,56},{32,0},{40,8},{48,16},{56,24},{64,96... | collective-permute-start | bytes 1572872 | tf_op jit(solution)/shard_map/ppermute | solution.py:29
  72.3 23.0 %collective-permute-start.3 = (bf16[2,4,32,1024]{3,2,1,0:T(8,128)(2,1)S(1)}, bf16[2,4,32,1024]{3,2,1,0:T(8,128)(2,1)S(1)}, u32[]{:S(2)}, u32[]{:S(2)}) collective-permute-start(bf16[2,4,32,1024]{3,2,1,0:T(8,128)(2,1)S(1)} %get-tuple-element.12), channel_id=1, source_target_pairs={{0,48},{8,56},{16,0},{24,8},{32,16},{40,24},{48,32},{56,40},{64,11... | collective-permute-start | bytes 1572872 | tf_op jit(solution)/shard_map/ppermute | solution.py:29
  74.9 41.2 %collective-permute-start.11 = (bf16[256,1024]{1,0:T(8,128)(2,1)S(1)}, bf16[256,1024]{1,0:T(8,128)(2,1)S(1)}, u32[]{:S(2)}, u32[]{:S(2)}) collective-permute-start(bf16[256,1024]{1,0:T(8,128)(2,1)S(1)} %pad_maximum_fusion.3), channel_id=1, source_target_pairs={{0,2},{1,3},{2,4},{3,5},{4,6},{5,7},{6,0},{7,1},{8,10},{9,11},{10,... | collective-permute-start | bytes 1572872 | tf_op jit(solution)/shard_map/ppermute | solution.py:29
  76.4 38.7 %copy-start.2 = (f32[2,32,1024]{2,1,0:T(8,128)S(1)}, f32[2,32,1024]{2,1,0:T(8,128)}, u32[]{:S(2)}) copy-start(f32[2,32,1024]{2,1,0:T(8,128)} %param.7) | copy-start | bytes 786436
  76.4 38.7 %copy-start.3 = (f32[2,32,1024]{2,1,0:T(8,128)S(1)}, f32[2,32,1024]{2,1,0:T(8,128)}, u32[]{:S(2)}) copy-start(f32[2,32,1024]{2,1,0:T(8,128)} %param.8) | copy-start | bytes 786436
  76.5 39.6 %collective-permute-start.14 = (bf16[256,1024]{1,0:T(8,128)(2,1)S(1)}, bf16[256,1024]{1,0:T(8,128)(2,1)S(1)}, u32[]{:S(2)}, u32[]{:S(2)}) collective-permute-start(bf16[256,1024]{1,0:T(8,128)(2,1)S(1)} %pad_maximum_fusion.4), channel_id=1, source_target_pairs={{0,6},{1,7},{2,0},{3,1},{4,2},{5,3},{6,4},{7,5},{8,14},{9,15},{10,... | collective-permute-start | bytes 1572872 | tf_op jit(solution)/shard_map/ppermute | solution.py:29
  95.7 10.5 %collective-permute-start.4 = (bf16[2,32,1024]{2,1,0:T(8,128)(2,1)S(1)}, bf16[2,32,1024]{2,1,0:T(8,128)(2,1)S(1)}, u32[]{:S(2)}, u32[]{:S(2)}) collective-permute-start(bf16[2,32,1024]{2,1,0:T(8,128)(2,1)S(1)} %get-tuple-element.16), channel_id=1, source_target_pairs={{0,64},{8,72},{16,80},{24,88},{32,96},{40,104},{48,112},{56,120},{... | collective-permute-start | bytes 393224 | tf_op jit(solution)/shard_map/ppermute | solution.py:29
  99.1 13.1 %collective-permute-start.5 = (bf16[2,32,1024]{2,1,0:T(8,128)(2,1)S(1)}, bf16[2,32,1024]{2,1,0:T(8,128)(2,1)S(1)}, u32[]{:S(2)}, u32[]{:S(2)}) collective-permute-start(bf16[2,32,1024]{2,1,0:T(8,128)(2,1)S(1)} %get-tuple-element.18), channel_id=1, source_target_pairs={{0,128},{8,136},{16,144},{24,152},{32,160},{40,168},{48,176},{56,1... | collective-permute-start | bytes 393224 | tf_op jit(solution)/shard_map/ppermute | solution.py:29
  103.6 11.6 %collective-permute-start.6 = (bf16[2,32,1024]{2,1,0:T(8,128)(2,1)S(1)}, bf16[2,32,1024]{2,1,0:T(8,128)(2,1)S(1)}, u32[]{:S(2)}, u32[]{:S(2)}) collective-permute-start(bf16[2,32,1024]{2,1,0:T(8,128)(2,1)S(1)} %get-tuple-element.17), channel_id=1, source_target_pairs={{0,192},{8,200},{16,208},{24,216},{32,224},{40,232},{48,240},{56,2... | collective-permute-start | bytes 393224 | tf_op jit(solution)/shard_map/ppermute | solution.py:29

commit v2 on v0

v2 whole, which is shorter than its diff:
```python
import functools

import jax
import jax.numpy as jnp
from jax import lax
from jax.experimental import pallas as pl
from jax.experimental.pallas import tpu as pltpu
from jax.sharding import PartitionSpec as P

F32, BF16 = jnp.float32, jnp.bfloat16
EPS = 1e-05
REP = (4, 4, 2)
FSDP = (4, 2)
MIB = 1 << 20
PARAMS = pltpu.CompilerParams(vmem_limit_bytes=20 * MIB)
ANY = pl.BlockSpec(memory_space=pl.ANY)
VMEM = pl.BlockSpec(memory_space=pltpu.VMEM)


def move(value, mesh_axis, sizes, axis, shift):
    total, stride = 1, 1
    for size in sizes:
        total *= size
    for size in sizes[axis + 1 :]:
        stride *= size
    pairs = []
    for index in range(total):
        at = index // stride % sizes[axis]
        pairs.append((index, index + ((at + shift) % sizes[axis] - at) * stride))
    return lax.ppermute(value, mesh_axis, pairs)


SLOW = 1 << 28
HBM = pl.BlockSpec(memory_space=pltpu.HBM)
DMA = pltpu.SemaphoreType.DMA


def like(shape, dtype):
    return jax.ShapeDtypeStruct(shape, dtype)


def x_of():
    return lax.axis_index("fsdp") // 2


def z_lo_of():
    return lax.axis_index("fsdp") % 2


def z_hi_of():
    return lax.axis_index("rep") // 8


def y_of():
    return lax.axis_index("rep") // 2 % 4


def core_of():
    return lax.axis_index("rep") % 2


def z_pairs(partner):
    return [(i, partner(i // 8) * 8 + i % 8) for i in range(32)]


def call(kernel, out_shape, flops=0, **rest):
    cost = pl.CostEstimate(flops=flops, bytes_accessed=0, transcendentals=0)
    return pl.pallas_call(
        kernel, out_shape=out_shape, compiler_params=PARAMS, cost_estimate=cost, **rest
    )


def in_hbm(array):
    return pltpu.with_memory_space_constraint(array, pltpu.HBM)


def gained(activations, norm_gain, shifts, after):
    rows, step, n = activations.shape[0], 1024, 2 * len(shifts)

    def kernel(a_ref, g_ref, after_ref, *refs):
        outs, (a_buf, sems), g_bufs = refs[: n // 2], refs[n // 2 : n // 2 + 2], refs[n // 2 + 2 :]
        copies = []
        for k in range(n):
            place = (x_of() + shifts[k // 2]) % 4 * 2 + (z_lo_of() + k % 2) % 2
            at = pl.ds(pl.multiple_of(place * step, step), step)
            copies.append(
                (
                    pltpu.make_async_copy(g_ref.at[at], g_bufs[k], sems.at[2 * k]),
                    pltpu.make_async_copy(a_ref.at[:, at], a_buf.at[k], sems.at[2 * k + 1]),
                )
            )
            for copy in copies[-1]:
                copy.start()
        for k in range(n):
            for copy in copies[k]:
                copy.wait()
            value = a_buf[k].astype(F32) * g_bufs[k][...].reshape(1, step)
            outs[k // 2][:, k % 2 * step : (k % 2 + 1) * step] = value.astype(BF16)

    return call(
        kernel,
        [like((rows, 2 * step), BF16)] * (n // 2),
        in_specs=[HBM, HBM, ANY],
        out_specs=[VMEM] * (n // 2),
        scratch_shapes=[pltpu.VMEM((n, rows, step), BF16), DMA((2 * n,))]
        + [pltpu.VMEM((step,), F32)] * n,
    )(in_hbm(activations), in_hbm(norm_gain), after)


def row_scale(activations, after):
    rows, width = activations.shape
    tile = 64

    def kernel(a_ref, after_ref, out_ref):
        wide = a_ref[...].astype(F32)
        out_ref[...] = lax.rsqrt(jnp.mean(wide * wide, axis=-1, keepdims=True) + EPS)

    return call(
        kernel,
        like((rows, 1), F32),
        grid=(rows // tile,),
        in_specs=[pl.BlockSpec((tile, width), lambda i: (i, 0)), ANY],
        out_specs=pl.BlockSpec((tile, 1), lambda i: (i, 0)),
    )(activations, after)


def pair_sum(mine, got, shift, after):
    shape = (2, 4, 4, 2, 32, 1024)

    def kernel(a_ref, b_ref, after_ref, out_ref):
        total = a_ref[...].astype(F32) + b_ref[...].astype(F32)
        out_ref[...] = total.astype(BF16).reshape(out_ref.shape)

    block = pl.BlockSpec(
        (1, 4, 1, 1, 32, 1024), lambda i: (i, 0, (y_of() + shift) % 4, core_of(), 0, 0)
    )
    return call(
        kernel,
        like((2, 4, 32, 1024), BF16),
        grid=(2,),
        in_specs=[block, block, ANY],
        out_specs=pl.BlockSpec((1, 4, 32, 1024), lambda i: (i, 0, 0, 0)),
    )(mine.reshape(shape), got.reshape(shape), after)


def line_sum(parts, after):
    def kernel(a, b, c, d, after_ref, send_ref, keep_ref):
        z_hi = z_hi_of()
        near = z_hi + 1 - 2 * (z_hi % 2)
        for ref, owner in ((send_ref, near), (keep_ref, z_hi)):
            for i, at in enumerate((owner, 3 - owner)):
                total = a[:, at].astype(F32) + b[:, at].astype(F32)
                total = total + c[:, at].astype(F32) + d[:, at].astype(F32)
                ref[i] = total.astype(BF16)

    return call(
        kernel,
        [like((2, 2, 32, 1024), BF16)] * 2,
        in_specs=[VMEM] * 4 + [ANY],
        out_specs=[VMEM] * 2,
    )(*parts, after)


def halves_sum(keep, got, after):
    def kernel(a_ref, b_ref, after_ref, own_ref, send_ref):
        own_ref[...] = a_ref[0].astype(F32) + b_ref[0].astype(F32)
        send_ref[...] = (a_ref[1].astype(F32) + b_ref[1].astype(F32)).astype(BF16)

    block = keep.shape[1:]
    return call(
        kernel,
        [like(block, F32), like(block, BF16)],
        SLOW,
        in_specs=[VMEM] * 2 + [ANY],
        out_specs=[VMEM] * 2,
    )(keep, got, after)


def add(parts, after):
    def kernel(*refs):
        total = refs[0][...].astype(F32)
        for ref in refs[1:-2]:
            total = total + ref[...].astype(F32)
        refs[-1][...] = total

    return call(
        kernel,
        like(parts[0].shape, F32),
        SLOW,
        in_specs=[VMEM] * len(parts) + [ANY],
        out_specs=VMEM,
    )(*parts, after)


TILE = 256


def half_product(a, half, w, dtype, plus, after):
    rows, (depth, width) = a.shape[0], w.shape

    def kernel(a_ref, w_ref, *refs):
        total = jnp.dot(a_ref[...], w_ref[...], preferred_element_type=F32)
        for ref in refs[: len(plus)]:
            total = total + ref[...].astype(F32)
        refs[-1][...] = total.astype(dtype)

    column = lambda j: (0, j)
    return call(
        kernel,
        like((rows, width), dtype),
        grid=(width // TILE,),
        in_specs=[
            pl.BlockSpec((rows, depth), lambda j: (0, half)),
            pl.BlockSpec((depth, TILE), column),
        ]
        + [pl.BlockSpec((rows, TILE), column)] * len(plus)
        + [ANY],
        out_specs=pl.BlockSpec((rows, TILE), column),
    )(a, w, *plus, after)


def products(acts, w, v, after):
    rows, depth, width = acts[0].shape[0], w.shape[0], w.shape[1]
    n = len(acts)

    def kernel(*refs):
        a_refs, (w_ref, v_ref, after_ref), outs = refs[:n], refs[n : n + 3], refs[n + 3 :]
        for j in range(0, width, TILE):
            at = slice(j, j + TILE)
            for a_ref, out_ref in zip(a_refs, outs):
                total = jnp.dot(a_ref[:, :depth], w_ref[:, at], preferred_element_type=F32)
                total = total + jnp.dot(
                    a_ref[:, depth:], v_ref[:, at], preferred_element_type=F32
                )
                out_ref[:, at] = total.astype(BF16)

    return call(
        kernel,
        [like((rows, width), BF16)] * n,
        in_specs=[VMEM] * (n + 2) + [ANY],
        out_specs=[VMEM] * n,
    )(*acts, w, v, after)


def last_sum(own, parts, scale):
    rows, width = own.shape

    def kernel(own_ref, a_ref, b_ref, scale_ref, out_ref):
        total = own_ref[...] + a_ref[...].astype(F32) + b_ref[...].astype(F32)
        out_ref[...] = (total * scale_ref[...]).astype(BF16)

    return call(kernel, like((rows, width), BF16), in_specs=[VMEM] * 4, out_specs=VMEM)(
        own, *parts, scale
    )


def shards(local_fragment, anchor, momentum, next_weights, activations, norm_gain):
    replicas = lax.axis_size("rep")
    along_x = lambda v, s: move(v, "fsdp", FSDP, 0, s)
    along_y = lambda v, s: move(v, "rep", REP, 1, s)
    mine, fragment = next_weights[0], local_fragment[0]

    other = move(mine, "fsdp", FSDP, 1, 1)
    sibling = move(fragment, "rep", REP, 2, 1)

    (a2,) = gained(activations, norm_gain, [2], norm_gain)
    far_a = along_x(a2, 2)
    a1, a3 = gained(activations, norm_gain, [1, 3], a2)
    down_a, up_a = along_x(a1, 1), along_x(a3, 3)
    scale = row_scale(activations, a1)
    (a0,) = gained(activations, norm_gain, [0], scale)

    s1 = pair_sum(fragment, sibling, 1, a0)
    y1 = along_y(s1, 1)
    s3 = pair_sum(fragment, sibling, 3, s1)
    y3 = along_y(s3, 3)
    s0 = pair_sum(fragment, sibling, 0, s3)
    own = half_product(a0, 0, mine, F32, [], s0)
    s2 = pair_sum(fragment, sibling, 2, y1)
    y2 = along_y(s2, 2)
    far = half_product(far_a, 0, mine, F32, [], s2)
    send, keep = line_sum([s0, y1, y2, y3], far)
    got = lax.ppermute(send, "rep", z_pairs(lambda z: z ^ 1))

    far = half_product(far_a, 1, other, BF16, [far], send)
    far_got = along_x(far, 2)
    to_up, to_down = products([up_a, down_a], mine, other, far)
    got_down, got_up = along_x(to_up, 1), along_x(to_down, 3)
    own = half_product(a0, 1, other, F32, [own], to_up)
    total, send = halves_sum(keep, got, own)
    got = lax.ppermute(send, "rep", z_pairs(lambda z: 3 - z))
    own = add([own, far_got], send)

    total = total + got.astype(F32)
    pseudo = anchor - total / replicas
    new_momentum = 0.9 * momentum + pseudo
    new_anchor = anchor - 0.7 * (pseudo + 0.9 * new_momentum)
    result = last_sum(own, [got_up, got_down], scale)
    return (new_anchor, new_momentum, result)


def solution(mesh):
    placed = (
        P("rep", None, "fsdp", None),
        P(None, ("fsdp", "rep"), None),
        P(None, ("fsdp", "rep"), None),
        P("rep", "fsdp", None),
        P(("rep", "fsdp"), None),
        P(),
    )
    return jax.shard_map(
        shards,
        mesh=mesh,
        in_specs=placed,
        out_specs=(
            P(None, ("fsdp", "rep"), None),
            P(None, ("fsdp", "rep"), None),
            P(("rep", "fsdp"), None),
        ),
        check_vma=False,
    )
```

time: 389 us -> 84.9 us (0.22)
  the two profiles are of different devices: /device:TPU:8 before, /device:TPU:1 now
where the time goes in v2:
time: 84.9 us; the launch traced here: 84.8 us
  waiting for transfers between devices  43.9 us (52%)
  starting transfers between devices  21.4 us (25%)
  Pallas kernels  17.7 us (21%)
  other arithmetic  0.88 us (1%)
    ppermute x11, waiting for transfers between devices, move(): return lax.ppermute(value, mesh_axis, pairs)  40.6 us
    ppermute x11, starting transfers between devices, move(): return lax.ppermute(value, mesh_axis, pairs)  15.7 us
    pallas_call x4, Pallas kernels, half_product(): call(kernel, like((rows, width), dtype), grid=(width // TILE,), in_specs=...  6.76 us
    pallas_call x3, Pallas kernels, gained(): call(kernel, [like((rows, 2 * step), BF16)] * (n // 2), in_specs=[HBM, HB...  4.62 us
    ppermute x1, waiting for transfers between devices, shards(): got = lax.ppermute(send, 'rep', z_pairs(lambda z: 3 - z))  3.27 us
    ppermute x1, starting transfers between devices, shards(): got = lax.ppermute(send, 'rep', z_pairs(lambda z: 3 - z))  3.04 us
    ppermute x1, starting transfers between devices, shards(): got = lax.ppermute(send, 'rep', z_pairs(lambda z: z ^ 1))  2.61 us
    pallas_call x1, Pallas kernels, products(): call(kernel, [like((rows, width), BF16)] * n, in_specs=[VMEM] * (n + 2) +...  2.33 us
  transfers between devices with their start and end apart: 13, of which 8 were waited for; matrix products, arithmetic and copies ran while one was open for 1% of the time, Pallas kernels for 20%

profile of v2, /device:TPU:1, one launch (start us, length us, event | category | flops | bytes accessed | tf_op | source)
XLA Modules:
  0.0 84.8 jit_solution(13448501418785916421)
XLA Ops:
  0.6 3.3 %collective-permute-start = (bf16[2,1024,1024]{2,1,0:T(8,128)(2,1)}, bf16[2,1024,1024]{2,1,0:T(8,128)(2,1)S(1)}, u32[]{:S(2)}, u32[]{:S(2)}) collective-permute-start(bf16[2,1024,1024]{2,1,0:T(8,128)(2,1)} %bitcast.4), channel_id=1, source_target_pairs={{0,8},{8,0},{16,24},{24,16},{32,40},{40,32},{48,56},{56,48},{64,72... | collective-permute-start | bytes 12582920 | tf_op jit(solution)/shard_map/ppermute | solution.py:30
  4.0 1.5 %shard_map.85.after_ref = bf16[256,2048]{1,0:T(8,128)(2,1)S(1)} custom-call(bf16[256,8192]{1,0:T(8,128)(2,1)} %a_ref.7, f32[8192]{0:T(1024)} %g_ref.5, f32[8192]{0:T(1024)} %g_ref.5), custom_call_target="tpu_custom_call" | custom-call | tf_op jit(solution)/shard_map/pallas_call | solution.py:100
  5.5 2.6 %collective-permute-start.4 = (bf16[256,2048]{1,0:T(8,128)(2,1)S(1)}, bf16[256,2048]{1,0:T(8,128)(2,1)S(1)}, u32[]{:S(2)}, u32[]{:S(2)}) collective-permute-start(bf16[256,2048]{1,0:T(8,128)(2,1)S(1)} %shard_map.85.after_ref), channel_id=1, source_target_pairs={{0,4},{1,5},{2,6},{3,7},{4,0},{5,1},{6,2},{7,3},{8,12},{9,13},{10,... | collective-permute-start | bytes 3145736 | tf_op jit(solution)/shard_map/ppermute | solution.py:30
  8.1 1.7 %shard_map.86 = (bf16[256,2048]{1,0:T(8,128)(2,1)S(1)}, bf16[256,2048]{1,0:T(8,128)(2,1)S(1)}) custom-call(bf16[256,8192]{1,0:T(8,128)(2,1)} %a_ref.7, f32[8192]{0:T(1024)} %g_ref.5, bf16[256,2048]{1,0:T(8,128)(2,1)S(1)} %shard_map.85.after_ref), custom_call_target="tpu_custom_call" | custom-call | tf_op jit(solution)/shard_map/pallas_call | solution.py:100
  9.9 1.3 %shard_map.87.after_ref.scale_ref = f32[256,1]{1,0:T(8,128)S(1)} custom-call(bf16[256,8192]{1,0:T(8,128)(2,1)S(1)} %copy-done, bf16[256,2048]{1,0:T(8,128)(2,1)S(1)} %get-tuple-element.11.after_ref), custom_call_target="tpu_custom_call" | custom-call | tf_op jit(solution)/shard_map/pallas_call | solution.py:118
  11.1 1.4 %shard_map.88.after_ref.a_ref = bf16[256,2048]{1,0:T(8,128)(2,1)S(1)} custom-call(bf16[256,8192]{1,0:T(8,128)(2,1)} %a_ref.7, f32[8192]{0:T(1024)} %g_ref.5, f32[256,1]{1,0:T(8,128)S(1)} %shard_map.87.after_ref.scale_ref), custom_call_target="tpu_custom_call" | custom-call | tf_op jit(solution)/shard_map/pallas_call | solution.py:100
  12.5 0.4 shard_map.89.after_ref
  12.9 1.4 %collective-permute-start.1 = (bf16[2,4,32,1024]{3,2,1,0:T(8,128)(2,1)S(1)}, bf16[2,4,32,1024]{3,2,1,0:T(8,128)(2,1)S(1)}, u32[]{:S(2)}, u32[]{:S(2)}) collective-permute-start(bf16[2,4,32,1024]{3,2,1,0:T(8,128)(2,1)S(1)} %shard_map.89.after_ref), channel_id=1, source_target_pairs={{0,16},{8,24},{16,32},{24,40},{32,48},{40,56},{48,0},{56,8},{64,80... | collective-permute-start | bytes 1572872 | tf_op jit(solution)/shard_map/ppermute | solution.py:30
  14.3 0.9 %collective-permute-start.7 = (bf16[256,2048]{1,0:T(8,128)(2,1)S(1)}, bf16[256,2048]{1,0:T(8,128)(2,1)S(1)}, u32[]{:S(2)}, u32[]{:S(2)}) collective-permute-start(bf16[256,2048]{1,0:T(8,128)(2,1)S(1)} %get-tuple-element.14), channel_id=1, source_target_pairs={{0,6},{1,7},{2,0},{3,1},{4,2},{5,3},{6,4},{7,5},{8,14},{9,15},{10,... | collective-permute-start | bytes 3145736 | tf_op jit(solution)/shard_map/ppermute | solution.py:30
  15.1 0.6 collective-permute-start.8
  16.1 11.1 %collective-permute-done.1.after_ref.b = bf16[2,4,32,1024]{3,2,1,0:T(8,128)(2,1)S(1)} collective-permute-done((bf16[2,4,32,1024]{3,2,1,0:T(8,128)(2,1)S(1)}, bf16[2,4,32,1024]{3,2,1,0:T(8,128)(2,1)S(1)}, u32[]{:S(2)}, u32[]{:S(2)}) %collective-permute-start.1) | collective-permute-done | bytes 524320 | tf_op jit(solution)/shard_map/ppermute | solution.py:30
  27.2 1.4 %collective-permute-start.3 = (bf16[2,4,32,1024]{3,2,1,0:T(8,128)(2,1)S(1)}, bf16[2,4,32,1024]{3,2,1,0:T(8,128)(2,1)S(1)}, u32[]{:S(2)}, u32[]{:S(2)}) collective-permute-start(bf16[2,4,32,1024]{3,2,1,0:T(8,128)(2,1)S(1)} %shard_map.90.after_ref), channel_id=1, source_target_pairs={{0,48},{8,56},{16,0},{24,8},{32,16},{40,24},{48,32},{56,40},{64,11... | collective-permute-start | bytes 1572872 | tf_op jit(solution)/shard_map/ppermute | solution.py:30
  28.9 2.7 %collective-permute-done.4.a_ref = bf16[256,2048]{1,0:T(8,128)(2,1)S(1)} collective-permute-done((bf16[256,2048]{1,0:T(8,128)(2,1)S(1)}, bf16[256,2048]{1,0:T(8,128)(2,1)S(1)}, u32[]{:S(2)}, u32[]{:S(2)}) %collective-permute-start.4) | collective-permute-done | bytes 1048608 | tf_op jit(solution)/shard_map/ppermute | solution.py:30
  31.6 2.6 %collective-permute-start.2 = (bf16[2,4,32,1024]{3,2,1,0:T(8,128)(2,1)S(1)}, bf16[2,4,32,1024]{3,2,1,0:T(8,128)(2,1)S(1)}, u32[]{:S(2)}, u32[]{:S(2)}) collective-permute-start(bf16[2,4,32,1024]{3,2,1,0:T(8,128)(2,1)S(1)} %shard_map.92.refs_0_), channel_id=1, source_target_pairs={{0,32},{8,40},{16,48},{24,56},{32,0},{40,8},{48,16},{56,24},{64,96... | collective-permute-start | bytes 1572872 | tf_op jit(solution)/shard_map/ppermute | solution.py:30
  34.5 1.7 %shard_map.93.after_ref.refs_0_ = f32[256,1024]{1,0:T(8,128)S(1)} custom-call(bf16[256,2048]{1,0:T(8,128)(2,1)S(1)} %collective-permute-done.4.a_ref, bf16[1024,1024]{1,0:T(8,128)(2,1)S(1)} %bitcast.14, bf16[2,4,32,1024]{3,2,1,0:T(8,128)(2,1)S(1)} %shard_map.92.refs_0_), custom_call_target="tpu_custom_call" | custom-call | tf_op jit(solution)/shard_map/pallas_call | solution.py:208
  36.2 2.9 %collective-permute-done.3.d = bf16[2,4,32,1024]{3,2,1,0:T(8,128)(2,1)S(1)} collective-permute-done((bf16[2,4,32,1024]{3,2,1,0:T(8,128)(2,1)S(1)}, bf16[2,4,32,1024]{3,2,1,0:T(8,128)(2,1)S(1)}, u32[]{:S(2)}, u32[]{:S(2)}) %collective-permute-start.3) | collective-permute-done | bytes 524320 | tf_op jit(solution)/shard_map/ppermute | solution.py:30
  39.1 5.5 %collective-permute-done.2.c = bf16[2,4,32,1024]{3,2,1,0:T(8,128)(2,1)S(1)} collective-permute-done((bf16[2,4,32,1024]{3,2,1,0:T(8,128)(2,1)S(1)}, bf16[2,4,32,1024]{3,2,1,0:T(8,128)(2,1)S(1)}, u32[]{:S(2)}, u32[]{:S(2)}) %collective-permute-start.2) | collective-permute-done | bytes 524320 | tf_op jit(solution)/shard_map/ppermute | solution.py:30
  44.9 2.6 %collective-permute-start.5 = (bf16[2,2,32,1024]{3,2,1,0:T(8,128)(2,1)S(1)}, bf16[2,2,32,1024]{3,2,1,0:T(8,128)(2,1)S(1)}, u32[]{:S(2)}, u32[]{:S(2)}) collective-permute-start(bf16[2,2,32,1024]{3,2,1,0:T(8,128)(2,1)S(1)} %get-tuple-element.13.refs_1_), channel_id=1, source_target_pairs={{0,64},{8,72},{16,80},{24,88},{32,96},{40,104},{48,112},{56,120},{... | collective-permute-start | bytes 786440 | tf_op jit(solution)/shard_map/ppermute | solution.py:283
  47.6 7.8 %collective-permute-done.6.w_ref.refs_3_ = bf16[1024,1024]{1,0:T(8,128)(2,1)S(1)} collective-permute-done((bf16[1024,1024]{1,0:T(8,128)(2,1)}, bf16[1024,1024]{1,0:T(8,128)(2,1)S(1)}, u32[]{:S(2)}, u32[]{:S(2)}) %collective-permute-start.6) | collective-permute-done | bytes 2097184 | tf_op jit(solution)/shard_map/ppermute | solution.py:30
  55.4 1.7 %shard_map.96.refs_4_ = bf16[256,1024]{1,0:T(8,128)(2,1)S(1)} custom-call(bf16[256,2048]{1,0:T(8,128)(2,1)S(1)} %collective-permute-done.4.a_ref, bf16[1024,1024]{1,0:T(8,128)(2,1)S(1)} %collective-permute-done.6.w_ref.refs_3_, f32[256,1024]{1,0:T(8,128)S(1)} %shard_map.93.after_ref.refs_0_, bf16[2,2,32,1024]{3,2,1,0:T(8,128)(2,1)S(1)} %get-tuple-element.13.refs_1_), custom_call_target="tpu_custom_call" | custom-call | tf_op jit(solution)/shard_map/pallas_call | solution.py:208
  57.1 1.4 %collective-permute-start.10 = (bf16[256,1024]{1,0:T(8,128)(2,1)S(1)}, bf16[256,1024]{1,0:T(8,128)(2,1)S(1)}, u32[]{:S(2)}, u32[]{:S(2)}) collective-permute-start(bf16[256,1024]{1,0:T(8,128)(2,1)S(1)} %shard_map.96.refs_4_), channel_id=1, source_target_pairs={{0,4},{1,5},{2,6},{3,7},{4,0},{5,1},{6,2},{7,3},{8,12},{9,13},{10,... | collective-permute-start | bytes 1572872 | tf_op jit(solution)/shard_map/ppermute | solution.py:30
  58.5 2.3 %shard_map.97 = (bf16[256,1024]{1,0:T(8,128)(2,1)S(1)}, bf16[256,1024]{1,0:T(8,128)(2,1)S(1)}) custom-call(bf16[256,2048]{1,0:T(8,128)(2,1)S(1)} %collective-permute-done.7.refs_0_, bf16[256,2048]{1,0:T(8,128)(2,1)S(1)} %collective-permute-done.8.refs_1_, bf16[1024,1024]{1,0:T(8,128)(2,1)S(1)} %bitcast.15, ...), custom_call_target="tpu_custom_call" | custom-call | tf_op jit(solution)/shard_map/pallas_call | solution.py:237
  60.8 0.9 %collective-permute-start.11 = (bf16[256,1024]{1,0:T(8,128)(2,1)S(1)}, bf16[256,1024]{1,0:T(8,128)(2,1)S(1)}, u32[]{:S(2)}, u32[]{:S(2)}) collective-permute-start(bf16[256,1024]{1,0:T(8,128)(2,1)S(1)} %get-tuple-element.18), channel_id=1, source_target_pairs={{0,6},{1,7},{2,0},{3,1},{4,2},{5,3},{6,4},{7,5},{8,14},{9,15},{10,... | collective-permute-start | bytes 1572872 | tf_op jit(solution)/shard_map/ppermute | solution.py:30
  61.8 0.6 collective-permute-start.12
  62.4 1.6 %shard_map.95.refs_0_ = f32[256,1024]{1,0:T(8,128)S(1)} custom-call(bf16[256,2048]{1,0:T(8,128)(2,1)S(1)} %shard_map.88.after_ref.a_ref, bf16[1024,1024]{1,0:T(8,128)(2,1)S(1)} %bitcast.16, bf16[2,4,32,1024]{3,2,1,0:T(8,128)(2,1)S(1)} %shard_map.91.a.refs_0_), custom_call_target="tpu_custom_call" | custom-call | tf_op jit(solution)/shard_map/pallas_call | solution.py:208
  64.1 1.7 %shard_map.98.after_ref.refs_0_ = f32[256,1024]{1,0:T(8,128)S(1)} custom-call(bf16[256,2048]{1,0:T(8,128)(2,1)S(1)} %shard_map.88.after_ref.a_ref, bf16[1024,1024]{1,0:T(8,128)(2,1)S(1)} %collective-permute-done.6.w_ref.refs_3_, f32[256,1024]{1,0:T(8,128)S(1)} %shard_map.95.refs_0_, bf16[256,1024]{1,0:T(8,128)(2,1)S(1)} %get-tuple-element.15.refs_1_), custom_call_target="tpu_custom_call" | custom-call | tf_op jit(solution)/shard_map/pallas_call | solution.py:208
  65.9 3.0 %collective-permute-start.9 = (bf16[2,32,1024]{2,1,0:T(8,128)(2,1)S(1)}, bf16[2,32,1024]{2,1,0:T(8,128)(2,1)S(1)}, u32[]{:S(2)}, u32[]{:S(2)}) collective-permute-start(bf16[2,32,1024]{2,1,0:T(8,128)(2,1)S(1)} %get-tuple-element.17.refs_2_), channel_id=1, source_target_pairs={{0,192},{8,200},{16,208},{24,216},{32,224},{40,232},{48,240},{56,2... | collective-permute-start | bytes 393224 | tf_op jit(solution)/shard_map/ppermute | solution.py:291
  68.9 3.3 %collective-permute-done.9 = bf16[2,32,1024]{2,1,0:T(8,128)(2,1)S(1)} collective-permute-done((bf16[2,32,1024]{2,1,0:T(8,128)(2,1)S(1)}, bf16[2,32,1024]{2,1,0:T(8,128)(2,1)S(1)}, u32[]{:S(2)}, u32[]{:S(2)}) %collective-permute-start.9) | collective-permute-done | bytes 131104 | tf_op jit(solution)/shard_map/ppermute | solution.py:291
  72.2 0.9 %multiply_subtract_fusion = (f32[2,32,1024]{2,1,0:T(8,128)}, f32[2,32,1024]{2,1,0:T(8,128)}) fusion(f32[2,32,1024]{2,1,0:T(8,128)S(1)} %copy-done.3, f32[2,32,1024]{2,1,0:T(8,128)S(1)} %get-tuple-element.16, bf16[2,32,1024]{2,1,0:T(8,128)(2,1)S(1)} %collective-permute-done.9, f32[2,32,1024]{2,1,0:T(8,128)S(1)} %copy-done.4), kind=kLoop, calls=%fused_computation | loop fusion | flops 655360 | bytes 1441792 | tf_op jit(solution)/shard_map/sub | solution.py:297
  73.2 8.2 %collective-permute-done.11.a_ref = bf16[256,1024]{1,0:T(8,128)(2,1)S(1)} collective-permute-done((bf16[256,1024]{1,0:T(8,128)(2,1)S(1)}, bf16[256,1024]{1,0:T(8,128)(2,1)S(1)}, u32[]{:S(2)}, u32[]{:S(2)}) %collective-permute-start.11) | collective-permute-done | bytes 524320 | tf_op jit(solution)/shard_map/ppermute | solution.py:30
  81.4 2.4 %collective-permute-done.12.b_ref = bf16[256,1024]{1,0:T(8,128)(2,1)S(1)} collective-permute-done((bf16[256,1024]{1,0:T(8,128)(2,1)S(1)}, bf16[256,1024]{1,0:T(8,128)(2,1)S(1)}, u32[]{:S(2)}, u32[]{:S(2)}) %collective-permute-start.12) | collective-permute-done | bytes 524320 | tf_op jit(solution)/shard_map/ppermute | solution.py:30
  83.8 1.0 %shard_map.101 = bf16[256,1024]{1,0:T(8,128)(2,1)} custom-call(f32[256,1024]{1,0:T(8,128)S(1)} %shard_map.100.own_ref, bf16[256,1024]{1,0:T(8,128)(2,1)S(1)} %collective-permute-done.11.a_ref, bf16[256,1024]{1,0:T(8,128)(2,1)S(1)} %collective-permute-done.12.b_ref, f32[256,1]{1,0:T(8,128)S(1)} %shard_map.87.after_ref.scale_ref), custom_call_target="tpu_custom_call" | custom-call | tf_op jit(solution)/shard_map/pallas_call | solution.py:252
  (22 shorter events, 1.4 us)
Async XLA Ops:
  0.6 11.9 %collective-permute-start = (bf16[2,1024,1024]{2,1,0:T(8,128)(2,1)}, bf16[2,1024,1024]{2,1,0:T(8,128)(2,1)S(1)}, u32[]{:S(2)}, u32[]{:S(2)}) collective-permute-start(bf16[2,1024,1024]{2,1,0:T(8,128)(2,1)} %bitcast.4), channel_id=1, source_target_pairs={{0,8},{8,0},{16,24},{24,16},{32,40},{40,32},{48,56},{56,48},{64,72... | collective-permute-start | bytes 12582920 | tf_op jit(solution)/shard_map/ppermute | solution.py:30
  4.0 5.9 %copy-start = (bf16[256,8192]{1,0:T(8,128)(2,1)S(1)}, bf16[256,8192]{1,0:T(8,128)(2,1)}, u32[]{:S(2)}) copy-start(bf16[256,8192]{1,0:T(8,128)(2,1)} %a_ref.7) | copy-start | bytes 12582916
  4.0 51.4 %collective-permute-start.6 = (bf16[1024,1024]{1,0:T(8,128)(2,1)}, bf16[1024,1024]{1,0:T(8,128)(2,1)S(1)}, u32[]{:S(2)}, u32[]{:S(2)}) collective-permute-start(bf16[1024,1024]{1,0:T(8,128)(2,1)} %bitcast.13), channel_id=1, source_target_pairs={{0,1},{1,0},{2,3},{3,2},{4,5},{5,4},{6,7},{7,6},{8,9},{9,8},{10,11... | collective-permute-start | bytes 6291464 | tf_op jit(solution)/shard_map/ppermute | solution.py:30
  5.5 26.1 %collective-permute-start.4 = (bf16[256,2048]{1,0:T(8,128)(2,1)S(1)}, bf16[256,2048]{1,0:T(8,128)(2,1)S(1)}, u32[]{:S(2)}, u32[]{:S(2)}) collective-permute-start(bf16[256,2048]{1,0:T(8,128)(2,1)S(1)} %shard_map.85.after_ref), channel_id=1, source_target_pairs={{0,4},{1,5},{2,6},{3,7},{4,0},{5,1},{6,2},{7,3},{8,12},{9,13},{10,... | collective-permute-start | bytes 3145736 | tf_op jit(solution)/shard_map/ppermute | solution.py:30
  9.8 2.7 %copy-start.1 = (bf16[1,2,1024,1024]{3,2,1,0:T(8,128)(2,1)S(1)}, bf16[1,2,1024,1024]{3,2,1,0:T(8,128)(2,1)}, u32[]{:S(2)}) copy-start(bf16[1,2,1024,1024]{3,2,1,0:T(8,128)(2,1)} %param.6) | copy-start | bytes 12582916
  12.9 14.2 %collective-permute-start.1 = (bf16[2,4,32,1024]{3,2,1,0:T(8,128)(2,1)S(1)}, bf16[2,4,32,1024]{3,2,1,0:T(8,128)(2,1)S(1)}, u32[]{:S(2)}, u32[]{:S(2)}) collective-permute-start(bf16[2,4,32,1024]{3,2,1,0:T(8,128)(2,1)S(1)} %shard_map.89.after_ref), channel_id=1, source_target_pairs={{0,16},{8,24},{16,32},{24,40},{32,48},{40,56},{48,0},{56,8},{64,80... | collective-permute-start | bytes 1572872 | tf_op jit(solution)/shard_map/ppermute | solution.py:30
  14.3 44.2 %collective-permute-start.7 = (bf16[256,2048]{1,0:T(8,128)(2,1)S(1)}, bf16[256,2048]{1,0:T(8,128)(2,1)S(1)}, u32[]{:S(2)}, u32[]{:S(2)}) collective-permute-start(bf16[256,2048]{1,0:T(8,128)(2,1)S(1)} %get-tuple-element.14), channel_id=1, source_target_pairs={{0,6},{1,7},{2,0},{3,1},{4,2},{5,3},{6,4},{7,5},{8,14},{9,15},{10,... | collective-permute-start | bytes 3145736 | tf_op jit(solution)/shard_map/ppermute | solution.py:30
  15.1 43.4 %collective-permute-start.8 = (bf16[256,2048]{1,0:T(8,128)(2,1)S(1)}, bf16[256,2048]{1,0:T(8,128)(2,1)S(1)}, u32[]{:S(2)}, u32[]{:S(2)}) collective-permute-start(bf16[256,2048]{1,0:T(8,128)(2,1)S(1)} %get-tuple-element.11.after_ref), channel_id=1, source_target_pairs={{0,2},{1,3},{2,4},{3,5},{4,6},{5,7},{6,0},{7,1},{8,10},{9,11},{10,... | collective-permute-start | bytes 3145736 | tf_op jit(solution)/shard_map/ppermute | solution.py:30
  27.2 12.0 %collective-permute-start.3 = (bf16[2,4,32,1024]{3,2,1,0:T(8,128)(2,1)S(1)}, bf16[2,4,32,1024]{3,2,1,0:T(8,128)(2,1)S(1)}, u32[]{:S(2)}, u32[]{:S(2)}) collective-permute-start(bf16[2,4,32,1024]{3,2,1,0:T(8,128)(2,1)S(1)} %shard_map.90.after_ref), channel_id=1, source_target_pairs={{0,48},{8,56},{16,0},{24,8},{32,16},{40,24},{48,32},{56,40},{64,11... | collective-permute-start | bytes 1572872 | tf_op jit(solution)/shard_map/ppermute | solution.py:30
  28.9 5.6 %copy-start.2 = (bf16[1,1024,1024]{2,1,0:T(8,128)(2,1)S(1)}, bf16[1,1024,1024]{2,1,0:T(8,128)(2,1)}, u32[]{:S(2)}) copy-start(bf16[1,1024,1024]{2,1,0:T(8,128)(2,1)} %param.9) | copy-start | bytes 6291460
  31.6 13.1 %collective-permute-start.2 = (bf16[2,4,32,1024]{3,2,1,0:T(8,128)(2,1)S(1)}, bf16[2,4,32,1024]{3,2,1,0:T(8,128)(2,1)S(1)}, u32[]{:S(2)}, u32[]{:S(2)}) collective-permute-start(bf16[2,4,32,1024]{3,2,1,0:T(8,128)(2,1)S(1)} %shard_map.92.refs_0_), channel_id=1, source_target_pairs={{0,32},{8,40},{16,48},{24,56},{32,0},{40,8},{48,16},{56,24},{64,96... | collective-permute-start | bytes 1572872 | tf_op jit(solution)/shard_map/ppermute | solution.py:30
  44.9 20.9 %collective-permute-start.5 = (bf16[2,2,32,1024]{3,2,1,0:T(8,128)(2,1)S(1)}, bf16[2,2,32,1024]{3,2,1,0:T(8,128)(2,1)S(1)}, u32[]{:S(2)}, u32[]{:S(2)}) collective-permute-start(bf16[2,2,32,1024]{3,2,1,0:T(8,128)(2,1)S(1)} %get-tuple-element.13.refs_1_), channel_id=1, source_target_pairs={{0,64},{8,72},{16,80},{24,88},{32,96},{40,104},{48,112},{56,120},{... | collective-permute-start | bytes 786440 | tf_op jit(solution)/shard_map/ppermute | solution.py:283
  57.1 16.0 %collective-permute-start.10 = (bf16[256,1024]{1,0:T(8,128)(2,1)S(1)}, bf16[256,1024]{1,0:T(8,128)(2,1)S(1)}, u32[]{:S(2)}, u32[]{:S(2)}) collective-permute-start(bf16[256,1024]{1,0:T(8,128)(2,1)S(1)} %shard_map.96.refs_4_), channel_id=1, source_target_pairs={{0,4},{1,5},{2,6},{3,7},{4,0},{5,1},{6,2},{7,3},{8,12},{9,13},{10,... | collective-permute-start | bytes 1572872 | tf_op jit(solution)/shard_map/ppermute | solution.py:30
  60.8 20.6 %collective-permute-start.11 = (bf16[256,1024]{1,0:T(8,128)(2,1)S(1)}, bf16[256,1024]{1,0:T(8,128)(2,1)S(1)}, u32[]{:S(2)}, u32[]{:S(2)}) collective-permute-start(bf16[256,1024]{1,0:T(8,128)(2,1)S(1)} %get-tuple-element.18), channel_id=1, source_target_pairs={{0,6},{1,7},{2,0},{3,1},{4,2},{5,3},{6,4},{7,5},{8,14},{9,15},{10,... | collective-permute-start | bytes 1572872 | tf_op jit(solution)/shard_map/ppermute | solution.py:30
  61.8 22.0 %collective-permute-start.12 = (bf16[256,1024]{1,0:T(8,128)(2,1)S(1)}, bf16[256,1024]{1,0:T(8,128)(2,1)S(1)}, u32[]{:S(2)}, u32[]{:S(2)}) collective-permute-start(bf16[256,1024]{1,0:T(8,128)(2,1)S(1)} %get-tuple-element.15.refs_1_), channel_id=1, source_target_pairs={{0,2},{1,3},{2,4},{3,5},{4,6},{5,7},{6,0},{7,1},{8,10},{9,11},{10,... | collective-permute-start | bytes 1572872 | tf_op jit(solution)/shard_map/ppermute | solution.py:30
  64.0 8.2 %copy-start.3 = (f32[2,32,1024]{2,1,0:T(8,128)S(1)}, f32[2,32,1024]{2,1,0:T(8,128)}, u32[]{:S(2)}) copy-start(f32[2,32,1024]{2,1,0:T(8,128)} %param.7) | copy-start | bytes 786436
  64.0 8.2 %copy-start.4 = (f32[2,32,1024]{2,1,0:T(8,128)S(1)}, f32[2,32,1024]{2,1,0:T(8,128)}, u32[]{:S(2)}) copy-start(f32[2,32,1024]{2,1,0:T(8,128)} %param.8) | copy-start | bytes 786436
  65.9 6.3 %collective-permute-start.9 = (bf16[2,32,1024]{2,1,0:T(8,128)(2,1)S(1)}, bf16[2,32,1024]{2,1,0:T(8,128)(2,1)S(1)}, u32[]{:S(2)}, u32[]{:S(2)}) collective-permute-start(bf16[2,32,1024]{2,1,0:T(8,128)(2,1)S(1)} %get-tuple-element.17.refs_2_), channel_id=1, source_target_pairs={{0,192},{8,200},{16,208},{24,216},{32,224},{40,232},{48,240},{56,2... | collective-permute-start | bytes 393224 | tf_op jit(solution)/shard_map/ppermute | solution.py:291

commit v3 on v2

v3 whole, which is shorter than its diff:
```python
import functools

import jax
import jax.numpy as jnp
from jax import lax
from jax.experimental import pallas as pl
from jax.experimental.pallas import tpu as pltpu
from jax.sharding import PartitionSpec as P

F32, BF16 = jnp.float32, jnp.bfloat16
EPS = 1e-05
MIB = 1 << 20
PARAMS = pltpu.CompilerParams(vmem_limit_bytes=20 * MIB)
ANY = pl.BlockSpec(memory_space=pl.ANY)
VMEM = pl.BlockSpec(memory_space=pltpu.VMEM)


def first(at, core):
    return (at + 1 - 2 * ((at + core) % 2)) % 4


def second(at, core):
    return (at + 3 + 2 * ((at + core) % 2)) % 4


def move(value, target):
    pairs = []
    for source in range(256):
        z_hi, y, core = source // 64, source // 16 % 4, source // 8 % 2
        x, z_lo = source // 2 % 4, source % 2
        z_hi, y, core, x, z_lo = target(z_hi, y, core, x, z_lo)
        pairs.append((source, (((z_hi * 4 + y) * 2 + core) * 4 + x) * 2 + z_lo))
    return lax.ppermute(value, ("rep", "fsdp"), pairs)


SLOW = 1 << 28
HBM = pl.BlockSpec(memory_space=pltpu.HBM)
DMA = pltpu.SemaphoreType.DMA


def like(shape, dtype):
    return jax.ShapeDtypeStruct(shape, dtype)


def x_of():
    return lax.axis_index("fsdp") // 2


def z_lo_of():
    return lax.axis_index("fsdp") % 2


def z_hi_of():
    return lax.axis_index("rep") // 8


def y_of():
    return lax.axis_index("rep") // 2 % 4


def core_of():
    return lax.axis_index("rep") % 2


def call(kernel, out_shape, flops=0, **rest):
    cost = pl.CostEstimate(flops=flops, bytes_accessed=0, transcendentals=0)
    return pl.pallas_call(
        kernel, out_shape=out_shape, compiler_params=PARAMS, cost_estimate=cost, **rest
    )


def in_hbm(array):
    return pltpu.with_memory_space_constraint(array, pltpu.HBM)


def gained(activations, norm_gain, owners, after):
    rows, step, n = activations.shape[0], 1024, 2 * len(owners)

    def kernel(a_ref, g_ref, after_ref, *refs):
        outs, (a_buf, sems), g_bufs = refs[: n // 2], refs[n // 2 : n // 2 + 2], refs[n // 2 + 2 :]
        copies = []
        for k in range(n):
            place = owners[k // 2]() * 2 + (z_lo_of() + k % 2) % 2
            at = pl.ds(pl.multiple_of(place * step, step), step)
            copies.append(
                (
                    pltpu.make_async_copy(g_ref.at[at], g_bufs[k], sems.at[2 * k]),
                    pltpu.make_async_copy(a_ref.at[:, at], a_buf.at[k], sems.at[2 * k + 1]),
                )
            )
            for copy in copies[-1]:
                copy.start()
        for k in range(n):
            for copy in copies[k]:
                copy.wait()
            value = a_buf[k].astype(F32) * g_bufs[k][...].reshape(1, step)
            outs[k // 2][:, k % 2 * step : (k % 2 + 1) * step] = value.astype(BF16)

    return call(
        kernel,
        [like((rows, 2 * step), BF16)] * (n // 2),
        in_specs=[HBM, HBM, ANY],
        out_specs=[VMEM] * (n // 2),
        scratch_shapes=[pltpu.VMEM((n, rows, step), BF16), DMA((2 * n,))]
        + [pltpu.VMEM((step,), F32)] * n,
    )(in_hbm(activations), in_hbm(norm_gain), after)


def row_scale(activations, after):
    rows, width = activations.shape
    tile = 64

    def kernel(a_ref, after_ref, out_ref):
        wide = a_ref[...].astype(F32)
        out_ref[...] = lax.rsqrt(jnp.mean(wide * wide, axis=-1, keepdims=True) + EPS)

    return call(
        kernel,
        like((rows, 1), F32),
        grid=(rows // tile,),
        in_specs=[pl.BlockSpec((tile, width), lambda i: (i, 0)), ANY],
        out_specs=pl.BlockSpec((tile, 1), lambda i: (i, 0)),
    )(activations, after)


def pair_sum(mine, got, owners, after):
    shape = (2, 4, 4, 2, 32, 1024)

    def kernel(a_ref, b_ref, after_ref, out_ref):
        total = a_ref[...].astype(F32) + b_ref[...].astype(F32)
        out_ref[...] = total.astype(BF16).reshape(out_ref.shape)

    def place(i):
        return owners[0]() * (1 - i) + owners[1]() * i

    block = pl.BlockSpec((2, 4, 1, 1, 32, 1024), lambda i: (0, 0, place(i), core_of(), 0, 0))
    return call(
        kernel,
        like((2, 2, 4, 32, 1024), BF16),
        grid=(2,),
        in_specs=[block, block, ANY],
        out_specs=pl.BlockSpec((1, 2, 4, 32, 1024), lambda i: (i, 0, 0, 0, 0)),
    )(mine.reshape(shape), got.reshape(shape), after)


def halves_sum(keep, got, after, flops=0):
    def kernel(a_ref, b_ref, after_ref, own_ref, send_ref):
        own_ref[...] = a_ref[0].astype(F32) + b_ref[0].astype(F32)
        send_ref[...] = (a_ref[1].astype(F32) + b_ref[1].astype(F32)).astype(BF16)

    block = keep.shape[1:]
    return call(
        kernel,
        [like(block, F32), like(block, BF16)],
        flops,
        in_specs=[VMEM] * 2 + [ANY],
        out_specs=[VMEM] * 2,
    )(keep, got, after)


def line_sum(own, got, after):
    def kernel(a_ref, b_ref, after_ref, send_ref, keep_ref):
        z_hi, core = z_hi_of(), core_of()
        owners = (first(z_hi, core), (z_hi + 2) % 4, z_hi, second(z_hi, core))
        for i, at in enumerate(owners):
            total = a_ref[:, at] + b_ref[:, at].astype(F32)
            (send_ref, keep_ref)[i // 2][i % 2] = total.astype(BF16)

    return call(
        kernel,
        [like((2, 2, 32, 1024), BF16)] * 2,
        in_specs=[VMEM] * 2 + [ANY],
        out_specs=[VMEM] * 2,
    )(own, got, after)


TILE = 256


def half_product(a, half, w, dtype, plus, after):
    rows, (depth, width) = a.shape[0], w.shape

    def kernel(a_ref, w_ref, *refs):
        total = jnp.dot(a_ref[...], w_ref[...], preferred_element_type=F32)
        for ref in refs[: len(plus)]:
            total = total + ref[...].astype(F32)
        refs[-1][...] = total.astype(dtype)

    column = lambda j: (0, j)
    return call(
        kernel,
        like((rows, width), dtype),
        grid=(width // TILE,),
        in_specs=[
            pl.BlockSpec((rows, depth), lambda j: (0, half)),
            pl.BlockSpec((depth, TILE), column),
        ]
        + [pl.BlockSpec((rows, TILE), column)] * len(plus)
        + [ANY],
        out_specs=pl.BlockSpec((rows, TILE), column),
    )(a, w, *plus, after)


def product(a, w, v, dtype, after):
    rows, depth, width = a.shape[0], w.shape[0], w.shape[1]

    def kernel(a_ref, w_ref, v_ref, after_ref, out_ref):
        for j in range(0, width, TILE):
            at = slice(j, j + TILE)
            total = jnp.dot(a_ref[:, :depth], w_ref[:, at], preferred_element_type=F32)
            total = total + jnp.dot(a_ref[:, depth:], v_ref[:, at], preferred_element_type=F32)
            out_ref[:, at] = total.astype(dtype)

    return call(
        kernel, like((rows, width), dtype), in_specs=[VMEM] * 3 + [ANY], out_specs=VMEM
    )(a, w, v, after)


def far_product(a, w, plus, after):
    rows, (depth, width) = a.shape[0], w.shape

    def kernel(a_ref, w_ref, plus_ref, after_ref, out_ref):
        for j in range(0, width, TILE):
            at = slice(j, j + TILE)
            total = jnp.dot(a_ref[:, depth:], w_ref[:, at], preferred_element_type=F32)
            out_ref[:, at] = (total + plus_ref[:, at]).astype(BF16)

    return call(
        kernel, like((rows, width), BF16), in_specs=[VMEM] * 3 + [ANY], out_specs=VMEM
    )(a, w, plus, after)


def plus(own, got, dtype, after, flops=0):
    def kernel(own_ref, got_ref, after_ref, out_ref):
        out_ref[...] = (own_ref[...] + got_ref[...].astype(F32)).astype(dtype)

    return call(
        kernel, like(own.shape, dtype), flops, in_specs=[VMEM] * 2 + [ANY], out_specs=VMEM
    )(own, got, after)


def last_sum(own, got, scale):
    def kernel(own_ref, got_ref, scale_ref, out_ref):
        out_ref[...] = ((own_ref[...] + got_ref[...].astype(F32)) * scale_ref[...]).astype(BF16)

    return call(kernel, like(own.shape, BF16), in_specs=[VMEM] * 3, out_specs=VMEM)(
        own, got, scale
    )


def shards(local_fragment, anchor, momentum, next_weights, activations, norm_gain):
    replicas = lax.axis_size("rep")
    mine, fragment = next_weights[0], local_fragment[0]
    x_first = lambda v: move(v, lambda z, y, c, x, l: (z, y, c, first(x, c), l))
    x_second = lambda v: move(v, lambda z, y, c, x, l: (z, y, c, second(x, c), l))
    x_far = lambda v: move(v, lambda z, y, c, x, l: (z, y, c, (x + 2) % 4, l))
    y_first = lambda v: move(v, lambda z, y, c, x, l: (z, first(y, c), c, x, l))
    y_second = lambda v: move(v, lambda z, y, c, x, l: (z, second(y, c), c, x, l))
    z_first = lambda v: move(v, lambda z, y, c, x, l: (first(z, c), y, c, x, l))
    z_second = lambda v: move(v, lambda z, y, c, x, l: (second(z, c), y, c, x, l))

    other = move(mine, lambda z, y, c, x, l: (z, y, c, x, 1 - l))
    sibling = move(fragment, lambda z, y, c, x, l: (z, y, 1 - c, x, l))

    (a_far,) = gained(activations, norm_gain, [lambda: (x_of() + 2) % 4], norm_gain)
    far_a = x_far(a_far)
    a_first, a_second = gained(
        activations,
        norm_gain,
        [lambda: first(x_of(), core_of()), lambda: second(x_of(), core_of())],
        a_far,
    )
    first_a, second_a = x_first(a_first), x_second(a_second)
    scale = row_scale(activations, a_first)
    (own_a,) = gained(activations, norm_gain, [x_of], scale)

    send = pair_sum(
        fragment, sibling, [lambda: first(y_of(), core_of()), lambda: (y_of() + 2) % 4], own_a
    )
    got = y_first(send)
    keep = pair_sum(fragment, sibling, [y_of, lambda: second(y_of(), core_of())], send)
    own = half_product(own_a, 0, mine, F32, [], keep)
    far = half_product(far_a, 0, mine, F32, [], own)
    line, send = halves_sum(keep, got, far)
    got = y_second(send)

    far = far_product(far_a, other, far, send)
    via = x_first(far)
    send, keep = line_sum(line, got, far)
    got = z_first(send)
    near = product(first_a, mine, other, BF16, send)
    from_first = x_first(near)
    part = product(second_a, mine, other, F32, near)
    own = half_product(own_a, 1, other, F32, [own], part)
    from_second = x_second(plus(part, via, BF16, own))
    total, send = halves_sum(keep, got, part, SLOW)
    got = z_second(send)
    own = plus(own, from_first, F32, send, SLOW)

    total = total + got.astype(F32)
    pseudo = anchor - total / replicas
    new_momentum = 0.9 * momentum + pseudo
    new_anchor = anchor - 0.7 * (pseudo + 0.9 * new_momentum)
    result = last_sum(own, from_second, scale)
    return (new_anchor, new_momentum, result)


def solution(mesh):
    placed = (
        P("rep", None, "fsdp", None),
        P(None, ("fsdp", "rep"), None),
        P(None, ("fsdp", "rep"), None),
        P("rep", "fsdp", None),
        P(("rep", "fsdp"), None),
        P(),
    )
    return jax.shard_map(
        shards,
        mesh=mesh,
        in_specs=placed,
        out_specs=(
            P(None, ("fsdp", "rep"), None),
            P(None, ("fsdp", "rep"), None),
            P(("rep", "fsdp"), None),
        ),
        check_vma=False,
    )
```

time: 84.9 us -> 75.6 us (0.89)
  the two profiles are of different devices: /device:TPU:1 before, /device:TPU:8 now
where the time goes in v3:
time: 75.6 us; the launch traced here: 75.5 us
  waiting for transfers between devices  34 us (45%)
  starting transfers between devices  22.6 us (30%)
  Pallas kernels  16.8 us (22%)
  other arithmetic  0.88 us (1%)
  between operations  0.83 us (1%)
    ppermute x12, waiting for transfers between devices, move(): return lax.ppermute(value, ('rep', 'fsdp'), pairs)  34 us
    ppermute x12, starting transfers between devices, move(): return lax.ppermute(value, ('rep', 'fsdp'), pairs)  22.6 us
    pallas_call x3, Pallas kernels, half_product(): call(kernel, like((rows, width), dtype), grid=(width // TILE,), in_specs=...  5.01 us
    pallas_call x3, Pallas kernels, gained(): call(kernel, [like((rows, 2 * step), BF16)] * (n // 2), in_specs=[HBM, HB...  4.47 us
    pallas_call x2, Pallas kernels, product(): call(kernel, like((rows, width), dtype), in_specs=[VMEM] * 3 + [ANY], out...  2.48 us
  transfers between devices with their start and end apart: 12, of which 4 were waited for; matrix products, arithmetic and copies ran while one was open for 1% of the time, Pallas kernels for 21%

profile of v3, /device:TPU:8, one launch (start us, length us, event | category | flops | bytes accessed | tf_op | source)
XLA Modules:
  0.0 75.5 jit_solution(4495727399852783348)
XLA Ops:
  0.6 0.1 collective-permute-start
  0.7 2.0 %collective-permute-start.4 = (bf16[1024,1024]{1,0:T(8,128)(2,1)}, bf16[1024,1024]{1,0:T(8,128)(2,1)S(1)}, u32[]{:S(2)}, u32[]{:S(2)}) collective-permute-start(bf16[1024,1024]{1,0:T(8,128)(2,1)} %bitcast.4), channel_id=1, source_target_pairs={{0,1},{1,0},{2,3},{3,2},{4,5},{5,4},{6,7},{7,6},{8,9},{9,8},{10,11... | collective-permute-start | bytes 6291464 | tf_op jit(solution)/shard_map/ppermute | solution.py:33
  2.7 1.4 %shard_map.85.after_ref = bf16[256,2048]{1,0:T(8,128)(2,1)S(1)} custom-call(bf16[256,8192]{1,0:T(8,128)(2,1)} %a_ref.7, f32[8192]{0:T(1024)} %g_ref.5, f32[8192]{0:T(1024)} %g_ref.5), custom_call_target="tpu_custom_call" | custom-call | tf_op jit(solution)/shard_map/pallas_call | solution.py:99
  4.1 3.1 %collective-permute-start.2 = (bf16[256,2048]{1,0:T(8,128)(2,1)S(1)}, bf16[256,2048]{1,0:T(8,128)(2,1)S(1)}, u32[]{:S(2)}, u32[]{:S(2)}) collective-permute-start(bf16[256,2048]{1,0:T(8,128)(2,1)S(1)} %shard_map.85.after_ref), channel_id=1, source_target_pairs={{0,4},{1,5},{2,6},{3,7},{4,0},{5,1},{6,2},{7,3},{8,12},{9,13},{10,... | collective-permute-start | bytes 3145736 | tf_op jit(solution)/shard_map/ppermute | solution.py:33
  7.2 1.7 %shard_map.86 = (bf16[256,2048]{1,0:T(8,128)(2,1)S(1)}, bf16[256,2048]{1,0:T(8,128)(2,1)S(1)}) custom-call(bf16[256,8192]{1,0:T(8,128)(2,1)} %a_ref.7, f32[8192]{0:T(1024)} %g_ref.5, bf16[256,2048]{1,0:T(8,128)(2,1)S(1)} %shard_map.85.after_ref), custom_call_target="tpu_custom_call" | custom-call | tf_op jit(solution)/shard_map/pallas_call | solution.py:99
  9.0 1.3 %shard_map.87.after_ref.scale_ref = f32[256,1]{1,0:T(8,128)S(1)} custom-call(bf16[256,8192]{1,0:T(8,128)(2,1)S(1)} %copy-done, bf16[256,2048]{1,0:T(8,128)(2,1)S(1)} %get-tuple-element.11.after_ref), custom_call_target="tpu_custom_call" | custom-call | tf_op jit(solution)/shard_map/pallas_call | solution.py:117
  10.3 1.4 %shard_map.88.after_ref.a_ref = bf16[256,2048]{1,0:T(8,128)(2,1)S(1)} custom-call(bf16[256,8192]{1,0:T(8,128)(2,1)} %a_ref.7, f32[8192]{0:T(1024)} %g_ref.5, f32[256,1]{1,0:T(8,128)S(1)} %shard_map.87.after_ref.scale_ref), custom_call_target="tpu_custom_call" | custom-call | tf_op jit(solution)/shard_map/pallas_call | solution.py:99
  11.7 0.7 shard_map.89.after_ref
  12.4 0.5 collective-permute-start.1
  12.9 0.6 collective-permute-start.7
  13.5 0.6 collective-permute-start.6
  14.1 0.6 shard_map.90.refs_0_.a_ref
  14.8 0.3 copy-done.1
  15.1 1.6 %shard_map.91.refs_0_ = f32[256,1024]{1,0:T(8,128)S(1)} custom-call(bf16[256,2048]{1,0:T(8,128)(2,1)S(1)} %shard_map.88.after_ref.a_ref, bf16[1024,1024]{1,0:T(8,128)(2,1)S(1)} %bitcast.5, bf16[2,2,4,32,1024]{4,3,2,1,0:T(8,128)(2,1)S(1)} %shard_map.90.refs_0_.a_ref), custom_call_target="tpu_custom_call" | custom-call | tf_op jit(solution)/shard_map/pallas_call | solution.py:190
  16.7 15.0 %collective-permute-done.2.a_ref = bf16[256,2048]{1,0:T(8,128)(2,1)S(1)} collective-permute-done((bf16[256,2048]{1,0:T(8,128)(2,1)S(1)}, bf16[256,2048]{1,0:T(8,128)(2,1)S(1)}, u32[]{:S(2)}, u32[]{:S(2)}) %collective-permute-start.2) | collective-permute-done | bytes 1048608 | tf_op jit(solution)/shard_map/ppermute | solution.py:33
  31.7 1.6 %shard_map.92.after_ref.plus_ref = f32[256,1024]{1,0:T(8,128)S(1)} custom-call(bf16[256,2048]{1,0:T(8,128)(2,1)S(1)} %collective-permute-done.2.a_ref, bf16[1024,1024]{1,0:T(8,128)(2,1)S(1)} %bitcast.6, f32[256,1024]{1,0:T(8,128)S(1)} %shard_map.91.refs_0_), custom_call_target="tpu_custom_call" | custom-call | tf_op jit(solution)/shard_map/pallas_call | solution.py:190
  33.4 0.2 shard_map.93
  33.6 1.7 %collective-permute-start.3 = (bf16[2,4,32,1024]{3,2,1,0:T(8,128)(2,1)S(1)}, bf16[2,4,32,1024]{3,2,1,0:T(8,128)(2,1)S(1)}, u32[]{:S(2)}, u32[]{:S(2)}) collective-permute-start(bf16[2,4,32,1024]{3,2,1,0:T(8,128)(2,1)S(1)} %get-tuple-element.13.after_ref), channel_id=1, source_target_pairs={{0,48},{1,49},{2,50},{3,51},{4,52},{5,53},{6,54},{7,55},{8,24},{9,... | collective-permute-start | bytes 1572872 | tf_op jit(solution)/shard_map/ppermute | solution.py:33
  35.3 13.9 %collective-permute-done.4.w_ref.v_ref = bf16[1024,1024]{1,0:T(8,128)(2,1)S(1)} collective-permute-done((bf16[1024,1024]{1,0:T(8,128)(2,1)}, bf16[1024,1024]{1,0:T(8,128)(2,1)S(1)}, u32[]{:S(2)}, u32[]{:S(2)}) %collective-permute-start.4) | collective-permute-done | bytes 2097184 | tf_op jit(solution)/shard_map/ppermute | solution.py:33
  49.1 0.7 shard_map.94.after_ref
  49.9 1.6 %collective-permute-start.10 = (bf16[256,1024]{1,0:T(8,128)(2,1)S(1)}, bf16[256,1024]{1,0:T(8,128)(2,1)S(1)}, u32[]{:S(2)}, u32[]{:S(2)}) collective-permute-start(bf16[256,1024]{1,0:T(8,128)(2,1)S(1)} %shard_map.94.after_ref), channel_id=1, source_target_pairs={{0,2},{1,3},{2,0},{3,1},{4,6},{5,7},{6,4},{7,5},{8,14},{9,15},{10,... | collective-permute-start | bytes 1572872 | tf_op jit(solution)/shard_map/ppermute | solution.py:33
  51.5 3.4 %collective-permute-start.5 = (bf16[2,2,32,1024]{3,2,1,0:T(8,128)(2,1)S(1)}, bf16[2,2,32,1024]{3,2,1,0:T(8,128)(2,1)S(1)}, u32[]{:S(2)}, u32[]{:S(2)}) collective-permute-start(bf16[2,2,32,1024]{3,2,1,0:T(8,128)(2,1)S(1)} %get-tuple-element.15.after_ref), channel_id=1, source_target_pairs={{0,64},{1,65},{2,66},{3,67},{4,68},{5,69},{6,70},{7,71},{8,200},{9... | collective-permute-start | bytes 786440 | tf_op jit(solution)/shard_map/ppermute | solution.py:33
  54.9 1.2 %shard_map.96.after_ref = bf16[256,1024]{1,0:T(8,128)(2,1)S(1)} custom-call(bf16[256,2048]{1,0:T(8,128)(2,1)S(1)} %collective-permute-done.7.a_ref, bf16[1024,1024]{1,0:T(8,128)(2,1)S(1)} %bitcast.7, bf16[1024,1024]{1,0:T(8,128)(2,1)S(1)} %collective-permute-done.4.w_ref.v_ref, bf16[2,2,32,1024]{3,2,1,0:T(8,128)(2,1)S(1)} %get-tuple-element.15.after_ref), custom_call_target="tpu_custom_call" | custom-call | tf_op jit(solution)/shard_map/pallas_call | solution.py:214
  56.1 0.6 collective-permute-start.9
  56.8 1.2 %shard_map.97.after_ref.refs_1_.own_ref = f32[256,1024]{1,0:T(8,128)S(1)} custom-call(bf16[256,2048]{1,0:T(8,128)(2,1)S(1)} %collective-permute-done.6.a_ref, bf16[1024,1024]{1,0:T(8,128)(2,1)S(1)} %bitcast.8, bf16[1024,1024]{1,0:T(8,128)(2,1)S(1)} %collective-permute-done.4.w_ref.v_ref, bf16[256,1024]{1,0:T(8,128)(2,1)S(1)} %shard_map.96.after_ref), custom_call_target="tpu_custom_call" | custom-call | tf_op jit(solution)/shard_map/pallas_call | solution.py:214
  58.0 1.7 %shard_map.99.own_ref.after_ref = f32[256,1024]{1,0:T(8,128)S(1)} custom-call(bf16[256,2048]{1,0:T(8,128)(2,1)S(1)} %shard_map.88.after_ref.a_ref, bf16[1024,1024]{1,0:T(8,128)(2,1)S(1)} %collective-permute-done.4.w_ref.v_ref, f32[256,1024]{1,0:T(8,128)S(1)} %shard_map.91.refs_0_, f32[256,1024]{1,0:T(8,128)S(1)} %shard_map.97.after_ref.refs_1_.own_ref), custom_call_target="tpu_custom_call" | custom-call | tf_op jit(solution)/shard_map/pallas_call | solution.py:190
  59.9 2.8 %collective-permute-start.11 = (bf16[256,1024]{1,0:T(8,128)(2,1)S(1)}, bf16[256,1024]{1,0:T(8,128)(2,1)S(1)}, u32[]{:S(2)}, u32[]{:S(2)}) collective-permute-start(bf16[256,1024]{1,0:T(8,128)(2,1)S(1)} %shard_map.101), channel_id=1, source_target_pairs={{0,6},{1,7},{2,4},{3,5},{4,2},{5,3},{6,0},{7,1},{8,10},{9,11},{10,... | collective-permute-start | bytes 1572872 | tf_op jit(solution)/shard_map/ppermute | solution.py:33
  62.8 5.6 %collective-permute-start.8 = (bf16[2,32,1024]{2,1,0:T(8,128)(2,1)S(1)}, bf16[2,32,1024]{2,1,0:T(8,128)(2,1)S(1)}, u32[]{:S(2)}, u32[]{:S(2)}) collective-permute-start(bf16[2,32,1024]{2,1,0:T(8,128)(2,1)S(1)} %get-tuple-element.18.after_ref), channel_id=1, source_target_pairs={{0,192},{1,193},{2,194},{3,195},{4,196},{5,197},{6,198},{7,199},{8... | collective-permute-start | bytes 393224 | tf_op jit(solution)/shard_map/ppermute | solution.py:33
  68.4 4.3 %collective-permute-done.8 = bf16[2,32,1024]{2,1,0:T(8,128)(2,1)S(1)} collective-permute-done((bf16[2,32,1024]{2,1,0:T(8,128)(2,1)S(1)}, bf16[2,32,1024]{2,1,0:T(8,128)(2,1)S(1)}, u32[]{:S(2)}, u32[]{:S(2)}) %collective-permute-start.8) | collective-permute-done | bytes 131104 | tf_op jit(solution)/shard_map/ppermute | solution.py:33
  72.7 0.9 %multiply_subtract_fusion = (f32[2,32,1024]{2,1,0:T(8,128)}, f32[2,32,1024]{2,1,0:T(8,128)}) fusion(f32[2,32,1024]{2,1,0:T(8,128)S(1)} %copy-done.3, f32[2,32,1024]{2,1,0:T(8,128)S(1)} %get-tuple-element.17, bf16[2,32,1024]{2,1,0:T(8,128)(2,1)S(1)} %collective-permute-done.8, f32[2,32,1024]{2,1,0:T(8,128)S(1)} %copy-done.4), kind=kLoop, calls=%fused_computation | loop fusion | flops 655360 | bytes 1441792 | tf_op jit(solution)/shard_map/sub | solution.py:303
  73.7 0.8 %collective-permute-done.11.got_ref = bf16[256,1024]{1,0:T(8,128)(2,1)S(1)} collective-permute-done((bf16[256,1024]{1,0:T(8,128)(2,1)S(1)}, bf16[256,1024]{1,0:T(8,128)(2,1)S(1)}, u32[]{:S(2)}, u32[]{:S(2)}) %collective-permute-start.11) | collective-permute-done | bytes 524320 | tf_op jit(solution)/shard_map/ppermute | solution.py:33
  74.5 0.9 %shard_map.102 = bf16[256,1024]{1,0:T(8,128)(2,1)} custom-call(f32[256,1024]{1,0:T(8,128)S(1)} %shard_map.100.own_ref, bf16[256,1024]{1,0:T(8,128)(2,1)S(1)} %collective-permute-done.11.got_ref, f32[256,1]{1,0:T(8,128)S(1)} %shard_map.87.after_ref.scale_ref), custom_call_target="tpu_custom_call" | custom-call | tf_op jit(solution)/shard_map/pallas_call | solution.py:246
  (21 shorter events, 0.4 us)
Async XLA Ops:
  0.6 11.0 %collective-permute-start = (bf16[2,1024,1024]{2,1,0:T(8,128)(2,1)}, bf16[2,1024,1024]{2,1,0:T(8,128)(2,1)S(1)}, u32[]{:S(2)}, u32[]{:S(2)}) collective-permute-start(bf16[2,1024,1024]{2,1,0:T(8,128)(2,1)} %bitcast.9), channel_id=1, source_target_pairs={{0,8},{1,9},{2,10},{3,11},{4,12},{5,13},{6,14},{7,15},{8,0},{9,1},... | collective-permute-start | bytes 12582920 | tf_op jit(solution)/shard_map/ppermute | solution.py:33
  0.7 8.2 %copy-start = (bf16[256,8192]{1,0:T(8,128)(2,1)S(1)}, bf16[256,8192]{1,0:T(8,128)(2,1)}, u32[]{:S(2)}) copy-start(bf16[256,8192]{1,0:T(8,128)(2,1)} %a_ref.7) | copy-start | bytes 12582916
  0.7 48.4 %collective-permute-start.4 = (bf16[1024,1024]{1,0:T(8,128)(2,1)}, bf16[1024,1024]{1,0:T(8,128)(2,1)S(1)}, u32[]{:S(2)}, u32[]{:S(2)}) collective-permute-start(bf16[1024,1024]{1,0:T(8,128)(2,1)} %bitcast.4), channel_id=1, source_target_pairs={{0,1},{1,0},{2,3},{3,2},{4,5},{5,4},{6,7},{7,6},{8,9},{9,8},{10,11... | collective-permute-start | bytes 6291464 | tf_op jit(solution)/shard_map/ppermute | solution.py:33
  4.1 27.6 %collective-permute-start.2 = (bf16[256,2048]{1,0:T(8,128)(2,1)S(1)}, bf16[256,2048]{1,0:T(8,128)(2,1)S(1)}, u32[]{:S(2)}, u32[]{:S(2)}) collective-permute-start(bf16[256,2048]{1,0:T(8,128)(2,1)S(1)} %shard_map.85.after_ref), channel_id=1, source_target_pairs={{0,4},{1,5},{2,6},{3,7},{4,0},{5,1},{6,2},{7,3},{8,12},{9,13},{10,... | collective-permute-start | bytes 3145736 | tf_op jit(solution)/shard_map/ppermute | solution.py:33
  9.0 2.7 %copy-start.2 = (bf16[1,2,1024,1024]{3,2,1,0:T(8,128)(2,1)S(1)}, bf16[1,2,1024,1024]{3,2,1,0:T(8,128)(2,1)}, u32[]{:S(2)}) copy-start(bf16[1,2,1024,1024]{3,2,1,0:T(8,128)(2,1)} %param.6) | copy-start | bytes 12582916
  12.4 21.0 %collective-permute-start.1 = (bf16[2,2,4,32,1024]{4,3,2,1,0:T(8,128)(2,1)S(1)}, bf16[2,2,4,32,1024]{4,3,2,1,0:T(8,128)(2,1)S(1)}, u32[]{:S(2)}, u32[]{:S(2)}) collective-permute-start(bf16[2,2,4,32,1024]{4,3,2,1,0:T(8,128)(2,1)S(1)} %shard_map.89.after_ref), channel_id=1, source_target_pairs={{0,16},{1,17},{2,18},{3,19},{4,20},{5,21},{6,22},{7,23},{8,56},{9,... | collective-permute-start | bytes 3145736 | tf_op jit(solution)/shard_map/ppermute | solution.py:33
  12.9 42.0 %collective-permute-start.7 = (bf16[256,2048]{1,0:T(8,128)(2,1)S(1)}, bf16[256,2048]{1,0:T(8,128)(2,1)S(1)}, u32[]{:S(2)}, u32[]{:S(2)}) collective-permute-start(bf16[256,2048]{1,0:T(8,128)(2,1)S(1)} %get-tuple-element.11.after_ref), channel_id=1, source_target_pairs={{0,2},{1,3},{2,0},{3,1},{4,6},{5,7},{6,4},{7,5},{8,14},{9,15},{10,... | collective-permute-start | bytes 3145736 | tf_op jit(solution)/shard_map/ppermute | solution.py:33
  13.5 1.6 %copy-start.1 = (bf16[1,1024,1024]{2,1,0:T(8,128)(2,1)S(1)}, bf16[1,1024,1024]{2,1,0:T(8,128)(2,1)}, u32[]{:S(2)}) copy-start(bf16[1,1024,1024]{2,1,0:T(8,128)(2,1)} %param.9) | copy-start | bytes 6291460
  13.5 43.3 %collective-permute-start.6 = (bf16[256,2048]{1,0:T(8,128)(2,1)S(1)}, bf16[256,2048]{1,0:T(8,128)(2,1)S(1)}, u32[]{:S(2)}, u32[]{:S(2)}) collective-permute-start(bf16[256,2048]{1,0:T(8,128)(2,1)S(1)} %get-tuple-element.16), channel_id=1, source_target_pairs={{0,6},{1,7},{2,4},{3,5},{4,2},{5,3},{6,0},{7,1},{8,10},{9,11},{10,... | collective-permute-start | bytes 3145736 | tf_op jit(solution)/shard_map/ppermute | solution.py:33
  33.6 17.8 %collective-permute-start.3 = (bf16[2,4,32,1024]{3,2,1,0:T(8,128)(2,1)S(1)}, bf16[2,4,32,1024]{3,2,1,0:T(8,128)(2,1)S(1)}, u32[]{:S(2)}, u32[]{:S(2)}) collective-permute-start(bf16[2,4,32,1024]{3,2,1,0:T(8,128)(2,1)S(1)} %get-tuple-element.13.after_ref), channel_id=1, source_target_pairs={{0,48},{1,49},{2,50},{3,51},{4,52},{5,53},{6,54},{7,55},{8,24},{9,... | collective-permute-start | bytes 1572872 | tf_op jit(solution)/shard_map/ppermute | solution.py:33
  49.9 9.9 %collective-permute-start.10 = (bf16[256,1024]{1,0:T(8,128)(2,1)S(1)}, bf16[256,1024]{1,0:T(8,128)(2,1)S(1)}, u32[]{:S(2)}, u32[]{:S(2)}) collective-permute-start(bf16[256,1024]{1,0:T(8,128)(2,1)S(1)} %shard_map.94.after_ref), channel_id=1, source_target_pairs={{0,2},{1,3},{2,0},{3,1},{4,6},{5,7},{6,4},{7,5},{8,14},{9,15},{10,... | collective-permute-start | bytes 1572872 | tf_op jit(solution)/shard_map/ppermute | solution.py:33
  51.5 11.2 %collective-permute-start.5 = (bf16[2,2,32,1024]{3,2,1,0:T(8,128)(2,1)S(1)}, bf16[2,2,32,1024]{3,2,1,0:T(8,128)(2,1)S(1)}, u32[]{:S(2)}, u32[]{:S(2)}) collective-permute-start(bf16[2,2,32,1024]{3,2,1,0:T(8,128)(2,1)S(1)} %get-tuple-element.15.after_ref), channel_id=1, source_target_pairs={{0,64},{1,65},{2,66},{3,67},{4,68},{5,69},{6,70},{7,71},{8,200},{9... | collective-permute-start | bytes 786440 | tf_op jit(solution)/shard_map/ppermute | solution.py:33
  56.1 17.4 %collective-permute-start.9 = (bf16[256,1024]{1,0:T(8,128)(2,1)S(1)}, bf16[256,1024]{1,0:T(8,128)(2,1)S(1)}, u32[]{:S(2)}, u32[]{:S(2)}) collective-permute-start(bf16[256,1024]{1,0:T(8,128)(2,1)S(1)} %shard_map.96.after_ref), channel_id=1, source_target_pairs={{0,2},{1,3},{2,0},{3,1},{4,6},{5,7},{6,4},{7,5},{8,14},{9,15},{10,... | collective-permute-start | bytes 1572872 | tf_op jit(solution)/shard_map/ppermute | solution.py:33
  58.0 14.7 %copy-start.3 = (f32[2,32,1024]{2,1,0:T(8,128)S(1)}, f32[2,32,1024]{2,1,0:T(8,128)}, u32[]{:S(2)}) copy-start(f32[2,32,1024]{2,1,0:T(8,128)} %param.7) | copy-start | bytes 786436
  58.0 14.7 %copy-start.4 = (f32[2,32,1024]{2,1,0:T(8,128)S(1)}, f32[2,32,1024]{2,1,0:T(8,128)}, u32[]{:S(2)}) copy-start(f32[2,32,1024]{2,1,0:T(8,128)} %param.8) | copy-start | bytes 786436
  59.9 14.6 %collective-permute-start.11 = (bf16[256,1024]{1,0:T(8,128)(2,1)S(1)}, bf16[256,1024]{1,0:T(8,128)(2,1)S(1)}, u32[]{:S(2)}, u32[]{:S(2)}) collective-permute-start(bf16[256,1024]{1,0:T(8,128)(2,1)S(1)} %shard_map.101), channel_id=1, source_target_pairs={{0,6},{1,7},{2,4},{3,5},{4,2},{5,3},{6,0},{7,1},{8,10},{9,11},{10,... | collective-permute-start | bytes 1572872 | tf_op jit(solution)/shard_map/ppermute | solution.py:33
  62.8 9.9 %collective-permute-start.8 = (bf16[2,32,1024]{2,1,0:T(8,128)(2,1)S(1)}, bf16[2,32,1024]{2,1,0:T(8,128)(2,1)S(1)}, u32[]{:S(2)}, u32[]{:S(2)}) collective-permute-start(bf16[2,32,1024]{2,1,0:T(8,128)(2,1)S(1)} %get-tuple-element.18.after_ref), channel_id=1, source_target_pairs={{0,192},{1,193},{2,194},{3,195},{4,196},{5,197},{6,198},{7,199},{8... | collective-permute-start | bytes 393224 | tf_op jit(solution)/shard_map/ppermute | solution.py:33

commit v4 on v3

--- a/solution.py
+++ b/solution.py
@@ -76,32 +76,41 @@
 def gained(activations, norm_gain, owners, after):
     rows, step, n = activations.shape[0], 1024, 2 * len(owners)
 
+    cuts = 4
+    tile = rows // cuts
+
     def kernel(a_ref, g_ref, after_ref, *refs):
-        outs, (a_buf, sems), g_bufs = refs[: n // 2], refs[n // 2 : n // 2 + 2], refs[n // 2 + 2 :]
-        copies = []
+        outs, (a_buf, a_sems, g_sems) = refs[: n // 2], refs[n // 2 : n // 2 + 3]
+        g_bufs = refs[n // 2 + 3 :]
+        a_copies, g_copies = [], []
         for k in range(n):
             place = owners[k // 2]() * 2 + (z_lo_of() + k % 2) % 2
             at = pl.ds(pl.multiple_of(place * step, step), step)
-            copies.append(
-                (
-                    pltpu.make_async_copy(g_ref.at[at], g_bufs[k], sems.at[2 * k]),
-                    pltpu.make_async_copy(a_ref.at[:, at], a_buf.at[k], sems.at[2 * k + 1]),
+            g_copies.append(pltpu.make_async_copy(g_ref.at[at], g_bufs[k], g_sems.at[k]))
+            g_copies[-1].start()
+            for i in range(cuts):
+                part = slice(i * tile, (i + 1) * tile)
+                a_copies.append(
+                    pltpu.make_async_copy(
+                        a_ref.at[part, at], a_buf.at[k, part], a_sems.at[k * cuts + i]
+                    )
                 )
-            )
-            for copy in copies[-1]:
-                copy.start()
+                a_copies[-1].start()
         for k in range(n):
-            for copy in copies[k]:
-                copy.wait()
-            value = a_buf[k].astype(F32) * g_bufs[k][...].reshape(1, step)
-            outs[k // 2][:, k % 2 * step : (k % 2 + 1) * step] = value.astype(BF16)
+            g_copies[k].wait()
+            gain = g_bufs[k][...].reshape(1, step)
+            for i in range(cuts):
+                part = slice(i * tile, (i + 1) * tile)
+                a_copies[k * cuts + i].wait()
+                value = a_buf[k, part].astype(F32) * gain
+                outs[k // 2][part, k % 2 * step : (k % 2 + 1) * step] = value.astype(BF16)
 
     return call(
         kernel,
         [like((rows, 2 * step), BF16)] * (n // 2),
         in_specs=[HBM, HBM, ANY],
         out_specs=[VMEM] * (n // 2),
-        scratch_shapes=[pltpu.VMEM((n, rows, step), BF16), DMA((2 * n,))]
+        scratch_shapes=[pltpu.VMEM((n, rows, step), BF16), DMA((cuts * n,)), DMA((n,))]
         + [pltpu.VMEM((step,), F32)] * n,
     )(in_hbm(activations), in_hbm(norm_gain), after)
 
@@ -240,12 +249,28 @@
 
 
 def last_sum(own, got, scale):
-    def kernel(own_ref, got_ref, scale_ref, out_ref):
-        out_ref[...] = ((own_ref[...] + got_ref[...].astype(F32)) * scale_ref[...]).astype(BF16)
-
-    return call(kernel, like(own.shape, BF16), in_specs=[VMEM] * 3, out_specs=VMEM)(
-        own, got, scale
-    )
+    rows, width = own.shape
+    cuts = 4
+    tile = rows // cuts
+
+    def kernel(own_ref, got_ref, scale_ref, out_ref, buf, sems):
+        copies = []
+        for i in range(cuts):
+            part = slice(i * tile, (i + 1) * tile)
+            total = own_ref[part] + got_ref[part].astype(F32)
+            buf[part] = (total * scale_ref[part]).astype(BF16)
+            copies.append(pltpu.make_async_copy(buf.at[part], out_ref.at[part], sems.at[i]))
+            copies[-1].start()
+        for copy in copies:
+            copy.wait()
+
+    return call(
+        kernel,
+        like(own.shape, BF16),
+        in_specs=[VMEM] * 3,
+        out_specs=ANY,
+        scratch_shapes=[pltpu.VMEM((rows, width), BF16), DMA((cuts,))],
+    )(own, got, scale)
 
 
 def shards(local_fragment, anchor, momentum, next_weights, activations, norm_gain):
@@ -291,11 +316,11 @@
     near = product(first_a, mine, other, BF16, send)
     from_first = x_first(near)
     part = product(second_a, mine, other, F32, near)
-    own = half_product(own_a, 1, other, F32, [own], part)
-    from_second = x_second(plus(part, via, BF16, own))
+    from_second = x_second(plus(part, via, BF16, part))
     total, send = halves_sum(keep, got, part, SLOW)
     got = z_second(send)
-    own = plus(own, from_first, F32, send, SLOW)
+    own = half_product(own_a, 1, other, F32, [own], send)
+    own = plus(own, from_first, F32, own, SLOW)
 
     total = total + got.astype(F32)
     pseudo = anchor - total / replicas

time: 75.6 us -> 75.6 us (level)
  waiting for transfers between devices: 34 us -> 33.2 us
    ppermute x12, waiting for transfers between devices: 34 us -> 33.2 us  [move(): return lax.ppermute(value, ('rep', 'fsdp'), pairs)]
  transfers between devices with their start and end apart: 12 -> 12, of which waited for: 4 -> 5; matrix products, arithmetic and copies ran while one was open for 1% -> 1% of each run, Pallas kernels for 21% -> 21%
where the time goes in v4:
time: 75.6 us; the launch traced here: 75.4 us
  waiting for transfers between devices  33.2 us (44%)
  starting transfers between devices  23.2 us (31%)
  Pallas kernels  16.9 us (22%)
  other arithmetic  0.88 us (1%)
  between operations  0.82 us (1%)
    ppermute x12, waiting for transfers between devices, move(): return lax.ppermute(value, ('rep', 'fsdp'), pairs)  33.2 us
    ppermute x12, starting transfers between devices, move(): return lax.ppermute(value, ('rep', 'fsdp'), pairs)  23.2 us
    pallas_call x3, Pallas kernels, half_product(): call(kernel, like((rows, width), dtype), grid=(width // TILE,), in_specs=...  4.99 us
    pallas_call x3, Pallas kernels, gained(): call(kernel, [like((rows, 2 * step), BF16)] * (n // 2), in_specs=[HBM, HB...  4.69 us
    pallas_call x2, Pallas kernels, product(): call(kernel, like((rows, width), dtype), in_specs=[VMEM] * 3 + [ANY], out...  2.48 us
  transfers between devices with their start and end apart: 12, of which 5 were waited for; matrix products, arithmetic and copies ran while one was open for 1% of the time, Pallas kernels for 21%

profile of v4, /device:TPU:8, one launch (start us, length us, event | category | flops | bytes accessed | tf_op | source)
XLA Modules:
  0.0 75.4 jit_solution(2630942021190621478)
XLA Ops:
  0.7 2.0 %collective-permute-start.4 = (bf16[1024,1024]{1,0:T(8,128)(2,1)}, bf16[1024,1024]{1,0:T(8,128)(2,1)S(1)}, u32[]{:S(2)}, u32[]{:S(2)}) collective-permute-start(bf16[1024,1024]{1,0:T(8,128)(2,1)} %bitcast.4), channel_id=1, source_target_pairs={{0,1},{1,0},{2,3},{3,2},{4,5},{5,4},{6,7},{7,6},{8,9},{9,8},{10,11... | collective-permute-start | bytes 6291464 | tf_op jit(solution)/shard_map/ppermute | solution.py:33
  2.7 1.4 %shard_map.85.after_ref = bf16[256,2048]{1,0:T(8,128)(2,1)S(1)} custom-call(bf16[256,8192]{1,0:T(8,128)(2,1)} %a_ref.7, f32[8192]{0:T(1024)} %g_ref.5, f32[8192]{0:T(1024)} %g_ref.5), custom_call_target="tpu_custom_call" | custom-call | tf_op jit(solution)/shard_map/pallas_call | solution.py:108
  4.2 3.1 %collective-permute-start.2 = (bf16[256,2048]{1,0:T(8,128)(2,1)S(1)}, bf16[256,2048]{1,0:T(8,128)(2,1)S(1)}, u32[]{:S(2)}, u32[]{:S(2)}) collective-permute-start(bf16[256,2048]{1,0:T(8,128)(2,1)S(1)} %shard_map.85.after_ref), channel_id=1, source_target_pairs={{0,4},{1,5},{2,6},{3,7},{4,0},{5,1},{6,2},{7,3},{8,12},{9,13},{10,... | collective-permute-start | bytes 3145736 | tf_op jit(solution)/shard_map/ppermute | solution.py:33
  7.3 1.8 %shard_map.86 = (bf16[256,2048]{1,0:T(8,128)(2,1)S(1)}, bf16[256,2048]{1,0:T(8,128)(2,1)S(1)}) custom-call(bf16[256,8192]{1,0:T(8,128)(2,1)} %a_ref.7, f32[8192]{0:T(1024)} %g_ref.5, bf16[256,2048]{1,0:T(8,128)(2,1)S(1)} %shard_map.85.after_ref), custom_call_target="tpu_custom_call" | custom-call | tf_op jit(solution)/shard_map/pallas_call | solution.py:108
  9.1 1.3 %shard_map.87.after_ref.scale_ref = f32[256,1]{1,0:T(8,128)S(1)} custom-call(bf16[256,8192]{1,0:T(8,128)(2,1)S(1)} %copy-done, bf16[256,2048]{1,0:T(8,128)(2,1)S(1)} %get-tuple-element.11.after_ref), custom_call_target="tpu_custom_call" | custom-call | tf_op jit(solution)/shard_map/pallas_call | solution.py:126
  10.4 1.4 %shard_map.88.after_ref.a_ref = bf16[256,2048]{1,0:T(8,128)(2,1)S(1)} custom-call(bf16[256,8192]{1,0:T(8,128)(2,1)} %a_ref.7, f32[8192]{0:T(1024)} %g_ref.5, f32[256,1]{1,0:T(8,128)S(1)} %shard_map.87.after_ref.scale_ref), custom_call_target="tpu_custom_call" | custom-call | tf_op jit(solution)/shard_map/pallas_call | solution.py:108
  11.9 0.7 shard_map.89.after_ref
  12.6 0.5 collective-permute-start.1
  13.1 0.6 collective-permute-start.7
  13.7 0.6 collective-permute-start.6
  14.3 0.6 shard_map.90.refs_0_.a_ref
  15.0 0.3 copy-done.1
  15.3 1.6 %shard_map.91.refs_0_ = f32[256,1024]{1,0:T(8,128)S(1)} custom-call(bf16[256,2048]{1,0:T(8,128)(2,1)S(1)} %shard_map.88.after_ref.a_ref, bf16[1024,1024]{1,0:T(8,128)(2,1)S(1)} %bitcast.5, bf16[2,2,4,32,1024]{4,3,2,1,0:T(8,128)(2,1)S(1)} %shard_map.90.refs_0_.a_ref), custom_call_target="tpu_custom_call" | custom-call | tf_op jit(solution)/shard_map/pallas_call | solution.py:199
  17.0 14.9 %collective-permute-done.2.a_ref = bf16[256,2048]{1,0:T(8,128)(2,1)S(1)} collective-permute-done((bf16[256,2048]{1,0:T(8,128)(2,1)S(1)}, bf16[256,2048]{1,0:T(8,128)(2,1)S(1)}, u32[]{:S(2)}, u32[]{:S(2)}) %collective-permute-start.2) | collective-permute-done | bytes 1048608 | tf_op jit(solution)/shard_map/ppermute | solution.py:33
  31.8 1.6 %shard_map.92.after_ref.plus_ref = f32[256,1024]{1,0:T(8,128)S(1)} custom-call(bf16[256,2048]{1,0:T(8,128)(2,1)S(1)} %collective-permute-done.2.a_ref, bf16[1024,1024]{1,0:T(8,128)(2,1)S(1)} %bitcast.6, f32[256,1024]{1,0:T(8,128)S(1)} %shard_map.91.refs_0_), custom_call_target="tpu_custom_call" | custom-call | tf_op jit(solution)/shard_map/pallas_call | solution.py:199
  33.5 0.2 shard_map.93
  33.7 1.7 %collective-permute-start.3 = (bf16[2,4,32,1024]{3,2,1,0:T(8,128)(2,1)S(1)}, bf16[2,4,32,1024]{3,2,1,0:T(8,128)(2,1)S(1)}, u32[]{:S(2)}, u32[]{:S(2)}) collective-permute-start(bf16[2,4,32,1024]{3,2,1,0:T(8,128)(2,1)S(1)} %get-tuple-element.13.after_ref), channel_id=1, source_target_pairs={{0,48},{1,49},{2,50},{3,51},{4,52},{5,53},{6,54},{7,55},{8,24},{9,... | collective-permute-start | bytes 1572872 | tf_op jit(solution)/shard_map/ppermute | solution.py:33
  35.4 13.8 %collective-permute-done.4.w_ref.v_ref = bf16[1024,1024]{1,0:T(8,128)(2,1)S(1)} collective-permute-done((bf16[1024,1024]{1,0:T(8,128)(2,1)}, bf16[1024,1024]{1,0:T(8,128)(2,1)S(1)}, u32[]{:S(2)}, u32[]{:S(2)}) %collective-permute-start.4) | collective-permute-done | bytes 2097184 | tf_op jit(solution)/shard_map/ppermute | solution.py:33
  49.1 0.7 shard_map.94.after_ref
  49.9 1.6 %collective-permute-start.10 = (bf16[256,1024]{1,0:T(8,128)(2,1)S(1)}, bf16[256,1024]{1,0:T(8,128)(2,1)S(1)}, u32[]{:S(2)}, u32[]{:S(2)}) collective-permute-start(bf16[256,1024]{1,0:T(8,128)(2,1)S(1)} %shard_map.94.after_ref), channel_id=1, source_target_pairs={{0,2},{1,3},{2,0},{3,1},{4,6},{5,7},{6,4},{7,5},{8,14},{9,15},{10,... | collective-permute-start | bytes 1572872 | tf_op jit(solution)/shard_map/ppermute | solution.py:33
  51.5 3.4 %collective-permute-start.5 = (bf16[2,2,32,1024]{3,2,1,0:T(8,128)(2,1)S(1)}, bf16[2,2,32,1024]{3,2,1,0:T(8,128)(2,1)S(1)}, u32[]{:S(2)}, u32[]{:S(2)}) collective-permute-start(bf16[2,2,32,1024]{3,2,1,0:T(8,128)(2,1)S(1)} %get-tuple-element.15.after_ref), channel_id=1, source_target_pairs={{0,64},{1,65},{2,66},{3,67},{4,68},{5,69},{6,70},{7,71},{8,200},{9... | collective-permute-start | bytes 786440 | tf_op jit(solution)/shard_map/ppermute | solution.py:33
  54.9 1.2 %shard_map.96.after_ref = bf16[256,1024]{1,0:T(8,128)(2,1)S(1)} custom-call(bf16[256,2048]{1,0:T(8,128)(2,1)S(1)} %collective-permute-done.7.a_ref, bf16[1024,1024]{1,0:T(8,128)(2,1)S(1)} %bitcast.7, bf16[1024,1024]{1,0:T(8,128)(2,1)S(1)} %collective-permute-done.4.w_ref.v_ref, bf16[2,2,32,1024]{3,2,1,0:T(8,128)(2,1)S(1)} %get-tuple-element.15.after_ref), custom_call_target="tpu_custom_call" | custom-call | tf_op jit(solution)/shard_map/pallas_call | solution.py:223
  56.1 0.6 collective-permute-start.9
  56.8 1.2 %shard_map.97.after_ref.own_ref = f32[256,1024]{1,0:T(8,128)S(1)} custom-call(bf16[256,2048]{1,0:T(8,128)(2,1)S(1)} %collective-permute-done.6.a_ref, bf16[1024,1024]{1,0:T(8,128)(2,1)S(1)} %bitcast.8, bf16[1024,1024]{1,0:T(8,128)(2,1)S(1)} %collective-permute-done.4.w_ref.v_ref, bf16[256,1024]{1,0:T(8,128)(2,1)S(1)} %shard_map.96.after_ref), custom_call_target="tpu_custom_call" | custom-call | tf_op jit(solution)/shard_map/pallas_call | solution.py:223
  58.0 1.2 %collective-permute-done.10.got_ref = bf16[256,1024]{1,0:T(8,128)(2,1)S(1)} collective-permute-done((bf16[256,1024]{1,0:T(8,128)(2,1)S(1)}, bf16[256,1024]{1,0:T(8,128)(2,1)S(1)}, u32[]{:S(2)}, u32[]{:S(2)}) %collective-permute-start.10) | collective-permute-done | bytes 524320 | tf_op jit(solution)/shard_map/ppermute | solution.py:33
  59.3 2.8 %collective-permute-start.11 = (bf16[256,1024]{1,0:T(8,128)(2,1)S(1)}, bf16[256,1024]{1,0:T(8,128)(2,1)S(1)}, u32[]{:S(2)}, u32[]{:S(2)}) collective-permute-start(bf16[256,1024]{1,0:T(8,128)(2,1)S(1)} %shard_map.101), channel_id=1, source_target_pairs={{0,6},{1,7},{2,4},{3,5},{4,2},{5,3},{6,0},{7,1},{8,10},{9,11},{10,... | collective-permute-start | bytes 1572872 | tf_op jit(solution)/shard_map/ppermute | solution.py:33
  62.2 6.2 %collective-permute-start.8 = (bf16[2,32,1024]{2,1,0:T(8,128)(2,1)S(1)}, bf16[2,32,1024]{2,1,0:T(8,128)(2,1)S(1)}, u32[]{:S(2)}, u32[]{:S(2)}) collective-permute-start(bf16[2,32,1024]{2,1,0:T(8,128)(2,1)S(1)} %get-tuple-element.18.refs_1_), channel_id=1, source_target_pairs={{0,192},{1,193},{2,194},{3,195},{4,196},{5,197},{6,198},{7,199},{8... | collective-permute-start | bytes 393224 | tf_op jit(solution)/shard_map/ppermute | solution.py:33
  68.4 1.7 %shard_map.99.own_ref.after_ref = f32[256,1024]{1,0:T(8,128)S(1)} custom-call(bf16[256,2048]{1,0:T(8,128)(2,1)S(1)} %shard_map.88.after_ref.a_ref, bf16[1024,1024]{1,0:T(8,128)(2,1)S(1)} %collective-permute-done.4.w_ref.v_ref, f32[256,1024]{1,0:T(8,128)S(1)} %shard_map.91.refs_0_, bf16[2,32,1024]{2,1,0:T(8,128)(2,1)S(1)} %get-tuple-element.18.refs_1_), custom_call_target="tpu_custom_call" | custom-call | tf_op jit(solution)/shard_map/pallas_call | solution.py:199
  70.1 2.5 %collective-permute-done.8 = bf16[2,32,1024]{2,1,0:T(8,128)(2,1)S(1)} collective-permute-done((bf16[2,32,1024]{2,1,0:T(8,128)(2,1)S(1)}, bf16[2,32,1024]{2,1,0:T(8,128)(2,1)S(1)}, u32[]{:S(2)}, u32[]{:S(2)}) %collective-permute-start.8) | collective-permute-done | bytes 131104 | tf_op jit(solution)/shard_map/ppermute | solution.py:33
  72.7 0.9 %multiply_subtract_fusion = (f32[2,32,1024]{2,1,0:T(8,128)}, f32[2,32,1024]{2,1,0:T(8,128)}) fusion(f32[2,32,1024]{2,1,0:T(8,128)S(1)} %copy-done.3, f32[2,32,1024]{2,1,0:T(8,128)S(1)} %get-tuple-element.17, bf16[2,32,1024]{2,1,0:T(8,128)(2,1)S(1)} %collective-permute-done.8, f32[2,32,1024]{2,1,0:T(8,128)S(1)} %copy-done.4), kind=kLoop, calls=%fused_computation | loop fusion | flops 655360 | bytes 1441792 | tf_op jit(solution)/shard_map/sub | solution.py:328
  73.7 0.8 %collective-permute-done.11.got_ref = bf16[256,1024]{1,0:T(8,128)(2,1)S(1)} collective-permute-done((bf16[256,1024]{1,0:T(8,128)(2,1)S(1)}, bf16[256,1024]{1,0:T(8,128)(2,1)S(1)}, u32[]{:S(2)}, u32[]{:S(2)}) %collective-permute-start.11) | collective-permute-done | bytes 524320 | tf_op jit(solution)/shard_map/ppermute | solution.py:33
  74.5 0.9 %shard_map.102 = bf16[256,1024]{1,0:T(8,128)(2,1)} custom-call(f32[256,1024]{1,0:T(8,128)S(1)} %shard_map.100.own_ref, bf16[256,1024]{1,0:T(8,128)(2,1)S(1)} %collective-permute-done.11.got_ref, f32[256,1]{1,0:T(8,128)S(1)} %shard_map.87.after_ref.scale_ref), custom_call_target="tpu_custom_call" | custom-call | tf_op jit(solution)/shard_map/pallas_call | solution.py:267
  (21 shorter events, 0.5 us)
Async XLA Ops:
  0.6 11.2 %collective-permute-start = (bf16[2,1024,1024]{2,1,0:T(8,128)(2,1)}, bf16[2,1024,1024]{2,1,0:T(8,128)(2,1)S(1)}, u32[]{:S(2)}, u32[]{:S(2)}) collective-permute-start(bf16[2,1024,1024]{2,1,0:T(8,128)(2,1)} %bitcast.9), channel_id=1, source_target_pairs={{0,8},{1,9},{2,10},{3,11},{4,12},{5,13},{6,14},{7,15},{8,0},{9,1},... | collective-permute-start | bytes 12582920 | tf_op jit(solution)/shard_map/ppermute | solution.py:33
  0.7 8.4 %copy-start = (bf16[256,8192]{1,0:T(8,128)(2,1)S(1)}, bf16[256,8192]{1,0:T(8,128)(2,1)}, u32[]{:S(2)}) copy-start(bf16[256,8192]{1,0:T(8,128)(2,1)} %a_ref.7) | copy-start | bytes 12582916
  0.7 48.4 %collective-permute-start.4 = (bf16[1024,1024]{1,0:T(8,128)(2,1)}, bf16[1024,1024]{1,0:T(8,128)(2,1)S(1)}, u32[]{:S(2)}, u32[]{:S(2)}) collective-permute-start(bf16[1024,1024]{1,0:T(8,128)(2,1)} %bitcast.4), channel_id=1, source_target_pairs={{0,1},{1,0},{2,3},{3,2},{4,5},{5,4},{6,7},{7,6},{8,9},{9,8},{10,11... | collective-permute-start | bytes 6291464 | tf_op jit(solution)/shard_map/ppermute | solution.py:33
  4.2 27.6 %collective-permute-start.2 = (bf16[256,2048]{1,0:T(8,128)(2,1)S(1)}, bf16[256,2048]{1,0:T(8,128)(2,1)S(1)}, u32[]{:S(2)}, u32[]{:S(2)}) collective-permute-start(bf16[256,2048]{1,0:T(8,128)(2,1)S(1)} %shard_map.85.after_ref), channel_id=1, source_target_pairs={{0,4},{1,5},{2,6},{3,7},{4,0},{5,1},{6,2},{7,3},{8,12},{9,13},{10,... | collective-permute-start | bytes 3145736 | tf_op jit(solution)/shard_map/ppermute | solution.py:33
  9.1 2.7 %copy-start.2 = (bf16[1,2,1024,1024]{3,2,1,0:T(8,128)(2,1)S(1)}, bf16[1,2,1024,1024]{3,2,1,0:T(8,128)(2,1)}, u32[]{:S(2)}) copy-start(bf16[1,2,1024,1024]{3,2,1,0:T(8,128)(2,1)} %param.6) | copy-start | bytes 12582916
  12.6 20.9 %collective-permute-start.1 = (bf16[2,2,4,32,1024]{4,3,2,1,0:T(8,128)(2,1)S(1)}, bf16[2,2,4,32,1024]{4,3,2,1,0:T(8,128)(2,1)S(1)}, u32[]{:S(2)}, u32[]{:S(2)}) collective-permute-start(bf16[2,2,4,32,1024]{4,3,2,1,0:T(8,128)(2,1)S(1)} %shard_map.89.after_ref), channel_id=1, source_target_pairs={{0,16},{1,17},{2,18},{3,19},{4,20},{5,21},{6,22},{7,23},{8,56},{9,... | collective-permute-start | bytes 3145736 | tf_op jit(solution)/shard_map/ppermute | solution.py:33
  13.1 41.8 %collective-permute-start.7 = (bf16[256,2048]{1,0:T(8,128)(2,1)S(1)}, bf16[256,2048]{1,0:T(8,128)(2,1)S(1)}, u32[]{:S(2)}, u32[]{:S(2)}) collective-permute-start(bf16[256,2048]{1,0:T(8,128)(2,1)S(1)} %get-tuple-element.11.after_ref), channel_id=1, source_target_pairs={{0,2},{1,3},{2,0},{3,1},{4,6},{5,7},{6,4},{7,5},{8,14},{9,15},{10,... | collective-permute-start | bytes 3145736 | tf_op jit(solution)/shard_map/ppermute | solution.py:33
  13.7 1.6 %copy-start.1 = (bf16[1,1024,1024]{2,1,0:T(8,128)(2,1)S(1)}, bf16[1,1024,1024]{2,1,0:T(8,128)(2,1)}, u32[]{:S(2)}) copy-start(bf16[1,1024,1024]{2,1,0:T(8,128)(2,1)} %param.9) | copy-start | bytes 6291460
  13.7 43.1 %collective-permute-start.6 = (bf16[256,2048]{1,0:T(8,128)(2,1)S(1)}, bf16[256,2048]{1,0:T(8,128)(2,1)S(1)}, u32[]{:S(2)}, u32[]{:S(2)}) collective-permute-start(bf16[256,2048]{1,0:T(8,128)(2,1)S(1)} %get-tuple-element.16), channel_id=1, source_target_pairs={{0,6},{1,7},{2,4},{3,5},{4,2},{5,3},{6,0},{7,1},{8,10},{9,11},{10,... | collective-permute-start | bytes 3145736 | tf_op jit(solution)/shard_map/ppermute | solution.py:33
  33.7 17.8 %collective-permute-start.3 = (bf16[2,4,32,1024]{3,2,1,0:T(8,128)(2,1)S(1)}, bf16[2,4,32,1024]{3,2,1,0:T(8,128)(2,1)S(1)}, u32[]{:S(2)}, u32[]{:S(2)}) collective-permute-start(bf16[2,4,32,1024]{3,2,1,0:T(8,128)(2,1)S(1)} %get-tuple-element.13.after_ref), channel_id=1, source_target_pairs={{0,48},{1,49},{2,50},{3,51},{4,52},{5,53},{6,54},{7,55},{8,24},{9,... | collective-permute-start | bytes 1572872 | tf_op jit(solution)/shard_map/ppermute | solution.py:33
  49.9 9.3 %collective-permute-start.10 = (bf16[256,1024]{1,0:T(8,128)(2,1)S(1)}, bf16[256,1024]{1,0:T(8,128)(2,1)S(1)}, u32[]{:S(2)}, u32[]{:S(2)}) collective-permute-start(bf16[256,1024]{1,0:T(8,128)(2,1)S(1)} %shard_map.94.after_ref), channel_id=1, source_target_pairs={{0,2},{1,3},{2,0},{3,1},{4,6},{5,7},{6,4},{7,5},{8,14},{9,15},{10,... | collective-permute-start | bytes 1572872 | tf_op jit(solution)/shard_map/ppermute | solution.py:33
  51.5 10.6 %collective-permute-start.5 = (bf16[2,2,32,1024]{3,2,1,0:T(8,128)(2,1)S(1)}, bf16[2,2,32,1024]{3,2,1,0:T(8,128)(2,1)S(1)}, u32[]{:S(2)}, u32[]{:S(2)}) collective-permute-start(bf16[2,2,32,1024]{3,2,1,0:T(8,128)(2,1)S(1)} %get-tuple-element.15.after_ref), channel_id=1, source_target_pairs={{0,64},{1,65},{2,66},{3,67},{4,68},{5,69},{6,70},{7,71},{8,200},{9... | collective-permute-start | bytes 786440 | tf_op jit(solution)/shard_map/ppermute | solution.py:33
  56.1 17.4 %collective-permute-start.9 = (bf16[256,1024]{1,0:T(8,128)(2,1)S(1)}, bf16[256,1024]{1,0:T(8,128)(2,1)S(1)}, u32[]{:S(2)}, u32[]{:S(2)}) collective-permute-start(bf16[256,1024]{1,0:T(8,128)(2,1)S(1)} %shard_map.96.after_ref), channel_id=1, source_target_pairs={{0,2},{1,3},{2,0},{3,1},{4,6},{5,7},{6,4},{7,5},{8,14},{9,15},{10,... | collective-permute-start | bytes 1572872 | tf_op jit(solution)/shard_map/ppermute | solution.py:33
  59.3 13.4 %copy-start.3 = (f32[2,32,1024]{2,1,0:T(8,128)S(1)}, f32[2,32,1024]{2,1,0:T(8,128)}, u32[]{:S(2)}) copy-start(f32[2,32,1024]{2,1,0:T(8,128)} %param.7) | copy-start | bytes 786436
  59.3 13.4 %copy-start.4 = (f32[2,32,1024]{2,1,0:T(8,128)S(1)}, f32[2,32,1024]{2,1,0:T(8,128)}, u32[]{:S(2)}) copy-start(f32[2,32,1024]{2,1,0:T(8,128)} %param.8) | copy-start | bytes 786436
  59.3 15.2 %collective-permute-start.11 = (bf16[256,1024]{1,0:T(8,128)(2,1)S(1)}, bf16[256,1024]{1,0:T(8,128)(2,1)S(1)}, u32[]{:S(2)}, u32[]{:S(2)}) collective-permute-start(bf16[256,1024]{1,0:T(8,128)(2,1)S(1)} %shard_map.101), channel_id=1, source_target_pairs={{0,6},{1,7},{2,4},{3,5},{4,2},{5,3},{6,0},{7,1},{8,10},{9,11},{10,... | collective-permute-start | bytes 1572872 | tf_op jit(solution)/shard_map/ppermute | solution.py:33
  62.2 10.5 %collective-permute-start.8 = (bf16[2,32,1024]{2,1,0:T(8,128)(2,1)S(1)}, bf16[2,32,1024]{2,1,0:T(8,128)(2,1)S(1)}, u32[]{:S(2)}, u32[]{:S(2)}) collective-permute-start(bf16[2,32,1024]{2,1,0:T(8,128)(2,1)S(1)} %get-tuple-element.18.refs_1_), channel_id=1, source_target_pairs={{0,192},{1,193},{2,194},{3,195},{4,196},{5,197},{6,198},{7,199},{8... | collective-permute-start | bytes 393224 | tf_op jit(solution)/shard_map/ppermute | solution.py:33

commit v5 on v4

--- a/solution.py
+++ b/solution.py
@@ -183,7 +183,7 @@
     )(own, got, after)
 
 
-TILE = 256
+TILE = 512
 
 
 def half_product(a, half, w, dtype, plus, after):

time: 75.6 us -> 75.6 us (level)
  Pallas kernels: 16.9 us -> 15.5 us
  waiting for transfers between devices: 33.2 us -> 34.6 us
    ppermute x12, waiting for transfers between devices: 33.2 us -> 34.6 us  [move(): return lax.ppermute(value, ('rep', 'fsdp'), pairs)]
    pallas_call x3, Pallas kernels: 4.99 us -> 3.57 us  [half_product(): call(kernel, like((rows, width), dtype), grid=(width // TILE,), in_specs=...]
  transfers between devices with their start and end apart: 12 -> 12, of which waited for: 5 -> 5; matrix products, arithmetic and copies ran while one was open for 1% -> 1% of each run, Pallas kernels for 21% -> 19%
where the time goes in v5:
time: 75.6 us; the launch traced here: 75.4 us
  waiting for transfers between devices  34.6 us (46%)
  starting transfers between devices  23.2 us (31%)
  Pallas kernels  15.5 us (21%)
  other arithmetic  0.88 us (1%)
  between operations  0.82 us (1%)
    ppermute x12, waiting for transfers between devices, move(): return lax.ppermute(value, ('rep', 'fsdp'), pairs)  34.6 us
    ppermute x12, starting transfers between devices, move(): return lax.ppermute(value, ('rep', 'fsdp'), pairs)  23.2 us
    pallas_call x3, Pallas kernels, gained(): call(kernel, [like((rows, 2 * step), BF16)] * (n // 2), in_specs=[HBM, HB...  4.69 us
    pallas_call x3, Pallas kernels, half_product(): call(kernel, like((rows, width), dtype), grid=(width // TILE,), in_specs=...  3.57 us
    pallas_call x2, Pallas kernels, product(): call(kernel, like((rows, width), dtype), in_specs=[VMEM] * 3 + [ANY], out...  2.48 us
  transfers between devices with their start and end apart: 12, of which 5 were waited for; matrix products, arithmetic and copies ran while one was open for 1% of the time, Pallas kernels for 19%

profile of v5, /device:TPU:8, one launch (start us, length us, event | category | flops | bytes accessed | tf_op | source)
XLA Modules:
  0.0 75.4 jit_solution(6703046544319762450)
XLA Ops:
  0.7 2.0 %collective-permute-start.4 = (bf16[1024,1024]{1,0:T(8,128)(2,1)}, bf16[1024,1024]{1,0:T(8,128)(2,1)S(1)}, u32[]{:S(2)}, u32[]{:S(2)}) collective-permute-start(bf16[1024,1024]{1,0:T(8,128)(2,1)} %bitcast.4), channel_id=1, source_target_pairs={{0,1},{1,0},{2,3},{3,2},{4,5},{5,4},{6,7},{7,6},{8,9},{9,8},{10,11... | collective-permute-start | bytes 6291464 | tf_op jit(solution)/shard_map/ppermute | solution.py:33
  2.7 1.4 %shard_map.85.after_ref = bf16[256,2048]{1,0:T(8,128)(2,1)S(1)} custom-call(bf16[256,8192]{1,0:T(8,128)(2,1)} %a_ref.7, f32[8192]{0:T(1024)} %g_ref.5, f32[8192]{0:T(1024)} %g_ref.5), custom_call_target="tpu_custom_call" | custom-call | tf_op jit(solution)/shard_map/pallas_call | solution.py:108
  4.2 3.1 %collective-permute-start.2 = (bf16[256,2048]{1,0:T(8,128)(2,1)S(1)}, bf16[256,2048]{1,0:T(8,128)(2,1)S(1)}, u32[]{:S(2)}, u32[]{:S(2)}) collective-permute-start(bf16[256,2048]{1,0:T(8,128)(2,1)S(1)} %shard_map.85.after_ref), channel_id=1, source_target_pairs={{0,4},{1,5},{2,6},{3,7},{4,0},{5,1},{6,2},{7,3},{8,12},{9,13},{10,... | collective-permute-start | bytes 3145736 | tf_op jit(solution)/shard_map/ppermute | solution.py:33
  7.3 1.8 %shard_map.86 = (bf16[256,2048]{1,0:T(8,128)(2,1)S(1)}, bf16[256,2048]{1,0:T(8,128)(2,1)S(1)}) custom-call(bf16[256,8192]{1,0:T(8,128)(2,1)} %a_ref.7, f32[8192]{0:T(1024)} %g_ref.5, bf16[256,2048]{1,0:T(8,128)(2,1)S(1)} %shard_map.85.after_ref), custom_call_target="tpu_custom_call" | custom-call | tf_op jit(solution)/shard_map/pallas_call | solution.py:108
  9.1 1.3 %shard_map.87.after_ref.scale_ref = f32[256,1]{1,0:T(8,128)S(1)} custom-call(bf16[256,8192]{1,0:T(8,128)(2,1)S(1)} %copy-done, bf16[256,2048]{1,0:T(8,128)(2,1)S(1)} %get-tuple-element.11.after_ref), custom_call_target="tpu_custom_call" | custom-call | tf_op jit(solution)/shard_map/pallas_call | solution.py:126
  10.4 1.4 %shard_map.88.after_ref.a_ref = bf16[256,2048]{1,0:T(8,128)(2,1)S(1)} custom-call(bf16[256,8192]{1,0:T(8,128)(2,1)} %a_ref.7, f32[8192]{0:T(1024)} %g_ref.5, f32[256,1]{1,0:T(8,128)S(1)} %shard_map.87.after_ref.scale_ref), custom_call_target="tpu_custom_call" | custom-call | tf_op jit(solution)/shard_map/pallas_call | solution.py:108
  11.9 0.7 shard_map.89.after_ref
  12.6 0.5 collective-permute-start.1
  13.1 0.6 collective-permute-start.7
  13.7 0.6 collective-permute-start.6
  14.3 0.6 shard_map.90.refs_0_.a_ref
  15.0 0.3 copy-done.1
  15.3 1.2 %shard_map.91.refs_0_ = f32[256,1024]{1,0:T(8,128)S(1)} custom-call(bf16[256,2048]{1,0:T(8,128)(2,1)S(1)} %shard_map.88.after_ref.a_ref, bf16[1024,1024]{1,0:T(8,128)(2,1)S(1)} %bitcast.5, bf16[2,2,4,32,1024]{4,3,2,1,0:T(8,128)(2,1)S(1)} %shard_map.90.refs_0_.a_ref), custom_call_target="tpu_custom_call" | custom-call | tf_op jit(solution)/shard_map/pallas_call | solution.py:199
  16.5 15.3 %collective-permute-done.2.a_ref = bf16[256,2048]{1,0:T(8,128)(2,1)S(1)} collective-permute-done((bf16[256,2048]{1,0:T(8,128)(2,1)S(1)}, bf16[256,2048]{1,0:T(8,128)(2,1)S(1)}, u32[]{:S(2)}, u32[]{:S(2)}) %collective-permute-start.2) | collective-permute-done | bytes 1048608 | tf_op jit(solution)/shard_map/ppermute | solution.py:33
  31.8 1.2 %shard_map.92.after_ref.plus_ref = f32[256,1024]{1,0:T(8,128)S(1)} custom-call(bf16[256,2048]{1,0:T(8,128)(2,1)S(1)} %collective-permute-done.2.a_ref, bf16[1024,1024]{1,0:T(8,128)(2,1)S(1)} %bitcast.6, f32[256,1024]{1,0:T(8,128)S(1)} %shard_map.91.refs_0_), custom_call_target="tpu_custom_call" | custom-call | tf_op jit(solution)/shard_map/pallas_call | solution.py:199
  33.0 0.2 shard_map.93
  33.2 1.7 %collective-permute-start.3 = (bf16[2,4,32,1024]{3,2,1,0:T(8,128)(2,1)S(1)}, bf16[2,4,32,1024]{3,2,1,0:T(8,128)(2,1)S(1)}, u32[]{:S(2)}, u32[]{:S(2)}) collective-permute-start(bf16[2,4,32,1024]{3,2,1,0:T(8,128)(2,1)S(1)} %get-tuple-element.13.after_ref), channel_id=1, source_target_pairs={{0,48},{1,49},{2,50},{3,51},{4,52},{5,53},{6,54},{7,55},{8,24},{9,... | collective-permute-start | bytes 1572872 | tf_op jit(solution)/shard_map/ppermute | solution.py:33
  34.9 14.3 %collective-permute-done.4.w_ref.v_ref = bf16[1024,1024]{1,0:T(8,128)(2,1)S(1)} collective-permute-done((bf16[1024,1024]{1,0:T(8,128)(2,1)}, bf16[1024,1024]{1,0:T(8,128)(2,1)S(1)}, u32[]{:S(2)}, u32[]{:S(2)}) %collective-permute-start.4) | collective-permute-done | bytes 2097184 | tf_op jit(solution)/shard_map/ppermute | solution.py:33
  49.1 0.7 shard_map.94.after_ref
  49.9 1.6 %collective-permute-start.10 = (bf16[256,1024]{1,0:T(8,128)(2,1)S(1)}, bf16[256,1024]{1,0:T(8,128)(2,1)S(1)}, u32[]{:S(2)}, u32[]{:S(2)}) collective-permute-start(bf16[256,1024]{1,0:T(8,128)(2,1)S(1)} %shard_map.94.after_ref), channel_id=1, source_target_pairs={{0,2},{1,3},{2,0},{3,1},{4,6},{5,7},{6,4},{7,5},{8,14},{9,15},{10,... | collective-permute-start | bytes 1572872 | tf_op jit(solution)/shard_map/ppermute | solution.py:33
  51.5 3.4 %collective-permute-start.5 = (bf16[2,2,32,1024]{3,2,1,0:T(8,128)(2,1)S(1)}, bf16[2,2,32,1024]{3,2,1,0:T(8,128)(2,1)S(1)}, u32[]{:S(2)}, u32[]{:S(2)}) collective-permute-start(bf16[2,2,32,1024]{3,2,1,0:T(8,128)(2,1)S(1)} %get-tuple-element.15.after_ref), channel_id=1, source_target_pairs={{0,64},{1,65},{2,66},{3,67},{4,68},{5,69},{6,70},{7,71},{8,200},{9... | collective-permute-start | bytes 786440 | tf_op jit(solution)/shard_map/ppermute | solution.py:33
  54.9 1.2 %shard_map.96.after_ref = bf16[256,1024]{1,0:T(8,128)(2,1)S(1)} custom-call(bf16[256,2048]{1,0:T(8,128)(2,1)S(1)} %collective-permute-done.7.a_ref, bf16[1024,1024]{1,0:T(8,128)(2,1)S(1)} %bitcast.7, bf16[1024,1024]{1,0:T(8,128)(2,1)S(1)} %collective-permute-done.4.w_ref.v_ref, bf16[2,2,32,1024]{3,2,1,0:T(8,128)(2,1)S(1)} %get-tuple-element.15.after_ref), custom_call_target="tpu_custom_call" | custom-call | tf_op jit(solution)/shard_map/pallas_call | solution.py:223
  56.1 0.6 collective-permute-start.9
  56.8 1.2 %shard_map.97.after_ref.own_ref = f32[256,1024]{1,0:T(8,128)S(1)} custom-call(bf16[256,2048]{1,0:T(8,128)(2,1)S(1)} %collective-permute-done.6.a_ref, bf16[1024,1024]{1,0:T(8,128)(2,1)S(1)} %bitcast.8, bf16[1024,1024]{1,0:T(8,128)(2,1)S(1)} %collective-permute-done.4.w_ref.v_ref, bf16[256,1024]{1,0:T(8,128)(2,1)S(1)} %shard_map.96.after_ref), custom_call_target="tpu_custom_call" | custom-call | tf_op jit(solution)/shard_map/pallas_call | solution.py:223
  58.0 1.2 %collective-permute-done.10.got_ref = bf16[256,1024]{1,0:T(8,128)(2,1)S(1)} collective-permute-done((bf16[256,1024]{1,0:T(8,128)(2,1)S(1)}, bf16[256,1024]{1,0:T(8,128)(2,1)S(1)}, u32[]{:S(2)}, u32[]{:S(2)}) %collective-permute-start.10) | collective-permute-done | bytes 524320 | tf_op jit(solution)/shard_map/ppermute | solution.py:33
  59.3 2.8 %collective-permute-start.11 = (bf16[256,1024]{1,0:T(8,128)(2,1)S(1)}, bf16[256,1024]{1,0:T(8,128)(2,1)S(1)}, u32[]{:S(2)}, u32[]{:S(2)}) collective-permute-start(bf16[256,1024]{1,0:T(8,128)(2,1)S(1)} %shard_map.101), channel_id=1, source_target_pairs={{0,6},{1,7},{2,4},{3,5},{4,2},{5,3},{6,0},{7,1},{8,10},{9,11},{10,... | collective-permute-start | bytes 1572872 | tf_op jit(solution)/shard_map/ppermute | solution.py:33
  62.2 6.2 %collective-permute-start.8 = (bf16[2,32,1024]{2,1,0:T(8,128)(2,1)S(1)}, bf16[2,32,1024]{2,1,0:T(8,128)(2,1)S(1)}, u32[]{:S(2)}, u32[]{:S(2)}) collective-permute-start(bf16[2,32,1024]{2,1,0:T(8,128)(2,1)S(1)} %get-tuple-element.18.refs_1_), channel_id=1, source_target_pairs={{0,192},{1,193},{2,194},{3,195},{4,196},{5,197},{6,198},{7,199},{8... | collective-permute-start | bytes 393224 | tf_op jit(solution)/shard_map/ppermute | solution.py:33
  68.4 1.2 %shard_map.99.own_ref.after_ref = f32[256,1024]{1,0:T(8,128)S(1)} custom-call(bf16[256,2048]{1,0:T(8,128)(2,1)S(1)} %shard_map.88.after_ref.a_ref, bf16[1024,1024]{1,0:T(8,128)(2,1)S(1)} %collective-permute-done.4.w_ref.v_ref, f32[256,1024]{1,0:T(8,128)S(1)} %shard_map.91.refs_0_, bf16[2,32,1024]{2,1,0:T(8,128)(2,1)S(1)} %get-tuple-element.18.refs_1_), custom_call_target="tpu_custom_call" | custom-call | tf_op jit(solution)/shard_map/pallas_call | solution.py:199
  69.6 3.0 %collective-permute-done.8 = bf16[2,32,1024]{2,1,0:T(8,128)(2,1)S(1)} collective-permute-done((bf16[2,32,1024]{2,1,0:T(8,128)(2,1)S(1)}, bf16[2,32,1024]{2,1,0:T(8,128)(2,1)S(1)}, u32[]{:S(2)}, u32[]{:S(2)}) %collective-permute-start.8) | collective-permute-done | bytes 131104 | tf_op jit(solution)/shard_map/ppermute | solution.py:33
  72.7 0.9 %multiply_subtract_fusion = (f32[2,32,1024]{2,1,0:T(8,128)}, f32[2,32,1024]{2,1,0:T(8,128)}) fusion(f32[2,32,1024]{2,1,0:T(8,128)S(1)} %copy-done.3, f32[2,32,1024]{2,1,0:T(8,128)S(1)} %get-tuple-element.17, bf16[2,32,1024]{2,1,0:T(8,128)(2,1)S(1)} %collective-permute-done.8, f32[2,32,1024]{2,1,0:T(8,128)S(1)} %copy-done.4), kind=kLoop, calls=%fused_computation | loop fusion | flops 655360 | bytes 1441792 | tf_op jit(solution)/shard_map/sub | solution.py:328
  73.7 0.8 %collective-permute-done.11.got_ref = bf16[256,1024]{1,0:T(8,128)(2,1)S(1)} collective-permute-done((bf16[256,1024]{1,0:T(8,128)(2,1)S(1)}, bf16[256,1024]{1,0:T(8,128)(2,1)S(1)}, u32[]{:S(2)}, u32[]{:S(2)}) %collective-permute-start.11) | collective-permute-done | bytes 524320 | tf_op jit(solution)/shard_map/ppermute | solution.py:33
  74.5 0.9 %shard_map.102 = bf16[256,1024]{1,0:T(8,128)(2,1)} custom-call(f32[256,1024]{1,0:T(8,128)S(1)} %shard_map.100.own_ref, bf16[256,1024]{1,0:T(8,128)(2,1)S(1)} %collective-permute-done.11.got_ref, f32[256,1]{1,0:T(8,128)S(1)} %shard_map.87.after_ref.scale_ref), custom_call_target="tpu_custom_call" | custom-call | tf_op jit(solution)/shard_map/pallas_call | solution.py:267
  (21 shorter events, 0.5 us)
Async XLA Ops:
  0.6 11.2 %collective-permute-start = (bf16[2,1024,1024]{2,1,0:T(8,128)(2,1)}, bf16[2,1024,1024]{2,1,0:T(8,128)(2,1)S(1)}, u32[]{:S(2)}, u32[]{:S(2)}) collective-permute-start(bf16[2,1024,1024]{2,1,0:T(8,128)(2,1)} %bitcast.9), channel_id=1, source_target_pairs={{0,8},{1,9},{2,10},{3,11},{4,12},{5,13},{6,14},{7,15},{8,0},{9,1},... | collective-permute-start | bytes 12582920 | tf_op jit(solution)/shard_map/ppermute | solution.py:33
  0.7 8.4 %copy-start = (bf16[256,8192]{1,0:T(8,128)(2,1)S(1)}, bf16[256,8192]{1,0:T(8,128)(2,1)}, u32[]{:S(2)}) copy-start(bf16[256,8192]{1,0:T(8,128)(2,1)} %a_ref.7) | copy-start | bytes 12582916
  0.7 48.4 %collective-permute-start.4 = (bf16[1024,1024]{1,0:T(8,128)(2,1)}, bf16[1024,1024]{1,0:T(8,128)(2,1)S(1)}, u32[]{:S(2)}, u32[]{:S(2)}) collective-permute-start(bf16[1024,1024]{1,0:T(8,128)(2,1)} %bitcast.4), channel_id=1, source_target_pairs={{0,1},{1,0},{2,3},{3,2},{4,5},{5,4},{6,7},{7,6},{8,9},{9,8},{10,11... | collective-permute-start | bytes 6291464 | tf_op jit(solution)/shard_map/ppermute | solution.py:33
  4.2 27.6 %collective-permute-start.2 = (bf16[256,2048]{1,0:T(8,128)(2,1)S(1)}, bf16[256,2048]{1,0:T(8,128)(2,1)S(1)}, u32[]{:S(2)}, u32[]{:S(2)}) collective-permute-start(bf16[256,2048]{1,0:T(8,128)(2,1)S(1)} %shard_map.85.after_ref), channel_id=1, source_target_pairs={{0,4},{1,5},{2,6},{3,7},{4,0},{5,1},{6,2},{7,3},{8,12},{9,13},{10,... | collective-permute-start | bytes 3145736 | tf_op jit(solution)/shard_map/ppermute | solution.py:33
  9.1 2.7 %copy-start.2 = (bf16[1,2,1024,1024]{3,2,1,0:T(8,128)(2,1)S(1)}, bf16[1,2,1024,1024]{3,2,1,0:T(8,128)(2,1)}, u32[]{:S(2)}) copy-start(bf16[1,2,1024,1024]{3,2,1,0:T(8,128)(2,1)} %param.6) | copy-start | bytes 12582916
  12.6 20.4 %collective-permute-start.1 = (bf16[2,2,4,32,1024]{4,3,2,1,0:T(8,128)(2,1)S(1)}, bf16[2,2,4,32,1024]{4,3,2,1,0:T(8,128)(2,1)S(1)}, u32[]{:S(2)}, u32[]{:S(2)}) collective-permute-start(bf16[2,2,4,32,1024]{4,3,2,1,0:T(8,128)(2,1)S(1)} %shard_map.89.after_ref), channel_id=1, source_target_pairs={{0,16},{1,17},{2,18},{3,19},{4,20},{5,21},{6,22},{7,23},{8,56},{9,... | collective-permute-start | bytes 3145736 | tf_op jit(solution)/shard_map/ppermute | solution.py:33
  13.1 41.8 %collective-permute-start.7 = (bf16[256,2048]{1,0:T(8,128)(2,1)S(1)}, bf16[256,2048]{1,0:T(8,128)(2,1)S(1)}, u32[]{:S(2)}, u32[]{:S(2)}) collective-permute-start(bf16[256,2048]{1,0:T(8,128)(2,1)S(1)} %get-tuple-element.11.after_ref), channel_id=1, source_target_pairs={{0,2},{1,3},{2,0},{3,1},{4,6},{5,7},{6,4},{7,5},{8,14},{9,15},{10,... | collective-permute-start | bytes 3145736 | tf_op jit(solution)/shard_map/ppermute | solution.py:33
  13.7 1.6 %copy-start.1 = (bf16[1,1024,1024]{2,1,0:T(8,128)(2,1)S(1)}, bf16[1,1024,1024]{2,1,0:T(8,128)(2,1)}, u32[]{:S(2)}) copy-start(bf16[1,1024,1024]{2,1,0:T(8,128)(2,1)} %param.9) | copy-start | bytes 6291460
  13.7 43.1 %collective-permute-start.6 = (bf16[256,2048]{1,0:T(8,128)(2,1)S(1)}, bf16[256,2048]{1,0:T(8,128)(2,1)S(1)}, u32[]{:S(2)}, u32[]{:S(2)}) collective-permute-start(bf16[256,2048]{1,0:T(8,128)(2,1)S(1)} %get-tuple-element.16), channel_id=1, source_target_pairs={{0,6},{1,7},{2,4},{3,5},{4,2},{5,3},{6,0},{7,1},{8,10},{9,11},{10,... | collective-permute-start | bytes 3145736 | tf_op jit(solution)/shard_map/ppermute | solution.py:33
  33.2 18.2 %collective-permute-start.3 = (bf16[2,4,32,1024]{3,2,1,0:T(8,128)(2,1)S(1)}, bf16[2,4,32,1024]{3,2,1,0:T(8,128)(2,1)S(1)}, u32[]{:S(2)}, u32[]{:S(2)}) collective-permute-start(bf16[2,4,32,1024]{3,2,1,0:T(8,128)(2,1)S(1)} %get-tuple-element.13.after_ref), channel_id=1, source_target_pairs={{0,48},{1,49},{2,50},{3,51},{4,52},{5,53},{6,54},{7,55},{8,24},{9,... | collective-permute-start | bytes 1572872 | tf_op jit(solution)/shard_map/ppermute | solution.py:33
  49.9 9.3 %collective-permute-start.10 = (bf16[256,1024]{1,0:T(8,128)(2,1)S(1)}, bf16[256,1024]{1,0:T(8,128)(2,1)S(1)}, u32[]{:S(2)}, u32[]{:S(2)}) collective-permute-start(bf16[256,1024]{1,0:T(8,128)(2,1)S(1)} %shard_map.94.after_ref), channel_id=1, source_target_pairs={{0,2},{1,3},{2,0},{3,1},{4,6},{5,7},{6,4},{7,5},{8,14},{9,15},{10,... | collective-permute-start | bytes 1572872 | tf_op jit(solution)/shard_map/ppermute | solution.py:33
  51.5 10.6 %collective-permute-start.5 = (bf16[2,2,32,1024]{3,2,1,0:T(8,128)(2,1)S(1)}, bf16[2,2,32,1024]{3,2,1,0:T(8,128)(2,1)S(1)}, u32[]{:S(2)}, u32[]{:S(2)}) collective-permute-start(bf16[2,2,32,1024]{3,2,1,0:T(8,128)(2,1)S(1)} %get-tuple-element.15.after_ref), channel_id=1, source_target_pairs={{0,64},{1,65},{2,66},{3,67},{4,68},{5,69},{6,70},{7,71},{8,200},{9... | collective-permute-start | bytes 786440 | tf_op jit(solution)/shard_map/ppermute | solution.py:33
  56.1 17.4 %collective-permute-start.9 = (bf16[256,1024]{1,0:T(8,128)(2,1)S(1)}, bf16[256,1024]{1,0:T(8,128)(2,1)S(1)}, u32[]{:S(2)}, u32[]{:S(2)}) collective-permute-start(bf16[256,1024]{1,0:T(8,128)(2,1)S(1)} %shard_map.96.after_ref), channel_id=1, source_target_pairs={{0,2},{1,3},{2,0},{3,1},{4,6},{5,7},{6,4},{7,5},{8,14},{9,15},{10,... | collective-permute-start | bytes 1572872 | tf_op jit(solution)/shard_map/ppermute | solution.py:33
  59.3 13.4 %copy-start.3 = (f32[2,32,1024]{2,1,0:T(8,128)S(1)}, f32[2,32,1024]{2,1,0:T(8,128)}, u32[]{:S(2)}) copy-start(f32[2,32,1024]{2,1,0:T(8,128)} %param.7) | copy-start | bytes 786436
  59.3 13.4 %copy-start.4 = (f32[2,32,1024]{2,1,0:T(8,128)S(1)}, f32[2,32,1024]{2,1,0:T(8,128)}, u32[]{:S(2)}) copy-start(f32[2,32,1024]{2,1,0:T(8,128)} %param.8) | copy-start | bytes 786436
  59.3 15.2 %collective-permute-start.11 = (bf16[256,1024]{1,0:T(8,128)(2,1)S(1)}, bf16[256,1024]{1,0:T(8,128)(2,1)S(1)}, u32[]{:S(2)}, u32[]{:S(2)}) collective-permute-start(bf16[256,1024]{1,0:T(8,128)(2,1)S(1)} %shard_map.101), channel_id=1, source_target_pairs={{0,6},{1,7},{2,4},{3,5},{4,2},{5,3},{6,0},{7,1},{8,10},{9,11},{10,... | collective-permute-start | bytes 1572872 | tf_op jit(solution)/shard_map/ppermute | solution.py:33
  62.2 10.5 %collective-permute-start.8 = (bf16[2,32,1024]{2,1,0:T(8,128)(2,1)S(1)}, bf16[2,32,1024]{2,1,0:T(8,128)(2,1)S(1)}, u32[]{:S(2)}, u32[]{:S(2)}) collective-permute-start(bf16[2,32,1024]{2,1,0:T(8,128)(2,1)S(1)} %get-tuple-element.18.refs_1_), channel_id=1, source_target_pairs={{0,192},{1,193},{2,194},{3,195},{4,196},{5,197},{6,198},{7,199},{8... | collective-permute-start | bytes 393224 | tf_op jit(solution)/shard_map/ppermute | solution.py:33

commit v6 on v4

--- a/solution.py
+++ b/solution.py
@@ -115,6 +115,40 @@
     )(in_hbm(activations), in_hbm(norm_gain), after)
 
 
+def gained_block(activations, norm_gain, owner, after):
+    rows, step, cuts = activations.shape[0], 2048, 4
+    tile = rows // cuts
+
+    def kernel(a_ref, g_ref, after_ref, out_ref, a_buf, g_buf, sems):
+        at = pl.ds(pl.multiple_of(owner() * step, step), step)
+        copies = [pltpu.make_async_copy(g_ref.at[at], g_buf, sems.at[cuts])]
+        for i in range(cuts):
+            part = slice(i * tile, (i + 1) * tile)
+            copies.append(
+                pltpu.make_async_copy(a_ref.at[part, at], a_buf.at[part], sems.at[i])
+            )
+        for copy in copies:
+            copy.start()
+        copies[0].wait()
+        gain = g_buf[...].reshape(1, step)
+        for i in range(cuts):
+            part = slice(i * tile, (i + 1) * tile)
+            copies[1 + i].wait()
+            out_ref[part] = (a_buf[part].astype(F32) * gain).astype(BF16)
+
+    return call(
+        kernel,
+        like((rows, step), BF16),
+        in_specs=[HBM, HBM, ANY],
+        out_specs=VMEM,
+        scratch_shapes=[
+            pltpu.VMEM((rows, step), BF16),
+            pltpu.VMEM((step,), F32),
+            DMA((cuts + 1,)),
+        ],
+    )(in_hbm(activations), in_hbm(norm_gain), after)
+
+
 def row_scale(activations, after):
     rows, width = activations.shape
     tile = 64
@@ -201,7 +235,7 @@
         like((rows, width), dtype),
         grid=(width // TILE,),
         in_specs=[
-            pl.BlockSpec((rows, depth), lambda j: (0, half)),
+            pl.BlockSpec((rows, depth), lambda j: (0, half())),
             pl.BlockSpec((depth, TILE), column),
         ]
         + [pl.BlockSpec((rows, TILE), column)] * len(plus)
@@ -229,9 +263,10 @@
     rows, (depth, width) = a.shape[0], w.shape
 
     def kernel(a_ref, w_ref, plus_ref, after_ref, out_ref):
+        value = a_ref[:, pl.ds(pl.multiple_of((1 - z_lo_of()) * depth, depth), depth)]
         for j in range(0, width, TILE):
             at = slice(j, j + TILE)
-            total = jnp.dot(a_ref[:, depth:], w_ref[:, at], preferred_element_type=F32)
+            total = jnp.dot(value, w_ref[:, at], preferred_element_type=F32)
             out_ref[:, at] = (total + plus_ref[:, at]).astype(BF16)
 
     return call(
@@ -287,7 +322,7 @@
     other = move(mine, lambda z, y, c, x, l: (z, y, c, x, 1 - l))
     sibling = move(fragment, lambda z, y, c, x, l: (z, y, 1 - c, x, l))
 
-    (a_far,) = gained(activations, norm_gain, [lambda: (x_of() + 2) % 4], norm_gain)
+    a_far = gained_block(activations, norm_gain, lambda: (x_of() + 2) % 4, norm_gain)
     far_a = x_far(a_far)
     a_first, a_second = gained(
         activations,
@@ -304,8 +339,8 @@
     )
     got = y_first(send)
     keep = pair_sum(fragment, sibling, [y_of, lambda: second(y_of(), core_of())], send)
-    own = half_product(own_a, 0, mine, F32, [], keep)
-    far = half_product(far_a, 0, mine, F32, [], own)
+    own = half_product(own_a, lambda: 0, mine, F32, [], keep)
+    far = half_product(far_a, z_lo_of, mine, F32, [], own)
     line, send = halves_sum(keep, got, far)
     got = y_second(send)
 
@@ -319,7 +354,7 @@
     from_second = x_second(plus(part, via, BF16, part))
     total, send = halves_sum(keep, got, part, SLOW)
     got = z_second(send)
-    own = half_product(own_a, 1, other, F32, [own], send)
+    own = half_product(own_a, lambda: 1, other, F32, [own], send)
     own = plus(own, from_first, F32, own, SLOW)
 
     total = total + got.astype(F32)

time: 75.6 us -> 75.6 us (level)
    pallas_call x3 -> x2, Pallas kernels: 4.69 us -> 3.28 us  [gained(): call(kernel, [like((rows, 2 * step), BF16)] * (n // 2), in_specs=[HBM, HB...]
    pallas_call x0 -> x1, Pallas kernels: none -> 1.29 us  [gained_block(): call(kernel, like((rows, step), BF16), in_specs=[HBM, HBM, ANY], out_spec...]
where the time goes in v6:
time: 75.6 us; the launch traced here: 75.4 us
  waiting for transfers between devices  33.3 us (44%)
  starting transfers between devices  23.3 us (31%)
  Pallas kernels  16.8 us (22%)
  other arithmetic  0.88 us (1%)
  between operations  0.82 us (1%)
    ppermute x12, waiting for transfers between devices, move(): return lax.ppermute(value, ('rep', 'fsdp'), pairs)  33.3 us
    ppermute x12, starting transfers between devices, move(): return lax.ppermute(value, ('rep', 'fsdp'), pairs)  23.3 us
    pallas_call x3, Pallas kernels, half_product(): call(kernel, like((rows, width), dtype), grid=(width // TILE,), in_specs=...  5.01 us
    pallas_call x2, Pallas kernels, gained(): call(kernel, [like((rows, 2 * step), BF16)] * (n // 2), in_specs=[HBM, HB...  3.28 us
    pallas_call x2, Pallas kernels, product(): call(kernel, like((rows, width), dtype), in_specs=[VMEM] * 3 + [ANY], out...  2.48 us
  transfers between devices with their start and end apart: 12, of which 5 were waited for; matrix products, arithmetic and copies ran while one was open for 1% of the time, Pallas kernels for 21%

profile of v6, /device:TPU:8, one launch (start us, length us, event | category | flops | bytes accessed | tf_op | source)
XLA Modules:
  0.0 75.4 jit_solution(1830972542753233554)
XLA Ops:
  0.7 2.0 %collective-permute-start.4 = (bf16[1024,1024]{1,0:T(8,128)(2,1)}, bf16[1024,1024]{1,0:T(8,128)(2,1)S(1)}, u32[]{:S(2)}, u32[]{:S(2)}) collective-permute-start(bf16[1024,1024]{1,0:T(8,128)(2,1)} %bitcast.4), channel_id=1, source_target_pairs={{0,1},{1,0},{2,3},{3,2},{4,5},{5,4},{6,7},{7,6},{8,9},{9,8},{10,11... | collective-permute-start | bytes 6291464 | tf_op jit(solution)/shard_map/ppermute | solution.py:33
  2.7 1.3 %shard_map.85.after_ref = bf16[256,2048]{1,0:T(8,128)(2,1)S(1)} custom-call(bf16[256,8192]{1,0:T(8,128)(2,1)} %a_ref.7, f32[8192]{0:T(1024)} %g_ref.5, f32[8192]{0:T(1024)} %g_ref.5), custom_call_target="tpu_custom_call" | custom-call | tf_op jit(solution)/shard_map/pallas_call | solution.py:139
  4.0 3.1 %collective-permute-start.2 = (bf16[256,2048]{1,0:T(8,128)(2,1)S(1)}, bf16[256,2048]{1,0:T(8,128)(2,1)S(1)}, u32[]{:S(2)}, u32[]{:S(2)}) collective-permute-start(bf16[256,2048]{1,0:T(8,128)(2,1)S(1)} %shard_map.85.after_ref), channel_id=1, source_target_pairs={{0,4},{1,5},{2,6},{3,7},{4,0},{5,1},{6,2},{7,3},{8,12},{9,13},{10,... | collective-permute-start | bytes 3145736 | tf_op jit(solution)/shard_map/ppermute | solution.py:33
  7.2 1.8 %shard_map.86 = (bf16[256,2048]{1,0:T(8,128)(2,1)S(1)}, bf16[256,2048]{1,0:T(8,128)(2,1)S(1)}) custom-call(bf16[256,8192]{1,0:T(8,128)(2,1)} %a_ref.7, f32[8192]{0:T(1024)} %g_ref.5, bf16[256,2048]{1,0:T(8,128)(2,1)S(1)} %shard_map.85.after_ref), custom_call_target="tpu_custom_call" | custom-call | tf_op jit(solution)/shard_map/pallas_call | solution.py:108
  9.0 1.3 %shard_map.87.after_ref.scale_ref = f32[256,1]{1,0:T(8,128)S(1)} custom-call(bf16[256,8192]{1,0:T(8,128)(2,1)S(1)} %copy-done, bf16[256,2048]{1,0:T(8,128)(2,1)S(1)} %get-tuple-element.11.after_ref), custom_call_target="tpu_custom_call" | custom-call | tf_op jit(solution)/shard_map/pallas_call | solution.py:160
  10.3 1.4 %shard_map.88.after_ref.a_ref = bf16[256,2048]{1,0:T(8,128)(2,1)S(1)} custom-call(bf16[256,8192]{1,0:T(8,128)(2,1)} %a_ref.7, f32[8192]{0:T(1024)} %g_ref.5, f32[256,1]{1,0:T(8,128)S(1)} %shard_map.87.after_ref.scale_ref), custom_call_target="tpu_custom_call" | custom-call | tf_op jit(solution)/shard_map/pallas_call | solution.py:108
  11.8 0.7 shard_map.89.after_ref
  12.5 0.5 collective-permute-start.1
  13.0 0.6 collective-permute-start.7
  13.6 0.6 collective-permute-start.6
  14.2 0.6 shard_map.90.refs_0_.a_ref
  14.9 0.3 copy-done.1
  15.2 1.6 %shard_map.91.refs_0_ = f32[256,1024]{1,0:T(8,128)S(1)} custom-call(bf16[256,2048]{1,0:T(8,128)(2,1)S(1)} %shard_map.88.after_ref.a_ref, bf16[1024,1024]{1,0:T(8,128)(2,1)S(1)} %bitcast.5, bf16[2,2,4,32,1024]{4,3,2,1,0:T(8,128)(2,1)S(1)} %shard_map.90.refs_0_.a_ref), custom_call_target="tpu_custom_call" | custom-call | tf_op jit(solution)/shard_map/pallas_call | solution.py:233
  16.8 14.9 %collective-permute-done.2.a_ref = bf16[256,2048]{1,0:T(8,128)(2,1)S(1)} collective-permute-done((bf16[256,2048]{1,0:T(8,128)(2,1)S(1)}, bf16[256,2048]{1,0:T(8,128)(2,1)S(1)}, u32[]{:S(2)}, u32[]{:S(2)}) %collective-permute-start.2) | collective-permute-done | bytes 1048608 | tf_op jit(solution)/shard_map/ppermute | solution.py:33
  31.7 1.7 %shard_map.92.after_ref.plus_ref = f32[256,1024]{1,0:T(8,128)S(1)} custom-call(bf16[256,2048]{1,0:T(8,128)(2,1)S(1)} %collective-permute-done.2.a_ref, bf16[1024,1024]{1,0:T(8,128)(2,1)S(1)} %bitcast.6, f32[256,1024]{1,0:T(8,128)S(1)} %shard_map.91.refs_0_), custom_call_target="tpu_custom_call" | custom-call | tf_op jit(solution)/shard_map/pallas_call | solution.py:233
  33.4 0.2 shard_map.93
  33.6 1.7 %collective-permute-start.3 = (bf16[2,4,32,1024]{3,2,1,0:T(8,128)(2,1)S(1)}, bf16[2,4,32,1024]{3,2,1,0:T(8,128)(2,1)S(1)}, u32[]{:S(2)}, u32[]{:S(2)}) collective-permute-start(bf16[2,4,32,1024]{3,2,1,0:T(8,128)(2,1)S(1)} %get-tuple-element.13.after_ref), channel_id=1, source_target_pairs={{0,48},{1,49},{2,50},{3,51},{4,52},{5,53},{6,54},{7,55},{8,24},{9,... | collective-permute-start | bytes 1572872 | tf_op jit(solution)/shard_map/ppermute | solution.py:33
  35.2 13.9 %collective-permute-done.4.w_ref.v_ref = bf16[1024,1024]{1,0:T(8,128)(2,1)S(1)} collective-permute-done((bf16[1024,1024]{1,0:T(8,128)(2,1)}, bf16[1024,1024]{1,0:T(8,128)(2,1)S(1)}, u32[]{:S(2)}, u32[]{:S(2)}) %collective-permute-start.4) | collective-permute-done | bytes 2097184 | tf_op jit(solution)/shard_map/ppermute | solution.py:33
  49.1 0.7 shard_map.94.after_ref
  49.9 1.6 %collective-permute-start.10 = (bf16[256,1024]{1,0:T(8,128)(2,1)S(1)}, bf16[256,1024]{1,0:T(8,128)(2,1)S(1)}, u32[]{:S(2)}, u32[]{:S(2)}) collective-permute-start(bf16[256,1024]{1,0:T(8,128)(2,1)S(1)} %shard_map.94.after_ref), channel_id=1, source_target_pairs={{0,2},{1,3},{2,0},{3,1},{4,6},{5,7},{6,4},{7,5},{8,14},{9,15},{10,... | collective-permute-start | bytes 1572872 | tf_op jit(solution)/shard_map/ppermute | solution.py:33
  51.5 3.4 %collective-permute-start.5 = (bf16[2,2,32,1024]{3,2,1,0:T(8,128)(2,1)S(1)}, bf16[2,2,32,1024]{3,2,1,0:T(8,128)(2,1)S(1)}, u32[]{:S(2)}, u32[]{:S(2)}) collective-permute-start(bf16[2,2,32,1024]{3,2,1,0:T(8,128)(2,1)S(1)} %get-tuple-element.15.after_ref), channel_id=1, source_target_pairs={{0,64},{1,65},{2,66},{3,67},{4,68},{5,69},{6,70},{7,71},{8,200},{9... | collective-permute-start | bytes 786440 | tf_op jit(solution)/shard_map/ppermute | solution.py:33
  54.9 1.2 %shard_map.96.after_ref = bf16[256,1024]{1,0:T(8,128)(2,1)S(1)} custom-call(bf16[256,2048]{1,0:T(8,128)(2,1)S(1)} %collective-permute-done.7.a_ref, bf16[1024,1024]{1,0:T(8,128)(2,1)S(1)} %bitcast.7, bf16[1024,1024]{1,0:T(8,128)(2,1)S(1)} %collective-permute-done.4.w_ref.v_ref, bf16[2,2,32,1024]{3,2,1,0:T(8,128)(2,1)S(1)} %get-tuple-element.15.after_ref), custom_call_target="tpu_custom_call" | custom-call | tf_op jit(solution)/shard_map/pallas_call | solution.py:257
  56.1 0.6 collective-permute-start.9
  56.8 1.2 %shard_map.97.after_ref.own_ref = f32[256,1024]{1,0:T(8,128)S(1)} custom-call(bf16[256,2048]{1,0:T(8,128)(2,1)S(1)} %collective-permute-done.6.a_ref, bf16[1024,1024]{1,0:T(8,128)(2,1)S(1)} %bitcast.8, bf16[1024,1024]{1,0:T(8,128)(2,1)S(1)} %collective-permute-done.4.w_ref.v_ref, bf16[256,1024]{1,0:T(8,128)(2,1)S(1)} %shard_map.96.after_ref), custom_call_target="tpu_custom_call" | custom-call | tf_op jit(solution)/shard_map/pallas_call | solution.py:257
  58.0 1.1 %collective-permute-done.10.got_ref = bf16[256,1024]{1,0:T(8,128)(2,1)S(1)} collective-permute-done((bf16[256,1024]{1,0:T(8,128)(2,1)S(1)}, bf16[256,1024]{1,0:T(8,128)(2,1)S(1)}, u32[]{:S(2)}, u32[]{:S(2)}) %collective-permute-start.10) | collective-permute-done | bytes 524320 | tf_op jit(solution)/shard_map/ppermute | solution.py:33
  59.2 2.8 %collective-permute-start.11 = (bf16[256,1024]{1,0:T(8,128)(2,1)S(1)}, bf16[256,1024]{1,0:T(8,128)(2,1)S(1)}, u32[]{:S(2)}, u32[]{:S(2)}) collective-permute-start(bf16[256,1024]{1,0:T(8,128)(2,1)S(1)} %shard_map.101), channel_id=1, source_target_pairs={{0,6},{1,7},{2,4},{3,5},{4,2},{5,3},{6,0},{7,1},{8,10},{9,11},{10,... | collective-permute-start | bytes 1572872 | tf_op jit(solution)/shard_map/ppermute | solution.py:33
  62.2 6.2 %collective-permute-start.8 = (bf16[2,32,1024]{2,1,0:T(8,128)(2,1)S(1)}, bf16[2,32,1024]{2,1,0:T(8,128)(2,1)S(1)}, u32[]{:S(2)}, u32[]{:S(2)}) collective-permute-start(bf16[2,32,1024]{2,1,0:T(8,128)(2,1)S(1)} %get-tuple-element.18.refs_1_), channel_id=1, source_target_pairs={{0,192},{1,193},{2,194},{3,195},{4,196},{5,197},{6,198},{7,199},{8... | collective-permute-start | bytes 393224 | tf_op jit(solution)/shard_map/ppermute | solution.py:33
  68.4 1.7 %shard_map.99.own_ref.after_ref = f32[256,1024]{1,0:T(8,128)S(1)} custom-call(bf16[256,2048]{1,0:T(8,128)(2,1)S(1)} %shard_map.88.after_ref.a_ref, bf16[1024,1024]{1,0:T(8,128)(2,1)S(1)} %collective-permute-done.4.w_ref.v_ref, f32[256,1024]{1,0:T(8,128)S(1)} %shard_map.91.refs_0_, bf16[2,32,1024]{2,1,0:T(8,128)(2,1)S(1)} %get-tuple-element.18.refs_1_), custom_call_target="tpu_custom_call" | custom-call | tf_op jit(solution)/shard_map/pallas_call | solution.py:233
  70.1 2.5 %collective-permute-done.8 = bf16[2,32,1024]{2,1,0:T(8,128)(2,1)S(1)} collective-permute-done((bf16[2,32,1024]{2,1,0:T(8,128)(2,1)S(1)}, bf16[2,32,1024]{2,1,0:T(8,128)(2,1)S(1)}, u32[]{:S(2)}, u32[]{:S(2)}) %collective-permute-start.8) | collective-permute-done | bytes 131104 | tf_op jit(solution)/shard_map/ppermute | solution.py:33
  72.7 0.9 %multiply_subtract_fusion = (f32[2,32,1024]{2,1,0:T(8,128)}, f32[2,32,1024]{2,1,0:T(8,128)}) fusion(f32[2,32,1024]{2,1,0:T(8,128)S(1)} %copy-done.3, f32[2,32,1024]{2,1,0:T(8,128)S(1)} %get-tuple-element.17, bf16[2,32,1024]{2,1,0:T(8,128)(2,1)S(1)} %collective-permute-done.8, f32[2,32,1024]{2,1,0:T(8,128)S(1)} %copy-done.4), kind=kLoop, calls=%fused_computation | loop fusion | flops 655360 | bytes 1441792 | tf_op jit(solution)/shard_map/sub | solution.py:363
  73.7 0.8 %collective-permute-done.11.got_ref = bf16[256,1024]{1,0:T(8,128)(2,1)S(1)} collective-permute-done((bf16[256,1024]{1,0:T(8,128)(2,1)S(1)}, bf16[256,1024]{1,0:T(8,128)(2,1)S(1)}, u32[]{:S(2)}, u32[]{:S(2)}) %collective-permute-start.11) | collective-permute-done | bytes 524320 | tf_op jit(solution)/shard_map/ppermute | solution.py:33
  74.5 0.9 %shard_map.102 = bf16[256,1024]{1,0:T(8,128)(2,1)} custom-call(f32[256,1024]{1,0:T(8,128)S(1)} %shard_map.100.own_ref, bf16[256,1024]{1,0:T(8,128)(2,1)S(1)} %collective-permute-done.11.got_ref, f32[256,1]{1,0:T(8,128)S(1)} %shard_map.87.after_ref.scale_ref), custom_call_target="tpu_custom_call" | custom-call | tf_op jit(solution)/shard_map/pallas_call | solution.py:302
  (21 shorter events, 0.5 us)
Async XLA Ops:
  0.6 11.1 %collective-permute-start = (bf16[2,1024,1024]{2,1,0:T(8,128)(2,1)}, bf16[2,1024,1024]{2,1,0:T(8,128)(2,1)S(1)}, u32[]{:S(2)}, u32[]{:S(2)}) collective-permute-start(bf16[2,1024,1024]{2,1,0:T(8,128)(2,1)} %bitcast.9), channel_id=1, source_target_pairs={{0,8},{1,9},{2,10},{3,11},{4,12},{5,13},{6,14},{7,15},{8,0},{9,1},... | collective-permute-start | bytes 12582920 | tf_op jit(solution)/shard_map/ppermute | solution.py:33
  0.7 8.3 %copy-start = (bf16[256,8192]{1,0:T(8,128)(2,1)S(1)}, bf16[256,8192]{1,0:T(8,128)(2,1)}, u32[]{:S(2)}) copy-start(bf16[256,8192]{1,0:T(8,128)(2,1)} %a_ref.7) | copy-start | bytes 12582916
  0.7 48.4 %collective-permute-start.4 = (bf16[1024,1024]{1,0:T(8,128)(2,1)}, bf16[1024,1024]{1,0:T(8,128)(2,1)S(1)}, u32[]{:S(2)}, u32[]{:S(2)}) collective-permute-start(bf16[1024,1024]{1,0:T(8,128)(2,1)} %bitcast.4), channel_id=1, source_target_pairs={{0,1},{1,0},{2,3},{3,2},{4,5},{5,4},{6,7},{7,6},{8,9},{9,8},{10,11... | collective-permute-start | bytes 6291464 | tf_op jit(solution)/shard_map/ppermute | solution.py:33
  4.0 27.6 %collective-permute-start.2 = (bf16[256,2048]{1,0:T(8,128)(2,1)S(1)}, bf16[256,2048]{1,0:T(8,128)(2,1)S(1)}, u32[]{:S(2)}, u32[]{:S(2)}) collective-permute-start(bf16[256,2048]{1,0:T(8,128)(2,1)S(1)} %shard_map.85.after_ref), channel_id=1, source_target_pairs={{0,4},{1,5},{2,6},{3,7},{4,0},{5,1},{6,2},{7,3},{8,12},{9,13},{10,... | collective-permute-start | bytes 3145736 | tf_op jit(solution)/shard_map/ppermute | solution.py:33
  9.0 2.7 %copy-start.2 = (bf16[1,2,1024,1024]{3,2,1,0:T(8,128)(2,1)S(1)}, bf16[1,2,1024,1024]{3,2,1,0:T(8,128)(2,1)}, u32[]{:S(2)}) copy-start(bf16[1,2,1024,1024]{3,2,1,0:T(8,128)(2,1)} %param.6) | copy-start | bytes 12582916
  12.5 20.9 %collective-permute-start.1 = (bf16[2,2,4,32,1024]{4,3,2,1,0:T(8,128)(2,1)S(1)}, bf16[2,2,4,32,1024]{4,3,2,1,0:T(8,128)(2,1)S(1)}, u32[]{:S(2)}, u32[]{:S(2)}) collective-permute-start(bf16[2,2,4,32,1024]{4,3,2,1,0:T(8,128)(2,1)S(1)} %shard_map.89.after_ref), channel_id=1, source_target_pairs={{0,16},{1,17},{2,18},{3,19},{4,20},{5,21},{6,22},{7,23},{8,56},{9,... | collective-permute-start | bytes 3145736 | tf_op jit(solution)/shard_map/ppermute | solution.py:33
  13.0 41.9 %collective-permute-start.7 = (bf16[256,2048]{1,0:T(8,128)(2,1)S(1)}, bf16[256,2048]{1,0:T(8,128)(2,1)S(1)}, u32[]{:S(2)}, u32[]{:S(2)}) collective-permute-start(bf16[256,2048]{1,0:T(8,128)(2,1)S(1)} %get-tuple-element.11.after_ref), channel_id=1, source_target_pairs={{0,2},{1,3},{2,0},{3,1},{4,6},{5,7},{6,4},{7,5},{8,14},{9,15},{10,... | collective-permute-start | bytes 3145736 | tf_op jit(solution)/shard_map/ppermute | solution.py:33
  13.6 1.6 %copy-start.1 = (bf16[1,1024,1024]{2,1,0:T(8,128)(2,1)S(1)}, bf16[1,1024,1024]{2,1,0:T(8,128)(2,1)}, u32[]{:S(2)}) copy-start(bf16[1,1024,1024]{2,1,0:T(8,128)(2,1)} %param.9) | copy-start | bytes 6291460
  13.6 43.2 %collective-permute-start.6 = (bf16[256,2048]{1,0:T(8,128)(2,1)S(1)}, bf16[256,2048]{1,0:T(8,128)(2,1)S(1)}, u32[]{:S(2)}, u32[]{:S(2)}) collective-permute-start(bf16[256,2048]{1,0:T(8,128)(2,1)S(1)} %get-tuple-element.16), channel_id=1, source_target_pairs={{0,6},{1,7},{2,4},{3,5},{4,2},{5,3},{6,0},{7,1},{8,10},{9,11},{10,... | collective-permute-start | bytes 3145736 | tf_op jit(solution)/shard_map/ppermute | solution.py:33
  33.6 17.9 %collective-permute-start.3 = (bf16[2,4,32,1024]{3,2,1,0:T(8,128)(2,1)S(1)}, bf16[2,4,32,1024]{3,2,1,0:T(8,128)(2,1)S(1)}, u32[]{:S(2)}, u32[]{:S(2)}) collective-permute-start(bf16[2,4,32,1024]{3,2,1,0:T(8,128)(2,1)S(1)} %get-tuple-element.13.after_ref), channel_id=1, source_target_pairs={{0,48},{1,49},{2,50},{3,51},{4,52},{5,53},{6,54},{7,55},{8,24},{9,... | collective-permute-start | bytes 1572872 | tf_op jit(solution)/shard_map/ppermute | solution.py:33
  49.9 9.3 %collective-permute-start.10 = (bf16[256,1024]{1,0:T(8,128)(2,1)S(1)}, bf16[256,1024]{1,0:T(8,128)(2,1)S(1)}, u32[]{:S(2)}, u32[]{:S(2)}) collective-permute-start(bf16[256,1024]{1,0:T(8,128)(2,1)S(1)} %shard_map.94.after_ref), channel_id=1, source_target_pairs={{0,2},{1,3},{2,0},{3,1},{4,6},{5,7},{6,4},{7,5},{8,14},{9,15},{10,... | collective-permute-start | bytes 1572872 | tf_op jit(solution)/shard_map/ppermute | solution.py:33
  51.5 10.6 %collective-permute-start.5 = (bf16[2,2,32,1024]{3,2,1,0:T(8,128)(2,1)S(1)}, bf16[2,2,32,1024]{3,2,1,0:T(8,128)(2,1)S(1)}, u32[]{:S(2)}, u32[]{:S(2)}) collective-permute-start(bf16[2,2,32,1024]{3,2,1,0:T(8,128)(2,1)S(1)} %get-tuple-element.15.after_ref), channel_id=1, source_target_pairs={{0,64},{1,65},{2,66},{3,67},{4,68},{5,69},{6,70},{7,71},{8,200},{9... | collective-permute-start | bytes 786440 | tf_op jit(solution)/shard_map/ppermute | solution.py:33
  56.1 17.4 %collective-permute-start.9 = (bf16[256,1024]{1,0:T(8,128)(2,1)S(1)}, bf16[256,1024]{1,0:T(8,128)(2,1)S(1)}, u32[]{:S(2)}, u32[]{:S(2)}) collective-permute-start(bf16[256,1024]{1,0:T(8,128)(2,1)S(1)} %shard_map.96.after_ref), channel_id=1, source_target_pairs={{0,2},{1,3},{2,0},{3,1},{4,6},{5,7},{6,4},{7,5},{8,14},{9,15},{10,... | collective-permute-start | bytes 1572872 | tf_op jit(solution)/shard_map/ppermute | solution.py:33
  59.2 13.5 %copy-start.3 = (f32[2,32,1024]{2,1,0:T(8,128)S(1)}, f32[2,32,1024]{2,1,0:T(8,128)}, u32[]{:S(2)}) copy-start(f32[2,32,1024]{2,1,0:T(8,128)} %param.7) | copy-start | bytes 786436
  59.2 13.4 %copy-start.4 = (f32[2,32,1024]{2,1,0:T(8,128)S(1)}, f32[2,32,1024]{2,1,0:T(8,128)}, u32[]{:S(2)}) copy-start(f32[2,32,1024]{2,1,0:T(8,128)} %param.8) | copy-start | bytes 786436
  59.2 15.3 %collective-permute-start.11 = (bf16[256,1024]{1,0:T(8,128)(2,1)S(1)}, bf16[256,1024]{1,0:T(8,128)(2,1)S(1)}, u32[]{:S(2)}, u32[]{:S(2)}) collective-permute-start(bf16[256,1024]{1,0:T(8,128)(2,1)S(1)} %shard_map.101), channel_id=1, source_target_pairs={{0,6},{1,7},{2,4},{3,5},{4,2},{5,3},{6,0},{7,1},{8,10},{9,11},{10,... | collective-permute-start | bytes 1572872 | tf_op jit(solution)/shard_map/ppermute | solution.py:33
  62.2 10.5 %collective-permute-start.8 = (bf16[2,32,1024]{2,1,0:T(8,128)(2,1)S(1)}, bf16[2,32,1024]{2,1,0:T(8,128)(2,1)S(1)}, u32[]{:S(2)}, u32[]{:S(2)}) collective-permute-start(bf16[2,32,1024]{2,1,0:T(8,128)(2,1)S(1)} %get-tuple-element.18.refs_1_), channel_id=1, source_target_pairs={{0,192},{1,193},{2,194},{3,195},{4,196},{5,197},{6,198},{7,199},{8... | collective-permute-start | bytes 393224 | tf_op jit(solution)/shard_map/ppermute | solution.py:33
